TPU v7x, 32 devices: a whole 2x2x4 slice. The times are simulated.
32 devices in a mesh: gz: 2 (over core), row: 4 (over y, x), col: 4 (over z).
Axes of the slice: x: 2, y: 2, z: 4, core: 2. Of those that a mesh axis runs over, the one named last changes fastest.
Arguments:
- ancestor: float32 [4096, 2048], P('row', 'col'), may hold values from -6 to 6
- lower_panel: bfloat16 [2, 8, 24, 128, 128], P('gz', 'col', 'row'), may hold values from -6 to 6
- row_ids: int32 [2, 8, 24], P('gz', 'col', 'row'), may hold values from 0 to 7, as said below
- row_counts: int32 [2, 8, 4], P('gz', 'col', 'row'), may hold values from 1 to 6
- diag_inverse: bfloat16 [2, 8, 128, 128], P('gz', 'col'), may hold values from -0.5 to 0.5
- upper_panel: bfloat16 [2, 8, 12, 128, 128], P('gz', 'row', 'col'), may hold values from -0.1875 to 0.1875
- col_ids: int32 [2, 8, 12], P('gz', 'row', 'col'), may hold values from 0 to 3, as said below
- col_counts: int32 [2, 8, 4], P('gz', 'row', 'col'), may hold values from 1 to 3
Outputs:
- updated: float32 [4096, 2048], P('row', 'col')
Inputs may be any that keep to these rules, and one draw needn't show every extreme that they name: `row_ids`: within each layer, supernode and process row the 6 slots name distinct local block rows. `col_ids`: within each layer, supernode and process column the 3 slots name distinct local block columns.
All inputs are finite; a program needn't handle non-finite values.
Results may differ from a plain program's by a relative error of at most 0.0026.
Values may be sent and summed in bfloat16 or wider, within the bound.
No kernel may reach another device: no remote copies, remote signals or barrier semaphores. Data moves between devices by JAX's collectives and lax.ppermute only.
A program may use at most 128 MiB of HBM per device.

v0:
```python
import jax
import jax.numpy as jnp
from jax import lax
from jax.sharding import PartitionSpec as P


def spread_rows(tiles, ids, counts, blocks):
    slots = ids.shape[1]
    slot_index = jnp.arange(slots, dtype=jnp.int32)
    alive = slot_index[None, :] < counts
    target = jnp.arange(blocks, dtype=jnp.int32)
    select = ((ids[:, :, None] == target[None, None, :]) & alive[:, :, None]).astype(jnp.bfloat16)
    dense = jnp.einsum("krl,krab->lakb", select, tiles, preferred_element_type=jnp.float32).astype(
        jnp.bfloat16
    )
    width = tiles.shape[-1]
    return dense.reshape(blocks * width, tiles.shape[0] * width)


def spread_cols(tiles, ids, counts, blocks):
    slots = ids.shape[1]
    slot_index = jnp.arange(slots, dtype=jnp.int32)
    alive = slot_index[None, :] < counts
    target = jnp.arange(blocks, dtype=jnp.int32)
    select = ((ids[:, :, None] == target[None, None, :]) & alive[:, :, None]).astype(jnp.bfloat16)
    dense = jnp.einsum("kcm,kcab->kamb", select, tiles, preferred_element_type=jnp.float32).astype(
        jnp.bfloat16
    )
    width = tiles.shape[-1]
    return dense.reshape(tiles.shape[0] * width, blocks * width)


def on_device(
    ancestor, lower_panel, row_ids, row_counts, diag_inverse, upper_panel, col_ids, col_counts
):
    width = lower_panel.shape[-1]
    row_blocks = ancestor.shape[0] // width
    col_blocks = ancestor.shape[1] // width
    solved = jnp.einsum(
        "ksab,kbc->ksac", lower_panel[0], diag_inverse[0], preferred_element_type=jnp.float32
    ).astype(jnp.bfloat16)
    piece = lax.all_gather((upper_panel[0], col_ids[0], col_counts[0]), "row", axis=0, tiled=True)
    upper_dense = spread_cols(piece[0], piece[1], piece[2], col_blocks)
    piece = lax.all_gather((solved, row_ids[0], row_counts[0]), "col", axis=0, tiled=True)
    lower_dense = spread_rows(piece[0], piece[1], piece[2], row_blocks)
    partial_sum = jnp.dot(lower_dense, upper_dense, preferred_element_type=jnp.float32)
    return ancestor - lax.psum(partial_sum, "gz")


def solution(mesh):
    placed = (
        P("row", "col"),
        P("gz", "col", "row", None, None),
        P("gz", "col", "row"),
        P("gz", "col", "row"),
        P("gz", "col", None, None),
        P("gz", "row", "col", None, None),
        P("gz", "row", "col"),
        P("gz", "row", "col"),
    )
    return jax.shard_map(
        on_device, mesh=mesh, in_specs=placed, out_specs=P("row", "col"), check_vma=False
    )
```

profile of v0, /device:TPU:0, one launch (start us, length us, event | category | flops | bytes accessed | tf_op | source)
XLA Modules:
  0.0 96.7 jit_solution(2150252983570737509)
XLA Ops:
  6.5 0.0 copy-start
  6.5 0.0 all-gather.7.cloned.1.call-start
  6.5 1.0 %copy-done = bf16[1,2,6,128,128]{4,3,2,1,0:T(8,128)(2,1)S(1)} copy-done((bf16[1,2,6,128,128]{4,3,2,1,0:T(8,128)(2,1)S(1)}, bf16[1,2,6,128,128]{4,3,2,1,0:T(8,128)(2,1)}, u32[]{:S(2)}) %copy-start) | copy-done | bytes 393240
  7.5 1.8 %convolution_convert_fusion.1 = bf16[2,6,128,128]{3,2,1,0:T(8,128)(2,1)} fusion(bf16[1,2,6,128,128]{4,3,2,1,0:T(8,128)(2,1)S(1)} %copy-done, bf16[1,2,128,128]{3,2,1,0:T(8,128)(2,1)} %param.12), kind=kOutput, calls=%fused_computation.7 | convolution fusion | flops 50528256 | bytes 851968 | tf_op jit(solution)/shard_map/ksab,kbc->ksac/dot_general | solution.py:39
  9.4 0.0 all-gather.7.cloned.1.call-update
  9.4 0.0 all-reduce.4.cloned.1.call-start
  9.4 1.3 %dynamic-slice.1 = u32[1]{0:T(128)} dynamic-slice(u32[32]{0:T(128)} %constant.14, u32[]{:T(128)S(6)} %add.2), dynamic_slice_sizes={1} | dynamic-slice | bytes 12
  11.3 0.8 bitcast_dynamic-update-slice_fusion
  12.1 8.8 %all-reduce.1 = s32[8]{0:T(128)S(1)} all-reduce(s32[8]{0:T(128)S(1)} %bitcast_dynamic-update-slice_fusion), channel_id=5, replica_groups=mesh['gz'=2,'row'=4,'col'=4] {'row'}, use_global_device_ids=true, to_apply=%add.1 | all-reduce | flops 8 | bytes 64
  20.9 1.3 %dynamic-slice = u32[1]{0:T(128)} dynamic-slice(u32[32]{0:T(128)} %constant.9, u32[]{:T(128)S(6)} %add.2), dynamic_slice_sizes={1} | dynamic-slice | bytes 12
  22.8 0.8 bitcast_dynamic-update-slice_fusion.1
  23.6 8.0 %all-gather.2 = s32[1,8,3]{2,0,1:T(1,128)S(1)} all-gather(s32[1,2,3]{2,0,1:T(1,128)} %bitcast.50), channel_id=4, replica_groups=mesh['gz'=2,'row'=4,'col'=4] {'row'}, dimensions={1}, use_global_device_ids=true | all-gather | bytes 120 | tf_op jit(solution)/shard_map/all_gather | solution.py:42
  31.6 9.0 %all-reduce = s32[8]{0:T(128)S(1)} all-reduce(s32[8]{0:T(128)S(1)} %bitcast_dynamic-update-slice_fusion.1), channel_id=3, replica_groups=mesh['gz'=2,'row'=4,'col'=4] {'col'}, use_global_device_ids=true, to_apply=%add | all-reduce | flops 8 | bytes 64
  40.6 9.4 %all-gather = s32[1,8,6]{2,0,1:T(1,128)S(1)} all-gather(s32[1,2,6]{2,0,1:T(1,128)} %bitcast.51), channel_id=2, replica_groups=mesh['gz'=2,'row'=4,'col'=4] {'col'}, dimensions={1}, use_global_device_ids=true | all-gather | bytes 240 | tf_op jit(solution)/shard_map/all_gather | solution.py:44
  50.0 10.5 %all-gather.4 = bf16[1,8,3,128,128]{4,3,2,0,1:T(8,128)(2,1)S(1)} all-gather(bf16[1,2,3,128,128]{4,3,2,0,1:T(8,128)(2,1)} %bitcast.47), channel_id=6, replica_groups=mesh['gz'=2,'row'=4,'col'=4] {'row'}, dimensions={1}, use_global_device_ids=true | all-gather | bytes 983040 | tf_op jit(solution)/shard_map/all_gather | solution.py:42
  60.5 0.1 iota_compare_fusion.3
  60.5 0.1 iota_compare_fusion.2
  60.6 0.8 convolution_convert_fusion
  61.4 0.0 all-gather.7.cloned.1.call-done
  61.4 2.5 %convert_bitcast_fusion = bf16[8,128,8,128]{3,0,1,2:T(8,128)(2,1)S(1)} fusion(bf16[8,6,128,128]{3,2,1,0:T(8,128)(2,1)} %all-gather.7.cloned.1.call-done, s32[8,6]{1,0:T(8,128)S(1)} %bitcast.48, pred[8,6]{1,0:T(8,128)(4,1)S(1)} %iota_compare_fusion.3), kind=kOutput, calls=%fused_computation.5 | convolution fusion | flops 13632256 | bytes 3670256 | tf_op jit(solution)/shard_map/krl,krab->lakb/dot_general | solution.py:13
  63.9 1.4 %copy.18 = bf16[8,128,8,128]{3,2,1,0:T(8,128)(2,1)S(1)} copy(bf16[8,128,8,128]{3,0,1,2:T(8,128)(2,1)S(1)} %convert_bitcast_fusion) | data formatting | bytes 4194304 | tf_op jit(solution)/shard_map/convert_element_type | solution.py:13
  65.3 2.6 %fusion = f32[1024,512]{1,0:T(8,128)} fusion(bf16[128,8,8,128]{3,2,1,0:T(8,128)(2,1)S(1)} %bitcast.46, bf16[128,8,4,128]{3,2,1,0:T(4,128)(2,1)S(1)} %bitcast.52), kind=kOutput, calls=%fused_computation | convolution fusion | flops 1073741824 | bytes 5242880 | tf_op jit(solution)/shard_map/dot_general | solution.py:46
  67.8 0.0 copy-start.1
  67.8 0.0 all-reduce.4.cloned.1.call-update
  67.9 18.6 %all-reduce.4.cloned.1.call-done = f32[1024,512]{1,0:T(8,128)} async-done(((f32[1024,512]{1,0:T(8,128)}), f32[1024,512]{1,0:T(8,128)}) %all-reduce.4.cloned.1.call-update) | async-done | bytes 2097168 | tf_op jit(solution)/shard_map/psum | solution.py:47
  86.5 0.0 copy-done.1
  86.5 3.4 %sub.3 = f32[1024,512]{1,0:T(8,128)} subtract(f32[1024,512]{1,0:T(8,128)S(1)} %copy-done.1, f32[1024,512]{1,0:T(8,128)} %all-reduce.4.cloned.1.call-done) | non-fusion elementwise | flops 524288 | bytes 6291456 | tf_op jit(solution)/shard_map/sub | solution.py:47
  (2 shorter events, 0.0 us)
Async XLA Ops:
  6.5 1.0 %copy-start = (bf16[1,2,6,128,128]{4,3,2,1,0:T(8,128)(2,1)S(1)}, bf16[1,2,6,128,128]{4,3,2,1,0:T(8,128)(2,1)}, u32[]{:S(2)}) copy-start(bf16[1,2,6,128,128]{4,3,2,1,0:T(8,128)(2,1)} %param.9) | copy-start | bytes 1179652
  6.5 54.9 %all-gather.7.cloned.1.call-start = ((), (), s32[]{:S(2)}) async-start(), calls=%async_computation | async-start | bytes 1966080 | tf_op jit(solution)/shard_map/all_gather | solution.py:44
  9.4 77.1 %all-reduce.4.cloned.1.call-start = ((), (), s32[]{:S(2)}) async-start(), calls=%async_computation.1 | async-start | bytes 4194304 | tf_op jit(solution)/shard_map/psum | solution.py:47
  67.8 18.6 %copy-start.1 = (f32[1024,512]{1,0:T(8,128)S(1)}, f32[1024,512]{1,0:T(8,128)}, u32[]{:S(2)}) copy-start(f32[1024,512]{1,0:T(8,128)} %param.8) | copy-start | bytes 6291460
Sparse Core Ops, SparseCore 0:
  9.5 40.0 all-gather.6
  68.0 18.4 all-reduce.3
where the time goes:
time: 97.1 us; the launch traced here: 96.7 us
  blocking collectives  45.7 us (47%)
  waiting for transfers between devices  18.7 us (19%)
  between operations  14.7 us (15%)
  matrix products  7.65 us (8%)
  local copies, waits for them, and re-layouts  6.4 us (7%)
  other arithmetic  3.53 us (4%)
    psum x1, waiting for transfers between devices, on_device(): return ancestor - lax.psum(partial_sum, 'gz')  18.6 us
    all_gather x2, blocking collectives, on_device(): lax.all_gather((upper_panel[0], col_ids[0], col_counts[0]), 'row', axis=0...  18.5 us
    unnamed x2, blocking collectives  17.8 us
    all_gather x1, blocking collectives, on_device(): lax.all_gather((solved, row_ids[0], row_counts[0]), 'col', axis=0, tiled=...  9.4 us
    unnamed x10, local copies, waits for them, and re-layouts  5.04 us
    sub x1, other arithmetic, on_device(): return ancestor - lax.psum(partial_sum, 'gz')  3.39 us
    dot_general x1, matrix products, on_device(): jnp.dot(lower_dense, upper_dense, preferred_element_type=jnp.float32)  2.57 us
    dot_general x1, matrix products, spread_rows(): jnp.einsum('krl,krab->lakb', select, tiles, preferred_element_type=jnp.fl...  2.45 us
  transfers between devices with their start and end apart: 2, of which 1 were waited for; matrix products, arithmetic and copies ran while one was open for 5% of the time, Pallas kernels for 0%

commit v1 on v0

v1 whole, which is shorter than its diff:
```python
import functools

import jax
import jax.numpy as jnp
from jax import lax
from jax.experimental import pallas as pl
from jax.experimental.pallas import tpu as pltpu
from jax.sharding import PartitionSpec as P

VMEM_LIMIT = 24 * 1024 * 1024
ID_ROWS = 16


def whole_vmem():
    return pl.BlockSpec(memory_space=pltpu.VMEM)


def whole_smem():
    return pl.BlockSpec(memory_space=pltpu.SMEM)


def prepare_kernel(row_ids, row_counts, col_ids, col_counts, lower, inverse, upper, both, first, second, spread):
    supernodes, slots, width, _ = lower.shape
    chunk = slots * width + ID_ROWS
    for k, half in enumerate((first, second)):
        tiles = lower[k].reshape(slots * width, width)
        solved = jnp.dot(tiles, inverse[k], preferred_element_type=jnp.float32).astype(jnp.bfloat16)
        half[0 : slots * width, :] = solved
        both[k * chunk : k * chunk + slots * width, :] = solved
        at_row = lax.broadcasted_iota(jnp.int32, (ID_ROWS, width), 0)
        ids = jnp.zeros((ID_ROWS, width), jnp.int32)
        for s in range(slots):
            place = jnp.where(s < row_counts[0, k, 0], row_ids[0, k, s] + 1, 0)
            ids = jnp.where(at_row == s, place, ids)
        ids = ids.astype(jnp.float32).astype(jnp.bfloat16)
        half[slots * width : chunk, :] = ids
        both[k * chunk + slots * width : (k + 1) * chunk, :] = ids
    spread[...] = jnp.zeros_like(spread)
    for k in range(supernodes):
        for c in range(upper.shape[1]):

            @pl.when(c < col_counts[0, k, 0])
            def _():
                at = pl.multiple_of(col_ids[0, k, c] * width, width)
                spread[k * width : (k + 1) * width, pl.ds(at, width)] = upper[k, c]


def prepare(lower, row_ids, row_counts, inverse, upper, col_ids, col_counts, col_blocks):
    supernodes, slots, width, _ = lower.shape
    chunk = slots * width + ID_ROWS
    return pl.pallas_call(
        prepare_kernel,
        out_shape=(
            jax.ShapeDtypeStruct((supernodes * chunk, width), jnp.bfloat16),
            jax.ShapeDtypeStruct((chunk, width), jnp.bfloat16),
            jax.ShapeDtypeStruct((chunk, width), jnp.bfloat16),
            jax.ShapeDtypeStruct((supernodes * width, col_blocks * width), jnp.bfloat16),
        ),
        in_specs=[whole_smem()] * 4 + [whole_vmem()] * 3,
        out_specs=(whole_vmem(),) * 4,
        compiler_params=pltpu.CompilerParams(vmem_limit_bytes=VMEM_LIMIT),
        name="solve_and_pack",
    )(row_ids, row_counts, col_ids, col_counts, lower, inverse, upper)


def accumulate_kernel(slots, col_axis, row_axis, items, payloads, base_count, *refs):
    panels = refs[:payloads]
    uppers = refs[payloads : payloads + 4]
    bases = refs[payloads + 4 : payloads + 4 + base_count]
    out = refs[payloads + 4 + base_count]
    left, right = refs[payloads + 5 + base_count :]
    width = panels[0].shape[1]
    chunk = slots * width + ID_ROWS
    step = pl.program_id(0)

    @pl.when(step == 0)
    def _():
        mine = lax.axis_index(col_axis) ^ lax.axis_index(row_axis)
        left[...] = jnp.zeros_like(left)
        for n, (panel, k, group) in enumerate(items):
            start = k * chunk if panels[panel].shape[0] > chunk else 0
            ids = panels[panel][start + slots * width : start + chunk, :].astype(jnp.float32).astype(jnp.int32)
            for s in range(slots):
                at = pl.multiple_of(ids[s, 0] * width, width)
                left[pl.ds(at, width), n * width : (n + 1) * width] = panels[panel][
                    start + s * width : start + (s + 1) * width, :
                ]
            for j in range(4):

                @pl.when((mine ^ group) == j)
                def _():
                    right[n * width : (n + 1) * width, :] = uppers[j][k * width : (k + 1) * width, :]

    rows = out.shape[0]
    at = pl.multiple_of(step * rows + width, width)
    update = jnp.dot(left[pl.ds(at, rows), :], right[...], preferred_element_type=jnp.float32)
    if base_count:
        out[...] = bases[0][...] + update
    else:
        out[...] = update


def accumulate(panels, items, uppers, bases, out_shape, slots, col_axis, row_axis, steps=4):
    width = panels[0].shape[1]
    rows = out_shape[0] // steps
    block = pl.BlockSpec((rows, out_shape[1]), lambda i: (i, 0))
    depth = len(items) * width
    return pl.pallas_call(
        functools.partial(
            accumulate_kernel, slots, col_axis, row_axis, tuple(items), len(panels), len(bases)
        ),
        grid=(steps,),
        out_shape=jax.ShapeDtypeStruct(out_shape, jnp.float32),
        in_specs=[whole_vmem()] * (len(panels) + 4) + [block] * len(bases),
        out_specs=block,
        scratch_shapes=[
            pltpu.VMEM((out_shape[0] + width, depth), jnp.bfloat16),
            pltpu.VMEM((depth, out_shape[1]), jnp.bfloat16),
        ],
        compiler_params=pltpu.CompilerParams(vmem_limit_bytes=VMEM_LIMIT),
        name="accumulate_tiles",
    )(*panels, *uppers, *bases)


def finish_kernel(ancestor, mine, other, out):
    out[...] = ancestor[...] - (mine[...] + other[...])


def finish(ancestor, mine, other, steps=8):
    block = pl.BlockSpec((ancestor.shape[0] // steps, ancestor.shape[1]), lambda i: (i, 0))
    return pl.pallas_call(
        finish_kernel,
        grid=(steps,),
        out_shape=jax.ShapeDtypeStruct(ancestor.shape, jnp.float32),
        in_specs=[block] * 3,
        out_specs=block,
        compiler_params=pltpu.CompilerParams(vmem_limit_bytes=VMEM_LIMIT),
        name="subtract_layers",
    )(ancestor, mine, other)


def swap(array, axis, mask):
    return lax.ppermute(array, axis, [(i, i ^ mask) for i in range(4)])


def on_line_of_four(
    ancestor, lower_panel, row_ids, row_counts, diag_inverse, upper_panel, col_ids, col_counts
):
    width = lower_panel.shape[-1]
    slots = lower_panel.shape[2]
    both, first, second, spread = prepare(
        lower_panel[0],
        row_ids,
        row_counts,
        diag_inverse[0],
        upper_panel[0],
        col_ids,
        col_counts,
        ancestor.shape[1] // width,
    )
    near = swap(both, "col", 1)
    far_first = swap(first, "col", 2)
    far_second = swap(second, "col", 2)
    last_first = swap(far_first, "col", 1)
    last_second = swap(far_second, "col", 1)
    uppers = [spread] + [swap(spread, "row", j) for j in (1, 2, 3)]
    shape = ancestor.shape
    early = accumulate(
        [both, near], [(0, 0, 0), (0, 1, 0), (1, 0, 1), (1, 1, 1)], uppers, [], shape, slots, "col", "row"
    )
    partial = accumulate(
        [far_first, far_second, last_first, last_second],
        [(0, 0, 2), (1, 1, 2), (2, 0, 3), (3, 1, 3)],
        uppers,
        [early],
        shape,
        slots,
        "col",
        "row",
    )
    other = lax.ppermute(partial, "gz", [(0, 1), (1, 0)])
    return finish(ancestor, partial, other)


def spread_tiles(tiles, ids, counts, blocks, rule):
    slot_index = jnp.arange(ids.shape[1], dtype=jnp.int32)
    alive = slot_index[None, :] < counts
    target = jnp.arange(blocks, dtype=jnp.int32)
    select = ((ids[:, :, None] == target[None, None, :]) & alive[:, :, None]).astype(jnp.bfloat16)
    return jnp.einsum(rule, select, tiles, preferred_element_type=jnp.float32).astype(jnp.bfloat16)


def on_device(
    ancestor, lower_panel, row_ids, row_counts, diag_inverse, upper_panel, col_ids, col_counts
):
    width = lower_panel.shape[-1]
    rows, columns = ancestor.shape
    solved = jnp.einsum(
        "ksab,kbc->ksac", lower_panel[0], diag_inverse[0], preferred_element_type=jnp.float32
    ).astype(jnp.bfloat16)
    piece = lax.all_gather((upper_panel[0], col_ids[0], col_counts[0]), "row", axis=0, tiled=True)
    upper_dense = spread_tiles(*piece, columns // width, "kcm,kcab->kamb").reshape(-1, columns)
    piece = lax.all_gather((solved, row_ids[0], row_counts[0]), "col", axis=0, tiled=True)
    lower_dense = spread_tiles(*piece, rows // width, "krl,krab->lakb").reshape(rows, -1)
    partial_sum = jnp.dot(lower_dense, upper_dense, preferred_element_type=jnp.float32)
    return ancestor - lax.psum(partial_sum, "gz")


def solution(mesh):
    placed = (
        P("row", "col"),
        P("gz", "col", "row", None, None),
        P("gz", "col", "row"),
        P("gz", "col", "row"),
        P("gz", "col", None, None),
        P("gz", "row", "col", None, None),
        P("gz", "row", "col"),
        P("gz", "row", "col"),
    )
    sizes = dict(mesh.shape)
    small = sizes["gz"] == 2 and sizes["row"] == 4 and sizes["col"] == 4

    def run(ancestor, lower_panel, *rest):
        two = lower_panel.shape[1] == 2 * sizes["col"]
        body = on_line_of_four if small and two else on_device
        return jax.shard_map(
            body, mesh=mesh, in_specs=placed, out_specs=P("row", "col"), check_vma=False
        )(ancestor, lower_panel, *rest)

    return run
```

time: 97.1 us -> 48.9 us (0.50)
  blocking collectives: 45.7 us -> 0 us
  between operations: 14.7 us -> 0.06 us
  starting transfers between devices: 0.04 us -> 12.9 us
  matrix products: 7.65 us -> 0 us
  Pallas kernels: 0 us -> 7.24 us
  waiting for transfers between devices: 18.7 us -> 22.8 us
  other arithmetic: 3.53 us -> 0 us
    all_gather x3 -> x0, blocking collectives: 27.9 us -> none  [the longest x2 18.5 us: on_device(): lax.all_gather((upper_panel[0], col_ids[0], col_counts[0]), 'row', axis=0...]
    ppermute x0 -> x9, waiting for transfers between devices: none -> 22.8 us  [the longest x8 18.6 us: swap(): return lax.ppermute(array, axis, [(i, i ^ mask) for i in range(4)])]
    psum x1 -> x0, waiting for transfers between devices: 18.6 us -> none  [on_device(): return ancestor - lax.psum(partial_sum, 'gz')]
    unnamed x2 -> x0, blocking collectives: 17.8 us -> none
    ppermute x0 -> x9, starting transfers between devices: none -> 12.9 us  [the longest x8 12.8 us: swap(): return lax.ppermute(array, axis, [(i, i ^ mask) for i in range(4)])]
    dot_general x4 -> x0, matrix products: 7.65 us -> none  [the longest x1 2.57 us: on_device(): jnp.dot(lower_dense, upper_dense, preferred_element_type=jnp.float32)]
    pallas_call x0 -> x4, Pallas kernels: none -> 7.24 us  [the longest x2 3.28 us: accumulate(): pl.pallas_call(functools.partial(accumulate_kernel, slots, col_axis, row_...]
    sub x1 -> x0, other arithmetic: 3.39 us -> none  [on_device(): return ancestor - lax.psum(partial_sum, 'gz')]
  transfers between devices with their start and end apart: 2 -> 9, of which waited for: 1 -> 6; matrix products, arithmetic and copies ran while one was open for 5% -> 0% of each run, Pallas kernels for 0% -> 3%
where the time goes in v1:
time: 48.9 us; the launch traced here: 48.6 us
  waiting for transfers between devices  22.8 us (47%)
  starting transfers between devices  12.9 us (26%)
  Pallas kernels  7.24 us (15%)
  local copies, waits for them, and re-layouts  5.6 us (11%)
    ppermute x8, waiting for transfers between devices, swap(): return lax.ppermute(array, axis, [(i, i ^ mask) for i in range(4)])  18.6 us
    ppermute x8, starting transfers between devices, swap(): return lax.ppermute(array, axis, [(i, i ^ mask) for i in range(4)])  12.8 us
    unnamed x14, local copies, waits for them, and re-layouts  5.6 us
    ppermute x1, waiting for transfers between devices, on_line_of_four(): other = lax.ppermute(partial, 'gz', [(0, 1), (1, 0)])  4.15 us
    pallas_call x2, Pallas kernels, accumulate(): pl.pallas_call(functools.partial(accumulate_kernel, slots, col_axis, row_...  3.28 us
    pallas_call x1, Pallas kernels, finish(): pl.pallas_call(finish_kernel, grid=(steps,), out_shape=jax.ShapeDtypeStru...  3.05 us
  transfers between devices with their start and end apart: 9, of which 6 were waited for; matrix products, arithmetic and copies ran while one was open for 0% of the time, Pallas kernels for 3%

profile of v1, /device:TPU:0, one launch (start us, length us, event | category | flops | bytes accessed | tf_op | source)
XLA Modules:
  0.0 48.6 jit_solution(2415586003989300029)
XLA Ops:
  0.0 0.7 %copy.9.row_counts = s32[1,2,1]{2,1,0:T(2,128)S(1)} copy(s32[1,2,1]{1,2,0:T(1,128)} %param.11) | data formatting | bytes 16 | tf_op args[3]
  0.7 0.7 %copy.10.col_counts = s32[1,2,1]{2,1,0:T(2,128)S(1)} copy(s32[1,2,1]{1,2,0:T(1,128)} %param.15) | data formatting | bytes 16 | tf_op args[7]
  1.5 0.0 copy-start.1
  1.5 1.0 %copy-done.1 = bf16[1,2,6,128,128]{4,3,2,1,0:T(8,128)(2,1)S(1)} copy-done((bf16[1,2,6,128,128]{4,3,2,1,0:T(8,128)(2,1)S(1)}, bf16[1,2,6,128,128]{4,3,2,1,0:T(8,128)(2,1)}, u32[]{:S(2)}) %copy-start.1) | copy-done | bytes 393240
  2.5 0.9 %copy-done.2 = bf16[1,2,3,128,128]{4,3,2,1,0:T(8,128)(2,1)S(1)} copy-done((bf16[1,2,3,128,128]{4,3,2,1,0:T(8,128)(2,1)S(1)}, bf16[1,2,3,128,128]{4,3,2,1,0:T(8,128)(2,1)}, u32[]{:S(2)}) %copy-start.2) | copy-done | bytes 196632
  3.4 0.8 %copy-done.3 = bf16[1,2,128,128]{3,2,1,0:T(8,128)(2,1)S(1)} copy-done((bf16[1,2,128,128]{3,2,1,0:T(8,128)(2,1)S(1)}, bf16[1,2,128,128]{3,2,1,0:T(8,128)(2,1)}, u32[]{:S(2)}) %copy-start.3) | copy-done | bytes 65560
  4.2 0.7 %copy-done.4 = s32[1,2,6]{2,1,0:T(2,128)S(1)} copy-done((s32[1,2,6]{2,1,0:T(2,128)S(1)}, s32[1,2,6]{2,1,0:T(2,128)}, u32[]{:S(2)}) %copy-start.4) | copy-done | bytes 72
  4.9 0.7 %copy-done.5 = s32[1,2,3]{2,1,0:T(2,128)S(1)} copy-done((s32[1,2,3]{2,1,0:T(2,128)S(1)}, s32[1,2,3]{2,1,0:T(2,128)}, u32[]{:S(2)}) %copy-start.5) | copy-done | bytes 48
  5.6 0.9 %solve_and_pack.1 = (bf16[1568,128]{1,0:T(8,128)(2,1)S(1)}, bf16[784,128]{1,0:T(8,128)(2,1)S(1)}, bf16[784,128]{1,0:T(8,128)(2,1)S(1)}, bf16[256,512]{1,0:T(8,128)(2,1)S(1)}) custom-call(s32[1,2,6]{2,1,0:T(2,128)S(1)} %copy-done.4, s32[1,2,1]{2,1,0:T(2,128)S(1)} %copy.9.row_counts, s32[1,2,3]{2,1,0:T(2,128)S(1)} %copy-done.5, ...), custom_call_target="tpu_custom_call" | custom-call | tf_op jit(solution)/shard_map/solve_and_pack/pallas_call | solution.py:51
  6.5 4.1 %collective-permute-start = (bf16[784,128]{1,0:T(8,128)(2,1)S(1)}, bf16[784,128]{1,0:T(8,128)(2,1)S(1)}, u32[]{:S(2)}, u32[]{:S(2)}) collective-permute-start(bf16[784,128]{1,0:T(8,128)(2,1)S(1)} %get-tuple-element.9), channel_id=1, source_target_pairs={{0,2},{1,3},{2,0},{3,1},{4,6},{5,7},{6,4},{7,5},{8,10},{9,11},{10,... | collective-permute-start | bytes 602120 | tf_op jit(solution)/shard_map/ppermute | solution.py:143
  10.6 2.5 %collective-permute-start.6 = (bf16[256,512]{1,0:T(8,128)(2,1)S(1)}, bf16[256,512]{1,0:T(8,128)(2,1)S(1)}, u32[]{:S(2)}, u32[]{:S(2)}) collective-permute-start(bf16[256,512]{1,0:T(8,128)(2,1)S(1)} %get-tuple-element.11.refs_2_.refs_4_), channel_id=1, source_target_pairs={{0,12},{4,8},{8,4},{12,0},{1,13},{5,9},{9,5},{13,1},{2,14},{6,10},... | collective-permute-start | bytes 786440 | tf_op jit(solution)/shard_map/ppermute | solution.py:143
  13.1 0.3 collective-permute-start.1
  13.4 1.6 %collective-permute-start.7 = (bf16[1568,128]{1,0:T(8,128)(2,1)S(1)}, bf16[1568,128]{1,0:T(8,128)(2,1)S(1)}, u32[]{:S(2)}, u32[]{:S(2)}) collective-permute-start(bf16[1568,128]{1,0:T(8,128)(2,1)S(1)} %get-tuple-element.12.refs_0_), channel_id=1, source_target_pairs={{0,1},{1,0},{2,3},{3,2},{4,5},{5,4},{6,7},{7,6},{8,9},{9,8},{10,11... | collective-permute-start | bytes 1204232 | tf_op jit(solution)/shard_map/ppermute | solution.py:143
  15.0 0.5 %collective-permute-start.5 = (bf16[256,512]{1,0:T(8,128)(2,1)S(1)}, bf16[256,512]{1,0:T(8,128)(2,1)S(1)}, u32[]{:S(2)}, u32[]{:S(2)}) collective-permute-start(bf16[256,512]{1,0:T(8,128)(2,1)S(1)} %get-tuple-element.11.refs_2_.refs_4_), channel_id=1, source_target_pairs={{0,8},{4,12},{8,0},{12,4},{1,9},{5,13},{9,1},{13,5},{2,10},{6,14},... | collective-permute-start | bytes 786440 | tf_op jit(solution)/shard_map/ppermute | solution.py:143
  15.5 9.6 %collective-permute-done.refs_0_ = bf16[784,128]{1,0:T(8,128)(2,1)S(1)} collective-permute-done((bf16[784,128]{1,0:T(8,128)(2,1)S(1)}, bf16[784,128]{1,0:T(8,128)(2,1)S(1)}, u32[]{:S(2)}, u32[]{:S(2)}) %collective-permute-start) | collective-permute-done | bytes 200736 | tf_op jit(solution)/shard_map/ppermute | solution.py:143
  25.1 1.8 %collective-permute-start.4 = (bf16[256,512]{1,0:T(8,128)(2,1)S(1)}, bf16[256,512]{1,0:T(8,128)(2,1)S(1)}, u32[]{:S(2)}, u32[]{:S(2)}) collective-permute-start(bf16[256,512]{1,0:T(8,128)(2,1)S(1)} %get-tuple-element.11.refs_2_.refs_4_), channel_id=1, source_target_pairs={{0,4},{4,0},{8,12},{12,8},{1,5},{5,1},{9,13},{13,9},{2,6},{6,2},{1... | collective-permute-start | bytes 786440 | tf_op jit(solution)/shard_map/ppermute | solution.py:143
  27.0 1.6 %collective-permute-done.1.refs_1_ = bf16[784,128]{1,0:T(8,128)(2,1)S(1)} collective-permute-done((bf16[784,128]{1,0:T(8,128)(2,1)S(1)}, bf16[784,128]{1,0:T(8,128)(2,1)S(1)}, u32[]{:S(2)}, u32[]{:S(2)}) %collective-permute-start.1) | collective-permute-done | bytes 200736 | tf_op jit(solution)/shard_map/ppermute | solution.py:143
  28.6 0.7 %collective-permute-start.2 = (bf16[784,128]{1,0:T(8,128)(2,1)S(1)}, bf16[784,128]{1,0:T(8,128)(2,1)S(1)}, u32[]{:S(2)}, u32[]{:S(2)}) collective-permute-start(bf16[784,128]{1,0:T(8,128)(2,1)S(1)} %collective-permute-done.refs_0_), channel_id=1, source_target_pairs={{0,1},{1,0},{2,3},{3,2},{4,5},{5,4},{6,7},{7,6},{8,9},{9,8},{10,11... | collective-permute-start | bytes 602120 | tf_op jit(solution)/shard_map/ppermute | solution.py:143
  29.3 0.0 collective-permute-done.6.refs_5_.refs_7_
  29.3 1.4 %collective-permute-start.3 = (bf16[784,128]{1,0:T(8,128)(2,1)S(1)}, bf16[784,128]{1,0:T(8,128)(2,1)S(1)}, u32[]{:S(2)}, u32[]{:S(2)}) collective-permute-start(bf16[784,128]{1,0:T(8,128)(2,1)S(1)} %collective-permute-done.1.refs_1_), channel_id=1, source_target_pairs={{0,1},{1,0},{2,3},{3,2},{4,5},{5,4},{6,7},{7,6},{8,9},{9,8},{10,11... | collective-permute-start | bytes 602120 | tf_op jit(solution)/shard_map/ppermute | solution.py:143
  30.6 0.0 collective-permute-done.5.refs_4_.refs_6_
  30.7 1.1 %collective-permute-done.4.refs_3_.refs_5_ = bf16[256,512]{1,0:T(8,128)(2,1)S(1)} collective-permute-done((bf16[256,512]{1,0:T(8,128)(2,1)S(1)}, bf16[256,512]{1,0:T(8,128)(2,1)S(1)}, u32[]{:S(2)}, u32[]{:S(2)}) %collective-permute-start.4) | collective-permute-done | bytes 262176 | tf_op jit(solution)/shard_map/ppermute | solution.py:143
  31.7 0.0 collective-permute-done.7.refs_1_
  31.7 1.6 %accumulate_tiles.2.refs_8_ = f32[1024,512]{1,0:T(8,128)S(1)} custom-call(bf16[1568,128]{1,0:T(8,128)(2,1)S(1)} %get-tuple-element.12.refs_0_, bf16[1568,128]{1,0:T(8,128)(2,1)S(1)} %collective-permute-done.7.refs_1_, bf16[256,512]{1,0:T(8,128)(2,1)S(1)} %get-tuple-element.11.refs_2_.refs_4_, bf16[256,512]{1,0:T(8,128)(2,1)S(1)} %collective-permute-done.4.refs_3_.refs_5_, ...), custom_call_target="tpu_custom_call" | custom-call | tf_op jit(solution)/shard_map/accumulate_tiles/pallas_call | solution.py:108
  33.4 0.0 copy-start
  33.4 3.2 %collective-permute-done.2.refs_2_ = bf16[784,128]{1,0:T(8,128)(2,1)S(1)} collective-permute-done((bf16[784,128]{1,0:T(8,128)(2,1)S(1)}, bf16[784,128]{1,0:T(8,128)(2,1)S(1)}, u32[]{:S(2)}, u32[]{:S(2)}) %collective-permute-start.2) | collective-permute-done | bytes 200736 | tf_op jit(solution)/shard_map/ppermute | solution.py:143
  36.5 3.1 %collective-permute-done.3.refs_3_ = bf16[784,128]{1,0:T(8,128)(2,1)S(1)} collective-permute-done((bf16[784,128]{1,0:T(8,128)(2,1)S(1)}, bf16[784,128]{1,0:T(8,128)(2,1)S(1)}, u32[]{:S(2)}, u32[]{:S(2)}) %collective-permute-start.3) | collective-permute-done | bytes 200736 | tf_op jit(solution)/shard_map/ppermute | solution.py:143
  39.6 1.6 %accumulate_tiles.3.mine = f32[1024,512]{1,0:T(8,128)S(1)} custom-call(bf16[784,128]{1,0:T(8,128)(2,1)S(1)} %collective-permute-done.refs_0_, bf16[784,128]{1,0:T(8,128)(2,1)S(1)} %collective-permute-done.1.refs_1_, bf16[784,128]{1,0:T(8,128)(2,1)S(1)} %collective-permute-done.2.refs_2_, bf16[784,128]{1,0:T(8,128)(2,1)S(1)} %collective-permute-done.3.refs_3_, ...), custom_call_target="tpu_custom_call" | custom-call | tf_op jit(solution)/shard_map/accumulate_tiles/pallas_call | solution.py:108
  41.3 0.1 collective-permute-start.8
  41.4 4.1 %collective-permute-done.8.other = f32[1024,512]{1,0:T(8,128)S(1)} collective-permute-done((f32[1024,512]{1,0:T(8,128)S(1)}, f32[1024,512]{1,0:T(8,128)S(1)}, u32[]{:S(2)}, u32[]{:S(2)}) %collective-permute-start.8) | collective-permute-done | bytes 2097184 | tf_op jit(solution)/shard_map/ppermute | solution.py:181
  45.5 0.0 copy-done
  45.5 3.0 %subtract_layers.1 = f32[1024,512]{1,0:T(8,128)} custom-call(f32[1024,512]{1,0:T(8,128)S(1)} %copy-done, f32[1024,512]{1,0:T(8,128)S(1)} %accumulate_tiles.3.mine, f32[1024,512]{1,0:T(8,128)S(1)} %collective-permute-done.8.other), custom_call_target="tpu_custom_call" | custom-call | tf_op jit(solution)/shard_map/subtract_layers/pallas_call | solution.py:131
  (4 shorter events, 0.0 us)
Async XLA Ops:
  1.5 1.0 %copy-start.1 = (bf16[1,2,6,128,128]{4,3,2,1,0:T(8,128)(2,1)S(1)}, bf16[1,2,6,128,128]{4,3,2,1,0:T(8,128)(2,1)}, u32[]{:S(2)}) copy-start(bf16[1,2,6,128,128]{4,3,2,1,0:T(8,128)(2,1)} %param.9) | copy-start | bytes 1179652
  2.5 0.9 %copy-start.2 = (bf16[1,2,3,128,128]{4,3,2,1,0:T(8,128)(2,1)S(1)}, bf16[1,2,3,128,128]{4,3,2,1,0:T(8,128)(2,1)}, u32[]{:S(2)}) copy-start(bf16[1,2,3,128,128]{4,3,2,1,0:T(8,128)(2,1)} %param.13) | copy-start | bytes 589828
  3.4 0.8 %copy-start.3 = (bf16[1,2,128,128]{3,2,1,0:T(8,128)(2,1)S(1)}, bf16[1,2,128,128]{3,2,1,0:T(8,128)(2,1)}, u32[]{:S(2)}) copy-start(bf16[1,2,128,128]{3,2,1,0:T(8,128)(2,1)} %param.12) | copy-start | bytes 196612
  4.2 0.7 %copy-start.4 = (s32[1,2,6]{2,1,0:T(2,128)S(1)}, s32[1,2,6]{2,1,0:T(2,128)}, u32[]{:S(2)}) copy-start(s32[1,2,6]{2,1,0:T(2,128)} %row_ids.1) | copy-start | bytes 148
  4.9 0.7 %copy-start.5 = (s32[1,2,3]{2,1,0:T(2,128)S(1)}, s32[1,2,3]{2,1,0:T(2,128)}, u32[]{:S(2)}) copy-start(s32[1,2,3]{2,1,0:T(2,128)} %col_ids.1) | copy-start | bytes 76
  6.5 18.6 %collective-permute-start = (bf16[784,128]{1,0:T(8,128)(2,1)S(1)}, bf16[784,128]{1,0:T(8,128)(2,1)S(1)}, u32[]{:S(2)}, u32[]{:S(2)}) collective-permute-start(bf16[784,128]{1,0:T(8,128)(2,1)S(1)} %get-tuple-element.9), channel_id=1, source_target_pairs={{0,2},{1,3},{2,0},{3,1},{4,6},{5,7},{6,4},{7,5},{8,10},{9,11},{10,... | collective-permute-start | bytes 602120 | tf_op jit(solution)/shard_map/ppermute | solution.py:143
  10.6 18.7 %collective-permute-start.6 = (bf16[256,512]{1,0:T(8,128)(2,1)S(1)}, bf16[256,512]{1,0:T(8,128)(2,1)S(1)}, u32[]{:S(2)}, u32[]{:S(2)}) collective-permute-start(bf16[256,512]{1,0:T(8,128)(2,1)S(1)} %get-tuple-element.11.refs_2_.refs_4_), channel_id=1, source_target_pairs={{0,12},{4,8},{8,4},{12,0},{1,13},{5,9},{9,5},{13,1},{2,14},{6,10},... | collective-permute-start | bytes 786440 | tf_op jit(solution)/shard_map/ppermute | solution.py:143
  13.1 15.6 %collective-permute-start.1 = (bf16[784,128]{1,0:T(8,128)(2,1)S(1)}, bf16[784,128]{1,0:T(8,128)(2,1)S(1)}, u32[]{:S(2)}, u32[]{:S(2)}) collective-permute-start(bf16[784,128]{1,0:T(8,128)(2,1)S(1)} %get-tuple-element.10), channel_id=1, source_target_pairs={{0,2},{1,3},{2,0},{3,1},{4,6},{5,7},{6,4},{7,5},{8,10},{9,11},{10,... | collective-permute-start | bytes 602120 | tf_op jit(solution)/shard_map/ppermute | solution.py:143
  13.4 18.3 %collective-permute-start.7 = (bf16[1568,128]{1,0:T(8,128)(2,1)S(1)}, bf16[1568,128]{1,0:T(8,128)(2,1)S(1)}, u32[]{:S(2)}, u32[]{:S(2)}) collective-permute-start(bf16[1568,128]{1,0:T(8,128)(2,1)S(1)} %get-tuple-element.12.refs_0_), channel_id=1, source_target_pairs={{0,1},{1,0},{2,3},{3,2},{4,5},{5,4},{6,7},{7,6},{8,9},{9,8},{10,11... | collective-permute-start | bytes 1204232 | tf_op jit(solution)/shard_map/ppermute | solution.py:143
  15.0 15.7 %collective-permute-start.5 = (bf16[256,512]{1,0:T(8,128)(2,1)S(1)}, bf16[256,512]{1,0:T(8,128)(2,1)S(1)}, u32[]{:S(2)}, u32[]{:S(2)}) collective-permute-start(bf16[256,512]{1,0:T(8,128)(2,1)S(1)} %get-tuple-element.11.refs_2_.refs_4_), channel_id=1, source_target_pairs={{0,8},{4,12},{8,0},{12,4},{1,9},{5,13},{9,1},{13,5},{2,10},{6,14},... | collective-permute-start | bytes 786440 | tf_op jit(solution)/shard_map/ppermute | solution.py:143
  25.1 6.6 %collective-permute-start.4 = (bf16[256,512]{1,0:T(8,128)(2,1)S(1)}, bf16[256,512]{1,0:T(8,128)(2,1)S(1)}, u32[]{:S(2)}, u32[]{:S(2)}) collective-permute-start(bf16[256,512]{1,0:T(8,128)(2,1)S(1)} %get-tuple-element.11.refs_2_.refs_4_), channel_id=1, source_target_pairs={{0,4},{4,0},{8,12},{12,8},{1,5},{5,1},{9,13},{13,9},{2,6},{6,2},{1... | collective-permute-start | bytes 786440 | tf_op jit(solution)/shard_map/ppermute | solution.py:143
  28.6 7.9 %collective-permute-start.2 = (bf16[784,128]{1,0:T(8,128)(2,1)S(1)}, bf16[784,128]{1,0:T(8,128)(2,1)S(1)}, u32[]{:S(2)}, u32[]{:S(2)}) collective-permute-start(bf16[784,128]{1,0:T(8,128)(2,1)S(1)} %collective-permute-done.refs_0_), channel_id=1, source_target_pairs={{0,1},{1,0},{2,3},{3,2},{4,5},{5,4},{6,7},{7,6},{8,9},{9,8},{10,11... | collective-permute-start | bytes 602120 | tf_op jit(solution)/shard_map/ppermute | solution.py:143
  29.3 10.4 %collective-permute-start.3 = (bf16[784,128]{1,0:T(8,128)(2,1)S(1)}, bf16[784,128]{1,0:T(8,128)(2,1)S(1)}, u32[]{:S(2)}, u32[]{:S(2)}) collective-permute-start(bf16[784,128]{1,0:T(8,128)(2,1)S(1)} %collective-permute-done.1.refs_1_), channel_id=1, source_target_pairs={{0,1},{1,0},{2,3},{3,2},{4,5},{5,4},{6,7},{7,6},{8,9},{9,8},{10,11... | collective-permute-start | bytes 602120 | tf_op jit(solution)/shard_map/ppermute | solution.py:143
  33.4 12.2 %copy-start = (f32[1024,512]{1,0:T(8,128)S(1)}, f32[1024,512]{1,0:T(8,128)}, u32[]{:S(2)}) copy-start(f32[1024,512]{1,0:T(8,128)} %ancestor.1) | copy-start | bytes 6291460
  41.3 4.2 %collective-permute-start.8 = (f32[1024,512]{1,0:T(8,128)S(1)}, f32[1024,512]{1,0:T(8,128)S(1)}, u32[]{:S(2)}, u32[]{:S(2)}) collective-permute-start(f32[1024,512]{1,0:T(8,128)S(1)} %accumulate_tiles.3.mine), channel_id=1, source_target_pairs={{0,16},{16,0},{1,17},{17,1},{2,18},{18,2},{3,19},{19,3},{4,20},{20... | collective-permute-start | bytes 6291464 | tf_op jit(solution)/shard_map/ppermute | solution.py:181

commit v2 on v0

v2 whole, which is shorter than its diff:
```python
import functools

import jax
import jax.numpy as jnp
from jax import lax
from jax.experimental import pallas as pl
from jax.experimental.pallas import tpu as pltpu
from jax.sharding import PartitionSpec as P

VMEM_LIMIT = 24 * 1024 * 1024
ID_ROWS = 16
ROW_STEPS = 4


def whole_vmem():
    return pl.BlockSpec(memory_space=pltpu.VMEM)


def prepare_kernel(
    row_ids_in, row_counts_in, col_ids_in, col_counts_in, lower_in, inverse_in, upper_in,
    solved_out, spread,
    row_ids, row_counts, col_ids, col_counts, lower, inverse, upper, arrived,
):
    supernodes, slots, width, _ = lower.shape
    chunk = slots * width + ID_ROWS
    pairs = (
        (row_ids_in, row_ids),
        (row_counts_in, row_counts),
        (inverse_in.at[0], inverse),
        (lower_in.at[0, 0], lower.at[0]),
        (lower_in.at[0, 1], lower.at[1]),
        (col_ids_in, col_ids),
        (col_counts_in, col_counts),
        (upper_in.at[0], upper),
    )
    copies = [pltpu.make_async_copy(src, dst, arrived.at[n]) for n, (src, dst) in enumerate(pairs)]
    for copy in copies:
        copy.start()
    spread[...] = jnp.zeros_like(spread)
    for copy in copies[:3]:
        copy.wait()
    for k in range(supernodes):
        copies[3 + k].wait()
        tiles = lower[k].reshape(slots * width, width)
        solved = jnp.dot(tiles, inverse[k], preferred_element_type=jnp.float32).astype(jnp.bfloat16)
        solved_out[k * chunk : k * chunk + slots * width, :] = solved
        at_row = lax.broadcasted_iota(jnp.int32, (ID_ROWS, width), 0)
        ids = jnp.zeros((ID_ROWS, width), jnp.int32)
        for s in range(slots):
            place = jnp.where(s < row_counts[0, 0, k], row_ids[0, k, s] + 1, 0)
            ids = jnp.where(at_row == s, place, ids)
        solved_out[k * chunk + slots * width : (k + 1) * chunk, :] = ids.astype(jnp.float32).astype(jnp.bfloat16)
    for copy in copies[5:]:
        copy.wait()
    for k in range(supernodes):
        for c in range(upper.shape[1]):

            @pl.when(c < col_counts[0, 0, k])
            def _():
                at = pl.multiple_of(col_ids[0, k, c] * width, width)
                spread[k * width : (k + 1) * width, pl.ds(at, width)] = upper[k, c]


def prepare(lower, row_ids, row_counts, inverse, upper, col_ids, col_counts, col_blocks):
    _, supernodes, slots, width, _ = lower.shape
    chunk = slots * width + ID_ROWS
    row_counts = jnp.swapaxes(row_counts, 1, 2)
    col_counts = jnp.swapaxes(col_counts, 1, 2)
    return pl.pallas_call(
        prepare_kernel,
        out_shape=(
            jax.ShapeDtypeStruct((supernodes * chunk, width), jnp.bfloat16),
            jax.ShapeDtypeStruct((supernodes * width, col_blocks * width), jnp.bfloat16),
        ),
        in_specs=[pl.BlockSpec(memory_space=pltpu.HBM)] * 7,
        out_specs=(whole_vmem(),) * 2,
        scratch_shapes=[
            pltpu.SMEM(row_ids.shape, jnp.int32),
            pltpu.SMEM(row_counts.shape, jnp.int32),
            pltpu.SMEM(col_ids.shape, jnp.int32),
            pltpu.SMEM(col_counts.shape, jnp.int32),
            pltpu.VMEM(lower.shape[1:], jnp.bfloat16),
            pltpu.VMEM(inverse.shape[1:], jnp.bfloat16),
            pltpu.VMEM(upper.shape[1:], jnp.bfloat16),
            pltpu.SemaphoreType.DMA((8,)),
        ],
        compiler_params=pltpu.CompilerParams(vmem_limit_bytes=VMEM_LIMIT),
        name="solve_and_pack",
    )(
        *(
            pltpu.with_memory_space_constraint(array, pltpu.HBM)
            for array in (row_ids, row_counts, col_ids, col_counts, lower, inverse, upper)
        )
    )


def place_tiles(panel, k, slots, left, at_col):
    width = panel.shape[1]
    chunk = slots * width + ID_ROWS
    start = k * chunk
    ids = panel[start + slots * width : start + chunk, :].astype(jnp.float32).astype(jnp.int32)
    for s in range(slots):
        at = pl.multiple_of(ids[s, 0] * width, width)
        left[pl.ds(at, width), at_col] = panel[start + s * width : start + (s + 1) * width, :]


def order_kernel(count, *refs):
    pieces, out = refs[:count], refs[-1]
    tall = pieces[0].shape[0]
    row = lax.axis_index("row")
    for j, piece in enumerate(pieces):
        out[pl.ds(pl.multiple_of((row ^ j) * tall, tall), tall), :] = piece[...]


def in_order(pieces, after):
    tall, columns = pieces[0].shape
    return pl.pallas_call(
        functools.partial(order_kernel, len(pieces)),
        out_shape=jax.ShapeDtypeStruct((len(pieces) * tall, columns), jnp.bfloat16),
        in_specs=[whole_vmem()] * len(pieces) + [pl.BlockSpec(memory_space=pl.ANY)] * len(after),
        out_specs=whole_vmem(),
        compiler_params=pltpu.CompilerParams(vmem_limit_bytes=VMEM_LIMIT),
        name="order_uppers",
    )(*pieces, *after)


def place_groups(slots, supernodes, masks, panels, uppers, left, right):
    width = panels[0][0].shape[1]
    tall = supernodes * width
    column = lax.axis_index("col")
    layer = lax.axis_index("gz")
    left[...] = jnp.zeros_like(left)
    for side, (tiles, upper) in enumerate(zip(panels, uppers)):
        base = (layer if side == 0 else 1 - layer) * (len(masks) * tall)
        for n, mask in enumerate(masks):
            start = pl.multiple_of(base + n * tall, width)
            right[pl.ds(start, tall), :] = upper[pl.ds(pl.multiple_of((column ^ mask) * tall, tall), tall), :]
            for k in range(supernodes):
                at = pl.multiple_of(base + n * tall + k * width, width)
                place_tiles(tiles[n], k, slots, left, pl.ds(at, width))


def sum_kernel(slots, supernodes, masks, *refs):
    groups = len(masks)
    panels = (refs[:groups], refs[groups : 2 * groups])
    uppers, (out, left, right) = refs[2 * groups : 2 * groups + 2], refs[2 * groups + 2 :]
    width = panels[0][0].shape[1]
    place_groups(slots, supernodes, masks, panels, uppers, left, right)
    rows = out.shape[0] // ROW_STEPS
    for i in range(ROW_STEPS):
        out[i * rows : (i + 1) * rows, :] = jnp.dot(
            left[width + i * rows : width + (i + 1) * rows, :], right[...], preferred_element_type=jnp.float32
        )


def sum_groups(masks, own, other, uppers, shape, slots, supernodes):
    width = own[0].shape[1]
    depth = 2 * len(masks) * supernodes * width
    return pl.pallas_call(
        functools.partial(sum_kernel, slots, supernodes, tuple(masks)),
        out_shape=jax.ShapeDtypeStruct(shape, jnp.float32),
        in_specs=[whole_vmem()] * (2 * len(masks) + 2),
        out_specs=whole_vmem(),
        scratch_shapes=[
            pltpu.VMEM((shape[0] + width, depth), jnp.bfloat16),
            pltpu.VMEM((depth, shape[1]), jnp.bfloat16),
        ],
        compiler_params=pltpu.CompilerParams(vmem_limit_bytes=VMEM_LIMIT),
        name="sum_groups",
    )(*own, *other, *uppers)


def finish_kernel(slots, supernodes, mask, ancestor, early, own, other, own_upper, far_upper, out, left, right, result, sent):
    width = own.shape[1]
    place_groups(slots, supernodes, (mask,), ((own,), (other,)), (own_upper, far_upper), left, right)
    rows = out.shape[0] // ROW_STEPS
    copies = []
    for i in range(ROW_STEPS):
        block = slice(i * rows, (i + 1) * rows)
        update = jnp.dot(
            left[width + i * rows : width + (i + 1) * rows, :], right[...], preferred_element_type=jnp.float32
        )
        result[block, :] = ancestor[block, :] - (early[block, :] + update)
        copy = pltpu.make_async_copy(result.at[block], out.at[block], sent.at[i])
        copy.start()
        copies.append(copy)
    for copy in copies:
        copy.wait()


def finish(ancestor, early, mask, own, other, uppers, slots, supernodes):
    width = own.shape[1]
    depth = 2 * supernodes * width
    return pl.pallas_call(
        functools.partial(finish_kernel, slots, supernodes, mask),
        out_shape=jax.ShapeDtypeStruct(ancestor.shape, jnp.float32),
        in_specs=[whole_vmem()] * 6,
        out_specs=pl.BlockSpec(memory_space=pltpu.HBM),
        scratch_shapes=[
            pltpu.VMEM((ancestor.shape[0] + width, depth), jnp.bfloat16),
            pltpu.VMEM((depth, ancestor.shape[1]), jnp.bfloat16),
            pltpu.VMEM(ancestor.shape, jnp.float32),
            pltpu.SemaphoreType.DMA((ROW_STEPS,)),
        ],
        compiler_params=pltpu.CompilerParams(vmem_limit_bytes=VMEM_LIMIT),
        name="last_group_and_subtract",
    )(ancestor, early, own, other, *uppers)


def swap(array, axis, mask):
    return lax.ppermute(array, axis, [(i, i ^ mask) for i in range(4)])


def siblings(array):
    return lax.ppermute(array, "gz", [(0, 1), (1, 0)])


def on_line_of_four(
    ancestor, lower_panel, row_ids, row_counts, diag_inverse, upper_panel, col_ids, col_counts
):
    width = lower_panel.shape[-1]
    supernodes, slots = lower_panel.shape[1:3]
    mine, spread = prepare(
        lower_panel,
        row_ids,
        row_counts,
        diag_inverse,
        upper_panel,
        col_ids,
        col_counts,
        ancestor.shape[1] // width,
    )
    far = swap(mine, "col", 2)
    near = swap(mine, "col", 1)
    last = swap(far, "col", 1)
    upper = in_order([spread] + [swap(spread, "row", j) for j in (1, 2, 3)], [near, far])
    uppers = (upper, siblings(upper))
    panels = (mine, near, far)
    early = sum_groups(
        (0, 1, 2), panels, [siblings(panel) for panel in panels], uppers, ancestor.shape, slots, supernodes
    )
    return finish(ancestor, early, 3, last, siblings(last), uppers, slots, supernodes)


def spread_tiles(tiles, ids, counts, blocks, rule):
    slot_index = jnp.arange(ids.shape[1], dtype=jnp.int32)
    alive = slot_index[None, :] < counts
    target = jnp.arange(blocks, dtype=jnp.int32)
    select = ((ids[:, :, None] == target[None, None, :]) & alive[:, :, None]).astype(jnp.bfloat16)
    return jnp.einsum(rule, select, tiles, preferred_element_type=jnp.float32).astype(jnp.bfloat16)


def on_device(
    ancestor, lower_panel, row_ids, row_counts, diag_inverse, upper_panel, col_ids, col_counts
):
    width = lower_panel.shape[-1]
    rows, columns = ancestor.shape
    solved = jnp.einsum(
        "ksab,kbc->ksac", lower_panel[0], diag_inverse[0], preferred_element_type=jnp.float32
    ).astype(jnp.bfloat16)
    piece = lax.all_gather((upper_panel[0], col_ids[0], col_counts[0]), "row", axis=0, tiled=True)
    upper_dense = spread_tiles(*piece, columns // width, "kcm,kcab->kamb").reshape(-1, columns)
    piece = lax.all_gather((solved, row_ids[0], row_counts[0]), "col", axis=0, tiled=True)
    lower_dense = spread_tiles(*piece, rows // width, "krl,krab->lakb").reshape(rows, -1)
    partial_sum = jnp.dot(lower_dense, upper_dense, preferred_element_type=jnp.float32)
    return ancestor - lax.psum(partial_sum, "gz")


def solution(mesh):
    placed = (
        P("row", "col"),
        P("gz", "col", "row", None, None),
        P("gz", "col", "row"),
        P("gz", "col", "row"),
        P("gz", "col", None, None),
        P("gz", "row", "col", None, None),
        P("gz", "row", "col"),
        P("gz", "row", "col"),
    )
    sizes = dict(mesh.shape)
    small = sizes["gz"] == 2 and sizes["row"] == 4 and sizes["col"] == 4

    def run(ancestor, lower_panel, *rest):
        two = lower_panel.shape[1] == 2 * sizes["col"]
        body = on_line_of_four if small and two else on_device
        return jax.shard_map(
            body, mesh=mesh, in_specs=placed, out_specs=P("row", "col"), check_vma=False
        )(ancestor, lower_panel, *rest)

    return run
```

time: 97.1 us -> 40.5 us (0.42)
  blocking collectives: 45.7 us -> 0 us
  between operations: 14.7 us -> 0.08 us
  starting transfers between devices: 0.04 us -> 11.5 us
  matrix products: 7.65 us -> 0 us
  local copies, waits for them, and re-layouts: 6.4 us -> 0.01 us
  Pallas kernels: 0 us -> 6.14 us
  waiting for transfers between devices: 18.7 us -> 22.6 us
  other arithmetic: 3.53 us -> 0 us
    all_gather x3 -> x0, blocking collectives: 27.9 us -> none  [the longest x2 18.5 us: on_device(): lax.all_gather((upper_panel[0], col_ids[0], col_counts[0]), 'row', axis=0...]
    ppermute x0 -> x11, waiting for transfers between devices: none -> 22.6 us  [the longest x6 22.6 us: swap(): return lax.ppermute(array, axis, [(i, i ^ mask) for i in range(4)])]
    psum x1 -> x0, waiting for transfers between devices: 18.6 us -> none  [on_device(): return ancestor - lax.psum(partial_sum, 'gz')]
    unnamed x2 -> x0, blocking collectives: 17.8 us -> none
    ppermute x0 -> x11, starting transfers between devices: none -> 11.5 us  [the longest x6 10.7 us: swap(): return lax.ppermute(array, axis, [(i, i ^ mask) for i in range(4)])]
    dot_general x4 -> x0, matrix products: 7.65 us -> none  [the longest x1 2.57 us: on_device(): jnp.dot(lower_dense, upper_dense, preferred_element_type=jnp.float32)]
    pallas_call x0 -> x4, Pallas kernels: none -> 6.14 us  [the longest x1 2.56 us: sum_groups(): pl.pallas_call(functools.partial(sum_kernel, slots, supernodes, tuple(mas...]
    unnamed x10 -> x2, local copies, waits for them, and re-layouts: 5.04 us -> 0.01 us
  transfers between devices with their start and end apart: 2 -> 11, of which waited for: 1 -> 5; matrix products, arithmetic and copies ran while one was open for 5% -> 0% of each run, Pallas kernels for 0% -> 6%
where the time goes in v2:
time: 40.5 us; the launch traced here: 40.3 us
  waiting for transfers between devices  22.6 us (56%)
  starting transfers between devices  11.5 us (28%)
  Pallas kernels  6.14 us (15%)
    ppermute x6, waiting for transfers between devices, swap(): return lax.ppermute(array, axis, [(i, i ^ mask) for i in range(4)])  22.6 us
    ppermute x6, starting transfers between devices, swap(): return lax.ppermute(array, axis, [(i, i ^ mask) for i in range(4)])  10.7 us
    pallas_call x1, Pallas kernels, sum_groups(): pl.pallas_call(functools.partial(sum_kernel, slots, supernodes, tuple(mas...  2.56 us
    pallas_call x1, Pallas kernels, finish(): pl.pallas_call(functools.partial(finish_kernel, slots, supernodes, mask),...  1.9 us
    pallas_call x1, Pallas kernels, prepare(): pl.pallas_call(prepare_kernel, out_shape=(jax.ShapeDtypeStruct((supernode...  1.6 us
  transfers between devices with their start and end apart: 11, of which 5 were waited for; matrix products, arithmetic and copies ran while one was open for 0% of the time, Pallas kernels for 6%

profile of v2, /device:TPU:0, one launch (start us, length us, event | category | flops | bytes accessed | tf_op | source)
XLA Modules:
  0.0 40.3 jit_solution(5118921843033098585)
XLA Ops:
  0.0 1.6 %solve_and_pack.1 = (bf16[1568,128]{1,0:T(8,128)(2,1)S(1)}, bf16[256,512]{1,0:T(8,128)(2,1)S(1)}) custom-call(s32[1,2,6]{2,1,0:T(2,128)} %row_ids_in.1, s32[1,1,2]{2,1,0:T(1,128)} %bitcast.2, s32[1,2,3]{2,1,0:T(2,128)} %col_ids_in.1, s32[1,1,2]{2,1,0:T(1,128)} %bitcast.3, bf16[1,2,6,128,128]{4,3,2,1,0:T(8,128)(2,1)} %lower_in.1, ...), custom_call_target="tpu_custom_call" | custom-call | tf_op jit(solution)/shard_map/solve_and_pack/pallas_call | solution.py:69
  1.6 4.1 %collective-permute-start.1 = (bf16[1568,128]{1,0:T(8,128)(2,1)S(1)}, bf16[1568,128]{1,0:T(8,128)(2,1)S(1)}, u32[]{:S(2)}, u32[]{:S(2)}) collective-permute-start(bf16[1568,128]{1,0:T(8,128)(2,1)S(1)} %get-tuple-element.7.refs_0_), channel_id=1, source_target_pairs={{0,2},{1,3},{2,0},{3,1},{4,6},{5,7},{6,4},{7,5},{8,10},{9,11},{10,... | collective-permute-start | bytes 1204232 | tf_op jit(solution)/shard_map/ppermute | solution.py:211
  5.7 1.6 %collective-permute-start = (bf16[1568,128]{1,0:T(8,128)(2,1)S(1)}, bf16[1568,128]{1,0:T(8,128)(2,1)S(1)}, u32[]{:S(2)}, u32[]{:S(2)}) collective-permute-start(bf16[1568,128]{1,0:T(8,128)(2,1)S(1)} %get-tuple-element.7.refs_0_), channel_id=1, source_target_pairs={{0,1},{1,0},{2,3},{3,2},{4,5},{5,4},{6,7},{7,6},{8,9},{9,8},{10,11... | collective-permute-start | bytes 1204232 | tf_op jit(solution)/shard_map/ppermute | solution.py:211
  7.3 1.5 %collective-permute-start.5 = (bf16[256,512]{1,0:T(8,128)(2,1)S(1)}, bf16[256,512]{1,0:T(8,128)(2,1)S(1)}, u32[]{:S(2)}, u32[]{:S(2)}) collective-permute-start(bf16[256,512]{1,0:T(8,128)(2,1)S(1)} %get-tuple-element.8.refs_0_), channel_id=1, source_target_pairs={{0,4},{4,0},{8,12},{12,8},{1,5},{5,1},{9,13},{13,9},{2,6},{6,2},{1... | collective-permute-start | bytes 786440 | tf_op jit(solution)/shard_map/ppermute | solution.py:211
  8.8 1.5 %collective-permute-start.6 = (bf16[256,512]{1,0:T(8,128)(2,1)S(1)}, bf16[256,512]{1,0:T(8,128)(2,1)S(1)}, u32[]{:S(2)}, u32[]{:S(2)}) collective-permute-start(bf16[256,512]{1,0:T(8,128)(2,1)S(1)} %get-tuple-element.8.refs_0_), channel_id=1, source_target_pairs={{0,8},{4,12},{8,0},{12,4},{1,9},{5,13},{9,1},{13,5},{2,10},{6,14},... | collective-permute-start | bytes 786440 | tf_op jit(solution)/shard_map/ppermute | solution.py:211
  10.3 0.5 %collective-permute-start.7 = (bf16[256,512]{1,0:T(8,128)(2,1)S(1)}, bf16[256,512]{1,0:T(8,128)(2,1)S(1)}, u32[]{:S(2)}, u32[]{:S(2)}) collective-permute-start(bf16[256,512]{1,0:T(8,128)(2,1)S(1)} %get-tuple-element.8.refs_0_), channel_id=1, source_target_pairs={{0,12},{4,8},{8,4},{12,0},{1,13},{5,9},{9,5},{13,1},{2,14},{6,10},... | collective-permute-start | bytes 786440 | tf_op jit(solution)/shard_map/ppermute | solution.py:211
  10.8 5.8 %collective-permute-done.5.refs_1_ = bf16[256,512]{1,0:T(8,128)(2,1)S(1)} collective-permute-done((bf16[256,512]{1,0:T(8,128)(2,1)S(1)}, bf16[256,512]{1,0:T(8,128)(2,1)S(1)}, u32[]{:S(2)}, u32[]{:S(2)}) %collective-permute-start.5) | collective-permute-done | bytes 262176 | tf_op jit(solution)/shard_map/ppermute | solution.py:211
  16.5 5.1 %collective-permute-done.6.refs_2_ = bf16[256,512]{1,0:T(8,128)(2,1)S(1)} collective-permute-done((bf16[256,512]{1,0:T(8,128)(2,1)S(1)}, bf16[256,512]{1,0:T(8,128)(2,1)S(1)}, u32[]{:S(2)}, u32[]{:S(2)}) %collective-permute-start.6) | collective-permute-done | bytes 262176 | tf_op jit(solution)/shard_map/ppermute | solution.py:211
  21.6 0.0 collective-permute-done.7.refs_3_
  21.6 2.1 %collective-permute-done.1.refs_5_.refs_2_ = bf16[1568,128]{1,0:T(8,128)(2,1)S(1)} collective-permute-done((bf16[1568,128]{1,0:T(8,128)(2,1)S(1)}, bf16[1568,128]{1,0:T(8,128)(2,1)S(1)}, u32[]{:S(2)}, u32[]{:S(2)}) %collective-permute-start.1) | collective-permute-done | bytes 401440 | tf_op jit(solution)/shard_map/ppermute | solution.py:211
  23.7 0.2 collective-permute-done.refs_4_.refs_1_
  23.9 0.1 order_uppers.1.refs_6_.own_upper
  24.0 0.0 copy-start
  24.0 0.1 collective-permute-start.8
  24.1 1.6 %collective-permute-start.9 = (bf16[1568,128]{1,0:T(8,128)(2,1)S(1)}, bf16[1568,128]{1,0:T(8,128)(2,1)S(1)}, u32[]{:S(2)}, u32[]{:S(2)}) collective-permute-start(bf16[1568,128]{1,0:T(8,128)(2,1)S(1)} %collective-permute-done.1.refs_5_.refs_2_), channel_id=1, source_target_pairs={{0,1},{1,0},{2,3},{3,2},{4,5},{5,4},{6,7},{7,6},{8,9},{9,8},{10,11... | collective-permute-start | bytes 1204232 | tf_op jit(solution)/shard_map/ppermute | solution.py:211
  25.6 0.2 collective-permute-start.2
  25.8 0.3 collective-permute-start.4
  26.1 0.2 collective-permute-start.3
  26.3 9.5 %collective-permute-done.9.own = bf16[1568,128]{1,0:T(8,128)(2,1)S(1)} collective-permute-done((bf16[1568,128]{1,0:T(8,128)(2,1)S(1)}, bf16[1568,128]{1,0:T(8,128)(2,1)S(1)}, u32[]{:S(2)}, u32[]{:S(2)}) %collective-permute-start.9) | collective-permute-done | bytes 401440 | tf_op jit(solution)/shard_map/ppermute | solution.py:211
  35.8 0.0 collective-permute-start.10
  35.8 0.0 collective-permute-done.2.refs_3_
  35.8 0.0 collective-permute-done.4.refs_5_
  35.8 0.0 collective-permute-done.3.refs_4_
  35.8 0.0 collective-permute-done.8.refs_7_.far_upper
  35.8 2.6 %sum_groups.1.early = f32[1024,512]{1,0:T(8,128)S(1)} custom-call(bf16[1568,128]{1,0:T(8,128)(2,1)S(1)} %get-tuple-element.7.refs_0_, bf16[1568,128]{1,0:T(8,128)(2,1)S(1)} %collective-permute-done.refs_4_.refs_1_, bf16[1568,128]{1,0:T(8,128)(2,1)S(1)} %collective-permute-done.1.refs_5_.refs_2_, bf16[1568,128]{1,0:T(8,128)(2,1)S(1)} %collective-permute-done.2.refs_3_, ...), custom_call_target="tpu_custom_call" | custom-call | tf_op jit(solution)/shard_map/sum_groups/pallas_call | solution.py:159
  38.4 0.0 collective-permute-done.10.other
  38.4 0.0 copy-done
  38.4 1.9 %last_group_and_subtract.1 = f32[1024,512]{1,0:T(8,128)} custom-call(f32[1024,512]{1,0:T(8,128)S(1)} %copy-done, f32[1024,512]{1,0:T(8,128)S(1)} %sum_groups.1.early, bf16[1568,128]{1,0:T(8,128)(2,1)S(1)} %collective-permute-done.9.own, bf16[1568,128]{1,0:T(8,128)(2,1)S(1)} %collective-permute-done.10.other, ...), custom_call_target="tpu_custom_call" | custom-call | tf_op jit(solution)/shard_map/last_group_and_subtract/pallas_call | solution.py:194
Async XLA Ops:
  1.6 22.1 %collective-permute-start.1 = (bf16[1568,128]{1,0:T(8,128)(2,1)S(1)}, bf16[1568,128]{1,0:T(8,128)(2,1)S(1)}, u32[]{:S(2)}, u32[]{:S(2)}) collective-permute-start(bf16[1568,128]{1,0:T(8,128)(2,1)S(1)} %get-tuple-element.7.refs_0_), channel_id=1, source_target_pairs={{0,2},{1,3},{2,0},{3,1},{4,6},{5,7},{6,4},{7,5},{8,10},{9,11},{10,... | collective-permute-start | bytes 1204232 | tf_op jit(solution)/shard_map/ppermute | solution.py:211
  5.7 18.2 %collective-permute-start = (bf16[1568,128]{1,0:T(8,128)(2,1)S(1)}, bf16[1568,128]{1,0:T(8,128)(2,1)S(1)}, u32[]{:S(2)}, u32[]{:S(2)}) collective-permute-start(bf16[1568,128]{1,0:T(8,128)(2,1)S(1)} %get-tuple-element.7.refs_0_), channel_id=1, source_target_pairs={{0,1},{1,0},{2,3},{3,2},{4,5},{5,4},{6,7},{7,6},{8,9},{9,8},{10,11... | collective-permute-start | bytes 1204232 | tf_op jit(solution)/shard_map/ppermute | solution.py:211
  7.3 9.2 %collective-permute-start.5 = (bf16[256,512]{1,0:T(8,128)(2,1)S(1)}, bf16[256,512]{1,0:T(8,128)(2,1)S(1)}, u32[]{:S(2)}, u32[]{:S(2)}) collective-permute-start(bf16[256,512]{1,0:T(8,128)(2,1)S(1)} %get-tuple-element.8.refs_0_), channel_id=1, source_target_pairs={{0,4},{4,0},{8,12},{12,8},{1,5},{5,1},{9,13},{13,9},{2,6},{6,2},{1... | collective-permute-start | bytes 786440 | tf_op jit(solution)/shard_map/ppermute | solution.py:211
  8.8 12.8 %collective-permute-start.6 = (bf16[256,512]{1,0:T(8,128)(2,1)S(1)}, bf16[256,512]{1,0:T(8,128)(2,1)S(1)}, u32[]{:S(2)}, u32[]{:S(2)}) collective-permute-start(bf16[256,512]{1,0:T(8,128)(2,1)S(1)} %get-tuple-element.8.refs_0_), channel_id=1, source_target_pairs={{0,8},{4,12},{8,0},{12,4},{1,9},{5,13},{9,1},{13,5},{2,10},{6,14},... | collective-permute-start | bytes 786440 | tf_op jit(solution)/shard_map/ppermute | solution.py:211
  10.3 11.3 %collective-permute-start.7 = (bf16[256,512]{1,0:T(8,128)(2,1)S(1)}, bf16[256,512]{1,0:T(8,128)(2,1)S(1)}, u32[]{:S(2)}, u32[]{:S(2)}) collective-permute-start(bf16[256,512]{1,0:T(8,128)(2,1)S(1)} %get-tuple-element.8.refs_0_), channel_id=1, source_target_pairs={{0,12},{4,8},{8,4},{12,0},{1,13},{5,9},{9,5},{13,1},{2,14},{6,10},... | collective-permute-start | bytes 786440 | tf_op jit(solution)/shard_map/ppermute | solution.py:211
  24.0 14.4 %copy-start = (f32[1024,512]{1,0:T(8,128)S(1)}, f32[1024,512]{1,0:T(8,128)}, u32[]{:S(2)}) copy-start(f32[1024,512]{1,0:T(8,128)} %ancestor.1) | copy-start | bytes 6291460
  24.0 11.8 %collective-permute-start.8 = (bf16[1024,512]{1,0:T(8,128)(2,1)S(1)}, bf16[1024,512]{1,0:T(8,128)(2,1)S(1)}, u32[]{:S(2)}, u32[]{:S(2)}) collective-permute-start(bf16[1024,512]{1,0:T(8,128)(2,1)S(1)} %order_uppers.1.refs_6_.own_upper), channel_id=1, source_target_pairs={{0,16},{16,0},{1,17},{17,1},{2,18},{18,2},{3,19},{19,3},{4,20},{20... | collective-permute-start | bytes 3145736 | tf_op jit(solution)/shard_map/ppermute | solution.py:215
  24.1 11.7 %collective-permute-start.9 = (bf16[1568,128]{1,0:T(8,128)(2,1)S(1)}, bf16[1568,128]{1,0:T(8,128)(2,1)S(1)}, u32[]{:S(2)}, u32[]{:S(2)}) collective-permute-start(bf16[1568,128]{1,0:T(8,128)(2,1)S(1)} %collective-permute-done.1.refs_5_.refs_2_), channel_id=1, source_target_pairs={{0,1},{1,0},{2,3},{3,2},{4,5},{5,4},{6,7},{7,6},{8,9},{9,8},{10,11... | collective-permute-start | bytes 1204232 | tf_op jit(solution)/shard_map/ppermute | solution.py:211
  25.6 10.2 %collective-permute-start.2 = (bf16[1568,128]{1,0:T(8,128)(2,1)S(1)}, bf16[1568,128]{1,0:T(8,128)(2,1)S(1)}, u32[]{:S(2)}, u32[]{:S(2)}) collective-permute-start(bf16[1568,128]{1,0:T(8,128)(2,1)S(1)} %get-tuple-element.7.refs_0_), channel_id=1, source_target_pairs={{0,16},{16,0},{1,17},{17,1},{2,18},{18,2},{3,19},{19,3},{4,20},{20... | collective-permute-start | bytes 1204232 | tf_op jit(solution)/shard_map/ppermute | solution.py:215
  25.8 10.0 %collective-permute-start.4 = (bf16[1568,128]{1,0:T(8,128)(2,1)S(1)}, bf16[1568,128]{1,0:T(8,128)(2,1)S(1)}, u32[]{:S(2)}, u32[]{:S(2)}) collective-permute-start(bf16[1568,128]{1,0:T(8,128)(2,1)S(1)} %collective-permute-done.1.refs_5_.refs_2_), channel_id=1, source_target_pairs={{0,16},{16,0},{1,17},{17,1},{2,18},{18,2},{3,19},{19,3},{4,20},{20... | collective-permute-start | bytes 1204232 | tf_op jit(solution)/shard_map/ppermute | solution.py:215
  26.1 9.6 %collective-permute-start.3 = (bf16[1568,128]{1,0:T(8,128)(2,1)S(1)}, bf16[1568,128]{1,0:T(8,128)(2,1)S(1)}, u32[]{:S(2)}, u32[]{:S(2)}) collective-permute-start(bf16[1568,128]{1,0:T(8,128)(2,1)S(1)} %collective-permute-done.refs_4_.refs_1_), channel_id=1, source_target_pairs={{0,16},{16,0},{1,17},{17,1},{2,18},{18,2},{3,19},{19,3},{4,20},{20... | collective-permute-start | bytes 1204232 | tf_op jit(solution)/shard_map/ppermute | solution.py:215
  35.8 2.6 %collective-permute-start.10 = (bf16[1568,128]{1,0:T(8,128)(2,1)S(1)}, bf16[1568,128]{1,0:T(8,128)(2,1)S(1)}, u32[]{:S(2)}, u32[]{:S(2)}) collective-permute-start(bf16[1568,128]{1,0:T(8,128)(2,1)S(1)} %collective-permute-done.9.own), channel_id=1, source_target_pairs={{0,16},{16,0},{1,17},{17,1},{2,18},{18,2},{3,19},{19,3},{4,20},{20... | collective-permute-start | bytes 1204232 | tf_op jit(solution)/shard_map/ppermute | solution.py:215

commit v3 on v2

v3 whole, which is shorter than its diff:
```python
import functools

import jax
import jax.numpy as jnp
from jax import lax
from jax.experimental import pallas as pl
from jax.experimental.pallas import tpu as pltpu
from jax.sharding import PartitionSpec as P

VMEM_LIMIT = 24 * 1024 * 1024
ID_ROWS = 16
ROW_STEPS = 4
DECLARED_FLOPS = 100_000_000_000


def whole_vmem():
    return pl.BlockSpec(memory_space=pltpu.VMEM)


def pack_ids(ids, counts, k, slots, width):
    at_row = lax.broadcasted_iota(jnp.int32, (ID_ROWS, width), 0)
    rows = jnp.zeros((ID_ROWS, width), jnp.int32)
    for s in range(slots):
        rows = jnp.where(at_row == s, jnp.where(s < counts[0, 0, k], ids[0, k, s] + 1, 0), rows)
    return rows.astype(jnp.float32).astype(jnp.bfloat16)


def prepare_kernel(
    row_ids_in, row_counts_in, col_ids_in, col_counts_in, lower_in, inverse_in, upper_in,
    both, first, second, packed,
    row_ids, row_counts, col_ids, col_counts, lower, inverse, upper, arrived,
):
    supernodes, slots, width, _ = lower.shape
    chunk = slots * width + ID_ROWS
    pairs = (
        (row_ids_in, row_ids),
        (row_counts_in, row_counts),
        (inverse_in.at[0], inverse),
        (lower_in.at[0, 0], lower.at[0]),
        (lower_in.at[0, 1], lower.at[1]),
        (col_ids_in, col_ids),
        (col_counts_in, col_counts),
        (upper_in.at[0], upper),
    )
    copies = [pltpu.make_async_copy(src, dst, arrived.at[n]) for n, (src, dst) in enumerate(pairs)]
    for copy in copies:
        copy.start()
    for copy in copies[:3]:
        copy.wait()
    for k, half in enumerate((first, second)):
        copies[3 + k].wait()
        tiles = lower[k].reshape(slots * width, width)
        solved = jnp.dot(tiles, inverse[k], preferred_element_type=jnp.float32).astype(jnp.bfloat16)
        ids = pack_ids(row_ids, row_counts, k, slots, width)
        half[0 : slots * width, :] = solved
        half[slots * width : chunk, :] = ids
        both[k * chunk : k * chunk + slots * width, :] = solved
        both[k * chunk + slots * width : (k + 1) * chunk, :] = ids
    for copy in copies[5:]:
        copy.wait()
    slots = upper.shape[1]
    chunk = slots * width + ID_ROWS
    for k in range(supernodes):
        packed[k * chunk : k * chunk + slots * width, :] = upper[k].reshape(slots * width, width)
        packed[k * chunk + slots * width : (k + 1) * chunk, :] = pack_ids(col_ids, col_counts, k, slots, width)


def prepare(lower, row_ids, row_counts, inverse, upper, col_ids, col_counts):
    _, supernodes, slots, width, _ = lower.shape
    chunk = slots * width + ID_ROWS
    row_counts = jnp.swapaxes(row_counts, 1, 2)
    col_counts = jnp.swapaxes(col_counts, 1, 2)
    return pl.pallas_call(
        prepare_kernel,
        out_shape=(
            jax.ShapeDtypeStruct((supernodes * chunk, width), jnp.bfloat16),
            jax.ShapeDtypeStruct((chunk, width), jnp.bfloat16),
            jax.ShapeDtypeStruct((chunk, width), jnp.bfloat16),
            jax.ShapeDtypeStruct((supernodes * (upper.shape[2] * width + ID_ROWS), width), jnp.bfloat16),
        ),
        in_specs=[pl.BlockSpec(memory_space=pltpu.HBM)] * 7,
        out_specs=(whole_vmem(),) * 4,
        scratch_shapes=[
            pltpu.SMEM(row_ids.shape, jnp.int32),
            pltpu.SMEM(row_counts.shape, jnp.int32),
            pltpu.SMEM(col_ids.shape, jnp.int32),
            pltpu.SMEM(col_counts.shape, jnp.int32),
            pltpu.VMEM(lower.shape[1:], jnp.bfloat16),
            pltpu.VMEM(inverse.shape[1:], jnp.bfloat16),
            pltpu.VMEM(upper.shape[1:], jnp.bfloat16),
            pltpu.SemaphoreType.DMA((8,)),
        ],
        compiler_params=pltpu.CompilerParams(vmem_limit_bytes=VMEM_LIMIT),
        name="solve_and_pack",
    )(
        *(
            pltpu.with_memory_space_constraint(array, pltpu.HBM)
            for array in (row_ids, row_counts, col_ids, col_counts, lower, inverse, upper)
        )
    )


def spread_kernel(slots, supernodes, packed, *refs):
    out, padded = refs[-2:]
    width = packed.shape[1]
    chunk = slots * width + ID_ROWS
    padded[...] = jnp.zeros_like(padded)
    for k in range(supernodes):
        ids = packed[k * chunk + slots * width : (k + 1) * chunk, :].astype(jnp.float32).astype(jnp.int32)
        for s in range(slots):
            at = pl.multiple_of(ids[s, 0] * width, width)
            padded[k * width : (k + 1) * width, pl.ds(at, width)] = packed[
                k * chunk + s * width : k * chunk + (s + 1) * width, :
            ]
    out[...] = padded[:, width:]


def spread_uppers(packed, after, slots, columns):
    width = packed.shape[1]
    supernodes = packed.shape[0] // (slots * width + ID_ROWS)
    return pl.pallas_call(
        functools.partial(spread_kernel, slots, supernodes),
        out_shape=jax.ShapeDtypeStruct((supernodes * width, columns), jnp.bfloat16),
        in_specs=[whole_vmem()] + [pl.BlockSpec(memory_space=pl.ANY)] * len(after),
        out_specs=whole_vmem(),
        scratch_shapes=[pltpu.VMEM((supernodes * width, columns + width), jnp.bfloat16)],
        compiler_params=pltpu.CompilerParams(vmem_limit_bytes=VMEM_LIMIT),
        name="spread_uppers",
    )(packed, *after)


def ids_kernel(panel, out):
    out[...] = panel[panel.shape[0] - ID_ROWS :, :]


def ids_of(panel):
    return pl.pallas_call(
        ids_kernel,
        out_shape=jax.ShapeDtypeStruct((ID_ROWS, panel.shape[1]), panel.dtype),
        in_specs=[whole_vmem()],
        out_specs=whole_vmem(),
        compiler_params=pltpu.CompilerParams(vmem_limit_bytes=VMEM_LIMIT),
        cost_estimate=pl.CostEstimate(flops=DECLARED_FLOPS, bytes_accessed=0, transcendentals=0),
        name="ids_of_last",
    )(panel)


def place_tiles(panel, k, slots, left, at_col):
    width = panel.shape[1]
    chunk = slots * width + ID_ROWS
    start = k * chunk
    ids = panel[start + slots * width : start + chunk, :].astype(jnp.float32).astype(jnp.int32)
    for s in range(slots):
        at = pl.multiple_of(ids[s, 0] * width, width)
        left[pl.ds(at, width), at_col] = panel[start + s * width : start + (s + 1) * width, :]


def place_items(slots, tall, items, panels, uppers, left, right):
    width = panels[0][0].shape[1]
    column = lax.axis_index("col")
    layer = lax.axis_index("gz")
    left[...] = jnp.zeros_like(left)
    for side, (tiles, upper) in enumerate(zip(panels, uppers)):
        base = (layer if side == 0 else 1 - layer) * (len(items) * width)
        for n, (panel, at, k, mask) in enumerate(items):
            start = pl.multiple_of(base + n * width, width)
            rows = pl.multiple_of((column ^ mask) * tall + k * width, width)
            right[pl.ds(start, width), :] = upper[pl.ds(rows, width), :]
            place_tiles(tiles[panel], at, slots, left, pl.ds(start, width))


def sum_kernel(slots, tall, items, count, *refs):
    panels = (refs[:count], refs[count : 2 * count])
    uppers, (out, left, right) = refs[2 * count : 2 * count + 2], refs[2 * count + 2 :]
    width = panels[0][0].shape[1]
    place_items(slots, tall, items, panels, uppers, left, right)
    rows = out.shape[0] // ROW_STEPS
    for i in range(ROW_STEPS):
        out[i * rows : (i + 1) * rows, :] = jnp.dot(
            left[width + i * rows : width + (i + 1) * rows, :], right[...], preferred_element_type=jnp.float32
        )


def sum_items(items, own, other, uppers, shape, slots, supernodes):
    width = own[0].shape[1]
    depth = 2 * len(items) * width
    return pl.pallas_call(
        functools.partial(sum_kernel, slots, supernodes * width, tuple(items), len(own)),
        out_shape=jax.ShapeDtypeStruct(shape, jnp.float32),
        in_specs=[whole_vmem()] * (2 * len(own) + 2),
        out_specs=whole_vmem(),
        scratch_shapes=[
            pltpu.VMEM((shape[0] + width, depth), jnp.bfloat16),
            pltpu.VMEM((depth, shape[1]), jnp.bfloat16),
        ],
        compiler_params=pltpu.CompilerParams(vmem_limit_bytes=VMEM_LIMIT),
        name="sum_groups",
    )(*own, *other, *uppers)


def finish_kernel(slots, tall, items, count, ancestor, early, *refs):
    panels = (refs[:count], refs[count : 2 * count])
    uppers, (out, left, right, result, sent) = refs[2 * count : 2 * count + 2], refs[-5:]
    width = panels[0][0].shape[1]
    place_items(slots, tall, items, panels, uppers, left, right)
    rows = out.shape[0] // ROW_STEPS
    copies = []
    for i in range(ROW_STEPS):
        block = slice(i * rows, (i + 1) * rows)
        update = jnp.dot(
            left[width + i * rows : width + (i + 1) * rows, :], right[...], preferred_element_type=jnp.float32
        )
        result[block, :] = ancestor[block, :] - (early[block, :] + update)
        copy = pltpu.make_async_copy(result.at[block], out.at[block], sent.at[i])
        copy.start()
        copies.append(copy)
    for copy in copies:
        copy.wait()


def finish(ancestor, early, items, own, other, uppers, after, slots, supernodes):
    width = own[0].shape[1]
    depth = 2 * len(items) * width
    return pl.pallas_call(
        functools.partial(finish_kernel, slots, supernodes * width, tuple(items), len(own)),
        out_shape=jax.ShapeDtypeStruct(ancestor.shape, jnp.float32),
        in_specs=[whole_vmem()] * (2 * len(own) + 4) + [pl.BlockSpec(memory_space=pl.ANY)] * len(after),
        out_specs=pl.BlockSpec(memory_space=pltpu.HBM),
        scratch_shapes=[
            pltpu.VMEM((ancestor.shape[0] + width, depth), jnp.bfloat16),
            pltpu.VMEM((depth, ancestor.shape[1]), jnp.bfloat16),
            pltpu.VMEM(ancestor.shape, jnp.float32),
            pltpu.SemaphoreType.DMA((ROW_STEPS,)),
        ],
        compiler_params=pltpu.CompilerParams(vmem_limit_bytes=VMEM_LIMIT),
        name="last_group_and_subtract",
    )(ancestor, early, *own, *other, *uppers, *after)


def swap(array, axis, mask):
    return lax.ppermute(array, axis, [(i, i ^ mask) for i in range(4)])


def siblings(array):
    return lax.ppermute(array, "gz", [(0, 1), (1, 0)])


def on_line_of_four(
    ancestor, lower_panel, row_ids, row_counts, diag_inverse, upper_panel, col_ids, col_counts
):
    supernodes, slots = lower_panel.shape[1:3]
    both, first, second, packed = prepare(
        lower_panel, row_ids, row_counts, diag_inverse, upper_panel, col_ids, col_counts
    )
    near = swap(both, "col", 1)
    far_first = swap(first, "col", 2)
    far_second = swap(second, "col", 2)
    packed = lax.all_gather(packed, "row", axis=0, tiled=True)
    far_first, packed = lax.optimization_barrier((far_first, packed))
    last_first = swap(far_first, "col", 1)
    last_second = swap(far_second, "col", 1)
    other_both, other_first = siblings(both), siblings(far_first)
    upper = spread_uppers(
        packed,
        [near, far_second, last_first, other_both, other_first],
        upper_panel.shape[2],
        ancestor.shape[1],
    )
    panels = [both, near, far_first, far_second]
    other_near, other_second, other_upper = siblings(near), siblings(far_second), siblings(upper)
    last_second, other_near, other_second, other_upper, ids = lax.optimization_barrier(
        (last_second, other_near, other_second, other_upper, ids_of(last_second))
    )
    others = [other_both, other_near, other_first, other_second]
    last = [last_first, last_second]
    early = sum_items(
        [(0, 0, 0, 0), (0, 1, 1, 0), (1, 0, 0, 1), (1, 1, 1, 1), (2, 0, 0, 2), (3, 0, 1, 2)],
        panels,
        others,
        (upper, other_upper),
        ancestor.shape,
        slots,
        supernodes,
    )
    return finish(
        ancestor,
        early,
        [(0, 0, 0, 3), (1, 0, 1, 3)],
        last,
        [siblings(panel) for panel in last],
        (upper, other_upper),
        [ids],
        slots,
        supernodes,
    )


def spread_tiles(tiles, ids, counts, blocks, rule):
    slot_index = jnp.arange(ids.shape[1], dtype=jnp.int32)
    alive = slot_index[None, :] < counts
    target = jnp.arange(blocks, dtype=jnp.int32)
    select = ((ids[:, :, None] == target[None, None, :]) & alive[:, :, None]).astype(jnp.bfloat16)
    return jnp.einsum(rule, select, tiles, preferred_element_type=jnp.float32).astype(jnp.bfloat16)


def on_device(
    ancestor, lower_panel, row_ids, row_counts, diag_inverse, upper_panel, col_ids, col_counts
):
    width = lower_panel.shape[-1]
    rows, columns = ancestor.shape
    solved = jnp.einsum(
        "ksab,kbc->ksac", lower_panel[0], diag_inverse[0], preferred_element_type=jnp.float32
    ).astype(jnp.bfloat16)
    piece = lax.all_gather((upper_panel[0], col_ids[0], col_counts[0]), "row", axis=0, tiled=True)
    upper_dense = spread_tiles(*piece, columns // width, "kcm,kcab->kamb").reshape(-1, columns)
    piece = lax.all_gather((solved, row_ids[0], row_counts[0]), "col", axis=0, tiled=True)
    lower_dense = spread_tiles(*piece, rows // width, "krl,krab->lakb").reshape(rows, -1)
    partial_sum = jnp.dot(lower_dense, upper_dense, preferred_element_type=jnp.float32)
    return ancestor - lax.psum(partial_sum, "gz")


def solution(mesh):
    placed = (
        P("row", "col"),
        P("gz", "col", "row", None, None),
        P("gz", "col", "row"),
        P("gz", "col", "row"),
        P("gz", "col", None, None),
        P("gz", "row", "col", None, None),
        P("gz", "row", "col"),
        P("gz", "row", "col"),
    )
    sizes = dict(mesh.shape)
    small = sizes["gz"] == 2 and sizes["row"] == 4 and sizes["col"] == 4

    def run(ancestor, lower_panel, *rest):
        two = lower_panel.shape[1] == 2 * sizes["col"]
        body = on_line_of_four if small and two else on_device
        return jax.shard_map(
            body, mesh=mesh, in_specs=placed, out_specs=P("row", "col"), check_vma=False
        )(ancestor, lower_panel, *rest)

    return run
```

time: 40.5 us -> 38.5 us (0.951)
  waiting for transfers between devices: 22.6 us -> 9.06 us
  blocking collectives: 0 us -> 12.5 us
  starting transfers between devices: 11.5 us -> 10.3 us
    ppermute x6 -> x5, waiting for transfers between devices: 22.6 us -> 8.09 us  [swap(): return lax.ppermute(array, axis, [(i, i ^ mask) for i in range(4)])]
    all_gather x0 -> x1, blocking collectives: none -> 12.5 us  [on_line_of_four(): packed = lax.all_gather(packed, 'row', axis=0, tiled=True)]
    ppermute x6 -> x5, starting transfers between devices: 10.7 us -> 8.85 us  [swap(): return lax.ppermute(array, axis, [(i, i ^ mask) for i in range(4)])]
    ppermute x5 -> x7, waiting for transfers between devices: 0.01 us -> 0.97 us  [siblings(): return lax.ppermute(array, 'gz', [(0, 1), (1, 0)])]
    ppermute x5 -> x7, starting transfers between devices: 0.75 us -> 1.46 us  [siblings(): return lax.ppermute(array, 'gz', [(0, 1), (1, 0)])]
    pallas_call x3 -> x4, Pallas kernels: 4.54 us -> 4.84 us  [the longest x1 2.56 us: sum_items(): pl.pallas_call(functools.partial(sum_kernel, slots, supernodes * width, t...]
  transfers between devices with their start and end apart: 11 -> 12, of which waited for: 5 -> 4; matrix products, arithmetic and copies ran while one was open for 0% -> 0% of each run, Pallas kernels for 6% -> 8%
where the time goes in v3:
time: 38.5 us; the launch traced here: 38.3 us
  blocking collectives  12.5 us (32%)
  starting transfers between devices  10.3 us (27%)
  waiting for transfers between devices  9.06 us (24%)
  Pallas kernels  6.37 us (17%)
    all_gather x1, blocking collectives, on_line_of_four(): packed = lax.all_gather(packed, 'row', axis=0, tiled=True)  12.5 us
    ppermute x5, starting transfers between devices, swap(): return lax.ppermute(array, axis, [(i, i ^ mask) for i in range(4)])  8.85 us
    ppermute x5, waiting for transfers between devices, swap(): return lax.ppermute(array, axis, [(i, i ^ mask) for i in range(4)])  8.09 us
    pallas_call x1, Pallas kernels, sum_items(): pl.pallas_call(functools.partial(sum_kernel, slots, supernodes * width, t...  2.56 us
    pallas_call x1, Pallas kernels, finish(): pl.pallas_call(functools.partial(finish_kernel, slots, supernodes * width...  1.94 us
    pallas_call x1, Pallas kernels, prepare(): pl.pallas_call(prepare_kernel, out_shape=(jax.ShapeDtypeStruct((supernode...  1.53 us
    ppermute x7, starting transfers between devices, siblings(): return lax.ppermute(array, 'gz', [(0, 1), (1, 0)])  1.46 us
    ppermute x7, waiting for transfers between devices, siblings(): return lax.ppermute(array, 'gz', [(0, 1), (1, 0)])  0.97 us
  transfers between devices with their start and end apart: 12, of which 4 were waited for; matrix products, arithmetic and copies ran while one was open for 0% of the time, Pallas kernels for 8%

profile of v3, /device:TPU:0, one launch (start us, length us, event | category | flops | bytes accessed | tf_op | source)
XLA Modules:
  0.0 38.3 jit_solution(5678106790905129995)
XLA Ops:
  0.0 1.5 %solve_and_pack.1 = (bf16[1568,128]{1,0:T(8,128)(2,1)S(1)}, bf16[784,128]{1,0:T(8,128)(2,1)S(1)}, bf16[784,128]{1,0:T(8,128)(2,1)S(1)}, bf16[800,128]{1,0:T(8,128)(2,1)S(1)}) custom-call(s32[1,2,6]{2,1,0:T(2,128)} %row_ids_in.1, s32[1,1,2]{2,1,0:T(1,128)} %bitcast.2, s32[1,2,3]{2,1,0:T(2,128)} %col_ids_in.1, s32[1,1,2]{2,1,0:T(1,128)} %bitcast.3, ...), custom_call_target="tpu_custom_call" | custom-call | tf_op jit(solution)/shard_map/solve_and_pack/pallas_call | solution.py:73
  1.5 4.1 %collective-permute-start.1 = (bf16[784,128]{1,0:T(8,128)(2,1)S(1)}, bf16[784,128]{1,0:T(8,128)(2,1)S(1)}, u32[]{:S(2)}, u32[]{:S(2)}) collective-permute-start(bf16[784,128]{1,0:T(8,128)(2,1)S(1)} %get-tuple-element.17), channel_id=1, source_target_pairs={{0,2},{1,3},{2,0},{3,1},{4,6},{5,7},{6,4},{7,5},{8,10},{9,11},{10,... | collective-permute-start | bytes 602120 | tf_op jit(solution)/shard_map/ppermute | solution.py:241
  5.6 1.6 %collective-permute-start = (bf16[1568,128]{1,0:T(8,128)(2,1)S(1)}, bf16[1568,128]{1,0:T(8,128)(2,1)S(1)}, u32[]{:S(2)}, u32[]{:S(2)}) collective-permute-start(bf16[1568,128]{1,0:T(8,128)(2,1)S(1)} %get-tuple-element.16.refs_0_), channel_id=1, source_target_pairs={{0,1},{1,0},{2,3},{3,2},{4,5},{5,4},{6,7},{7,6},{8,9},{9,8},{10,11... | collective-permute-start | bytes 1204232 | tf_op jit(solution)/shard_map/ppermute | solution.py:241
  7.2 0.0 collective-permute-start.3
  7.2 0.3 collective-permute-start.2
  7.6 12.5 %all_gather.3.packed = bf16[3200,128]{1,0:T(8,128)(2,1)S(1)} all-gather(bf16[800,128]{1,0:T(8,128)(2,1)S(1)} %get-tuple-element.18), channel_id=1, replica_groups=mesh['gz'=2,'row'=4,'col'=4] {'row'}, dimensions={0}, use_global_device_ids=true | all-gather | bytes 1024000 | tf_op jit(solution)/shard_map/all_gather | solution.py:258
  20.1 0.0 collective-permute-done.1.refs_2_
  20.1 0.5 %collective-permute-start.7 = (bf16[784,128]{1,0:T(8,128)(2,1)S(1)}, bf16[784,128]{1,0:T(8,128)(2,1)S(1)}, u32[]{:S(2)}, u32[]{:S(2)}) collective-permute-start(bf16[784,128]{1,0:T(8,128)(2,1)S(1)} %collective-permute-done.1.refs_2_), channel_id=1, source_target_pairs={{0,1},{1,0},{2,3},{3,2},{4,5},{5,4},{6,7},{7,6},{8,9},{9,8},{10,11... | collective-permute-start | bytes 602120 | tf_op jit(solution)/shard_map/ppermute | solution.py:241
  20.6 0.0 collective-permute-start.8
  20.6 3.4 %collective-permute-done.2.refs_1_.refs_3_ = bf16[784,128]{1,0:T(8,128)(2,1)S(1)} collective-permute-done((bf16[784,128]{1,0:T(8,128)(2,1)S(1)}, bf16[784,128]{1,0:T(8,128)(2,1)S(1)}, u32[]{:S(2)}, u32[]{:S(2)}) %collective-permute-start.2) | collective-permute-done | bytes 200736 | tf_op jit(solution)/shard_map/ppermute | solution.py:241
  24.0 2.3 %collective-permute-start.4 = (bf16[784,128]{1,0:T(8,128)(2,1)S(1)}, bf16[784,128]{1,0:T(8,128)(2,1)S(1)}, u32[]{:S(2)}, u32[]{:S(2)}) collective-permute-start(bf16[784,128]{1,0:T(8,128)(2,1)S(1)} %collective-permute-done.2.refs_1_.refs_3_), channel_id=1, source_target_pairs={{0,1},{1,0},{2,3},{3,2},{4,5},{5,4},{6,7},{7,6},{8,9},{9,8},{10,11... | collective-permute-start | bytes 602120 | tf_op jit(solution)/shard_map/ppermute | solution.py:241
  26.3 3.3 %collective-permute-done.7.refs_2_.refs_0_ = bf16[784,128]{1,0:T(8,128)(2,1)S(1)} collective-permute-done((bf16[784,128]{1,0:T(8,128)(2,1)S(1)}, bf16[784,128]{1,0:T(8,128)(2,1)S(1)}, u32[]{:S(2)}, u32[]{:S(2)}) %collective-permute-start.7) | collective-permute-done | bytes 200736 | tf_op jit(solution)/shard_map/ppermute | solution.py:241
  29.6 0.0 collective-permute-start.6
  29.6 0.0 collective-permute-done.8.refs_4_.refs_6_
  29.6 0.0 collective-permute-done.refs_0_.refs_1_
  29.6 0.0 collective-permute-done.3.refs_3_.refs_4_
  29.6 0.3 spread_uppers.1.refs_8_.refs_4_
  30.0 0.6 %collective-permute-start.9 = (bf16[1024,512]{1,0:T(8,128)(2,1)S(1)}, bf16[1024,512]{1,0:T(8,128)(2,1)S(1)}, u32[]{:S(2)}, u32[]{:S(2)}) collective-permute-start(bf16[1024,512]{1,0:T(8,128)(2,1)S(1)} %spread_uppers.1.refs_8_.refs_4_), channel_id=1, source_target_pairs={{0,16},{16,0},{1,17},{17,1},{2,18},{18,2},{3,19},{19,3},{4,20},{20... | collective-permute-start | bytes 3145736 | tf_op jit(solution)/shard_map/ppermute | solution.py:245
  30.5 0.1 collective-permute-start.5
  30.6 0.4 %collective-permute-start.10 = (bf16[784,128]{1,0:T(8,128)(2,1)S(1)}, bf16[784,128]{1,0:T(8,128)(2,1)S(1)}, u32[]{:S(2)}, u32[]{:S(2)}) collective-permute-start(bf16[784,128]{1,0:T(8,128)(2,1)S(1)} %collective-permute-done.7.refs_2_.refs_0_), channel_id=1, source_target_pairs={{0,16},{16,0},{1,17},{17,1},{2,18},{18,2},{3,19},{19,3},{4,20},{20... | collective-permute-start | bytes 602120 | tf_op jit(solution)/shard_map/ppermute | solution.py:245
  31.0 1.4 %collective-permute-done.4.panel.refs_1_ = bf16[784,128]{1,0:T(8,128)(2,1)S(1)} collective-permute-done((bf16[784,128]{1,0:T(8,128)(2,1)S(1)}, bf16[784,128]{1,0:T(8,128)(2,1)S(1)}, u32[]{:S(2)}, u32[]{:S(2)}) %collective-permute-start.4) | collective-permute-done | bytes 200736 | tf_op jit(solution)/shard_map/ppermute | solution.py:241
  32.4 0.0 copy-start
  32.4 0.0 collective-permute-done.6.refs_7_
  32.4 1.0 %collective-permute-done.5.refs_5_ = bf16[1568,128]{1,0:T(8,128)(2,1)S(1)} collective-permute-done((bf16[1568,128]{1,0:T(8,128)(2,1)S(1)}, bf16[1568,128]{1,0:T(8,128)(2,1)S(1)}, u32[]{:S(2)}, u32[]{:S(2)}) %collective-permute-start.5) | collective-permute-done | bytes 401440 | tf_op jit(solution)/shard_map/ppermute | solution.py:245
  33.4 0.0 collective-permute-done.9.refs_9_.refs_5_
  33.4 0.4 collective-permute-start.11
  33.8 2.6 %sum_groups.1.early = f32[1024,512]{1,0:T(8,128)S(1)} custom-call(bf16[1568,128]{1,0:T(8,128)(2,1)S(1)} %get-tuple-element.16.refs_0_, bf16[1568,128]{1,0:T(8,128)(2,1)S(1)} %collective-permute-done.refs_0_.refs_1_, bf16[784,128]{1,0:T(8,128)(2,1)S(1)} %collective-permute-done.1.refs_2_, bf16[784,128]{1,0:T(8,128)(2,1)S(1)} %collective-permute-done.2.refs_1_.refs_3_, ...), custom_call_target="tpu_custom_call" | custom-call | tf_op jit(solution)/shard_map/sum_groups/pallas_call | solution.py:187
  36.3 0.0 collective-permute-done.10.refs_2_
  36.3 0.0 collective-permute-done.11.refs_3_
  36.4 0.0 copy-done
  36.4 1.9 %last_group_and_subtract.1 = f32[1024,512]{1,0:T(8,128)} custom-call(f32[1024,512]{1,0:T(8,128)S(1)} %copy-done, f32[1024,512]{1,0:T(8,128)S(1)} %sum_groups.1.early, bf16[784,128]{1,0:T(8,128)(2,1)S(1)} %collective-permute-done.7.refs_2_.refs_0_, bf16[784,128]{1,0:T(8,128)(2,1)S(1)} %collective-permute-done.4.panel.refs_1_, ...), custom_call_target="tpu_custom_call" | custom-call | tf_op jit(solution)/shard_map/last_group_and_subtract/pallas_call | solution.py:224
  (1 shorter events, 0.0 us)
Async XLA Ops:
  1.5 18.5 %collective-permute-start.1 = (bf16[784,128]{1,0:T(8,128)(2,1)S(1)}, bf16[784,128]{1,0:T(8,128)(2,1)S(1)}, u32[]{:S(2)}, u32[]{:S(2)}) collective-permute-start(bf16[784,128]{1,0:T(8,128)(2,1)S(1)} %get-tuple-element.17), channel_id=1, source_target_pairs={{0,2},{1,3},{2,0},{3,1},{4,6},{5,7},{6,4},{7,5},{8,10},{9,11},{10,... | collective-permute-start | bytes 602120 | tf_op jit(solution)/shard_map/ppermute | solution.py:241
  5.6 24.0 %collective-permute-start = (bf16[1568,128]{1,0:T(8,128)(2,1)S(1)}, bf16[1568,128]{1,0:T(8,128)(2,1)S(1)}, u32[]{:S(2)}, u32[]{:S(2)}) collective-permute-start(bf16[1568,128]{1,0:T(8,128)(2,1)S(1)} %get-tuple-element.16.refs_0_), channel_id=1, source_target_pairs={{0,1},{1,0},{2,3},{3,2},{4,5},{5,4},{6,7},{7,6},{8,9},{9,8},{10,11... | collective-permute-start | bytes 1204232 | tf_op jit(solution)/shard_map/ppermute | solution.py:241
  7.2 22.4 %collective-permute-start.3 = (bf16[1568,128]{1,0:T(8,128)(2,1)S(1)}, bf16[1568,128]{1,0:T(8,128)(2,1)S(1)}, u32[]{:S(2)}, u32[]{:S(2)}) collective-permute-start(bf16[1568,128]{1,0:T(8,128)(2,1)S(1)} %get-tuple-element.16.refs_0_), channel_id=1, source_target_pairs={{0,16},{16,0},{1,17},{17,1},{2,18},{18,2},{3,19},{19,3},{4,20},{20... | collective-permute-start | bytes 1204232 | tf_op jit(solution)/shard_map/ppermute | solution.py:245
  7.2 16.8 %collective-permute-start.2 = (bf16[784,128]{1,0:T(8,128)(2,1)S(1)}, bf16[784,128]{1,0:T(8,128)(2,1)S(1)}, u32[]{:S(2)}, u32[]{:S(2)}) collective-permute-start(bf16[784,128]{1,0:T(8,128)(2,1)S(1)} %get-tuple-element.20), channel_id=1, source_target_pairs={{0,2},{1,3},{2,0},{3,1},{4,6},{5,7},{6,4},{7,5},{8,10},{9,11},{10,... | collective-permute-start | bytes 602120 | tf_op jit(solution)/shard_map/ppermute | solution.py:241
  20.1 9.5 %collective-permute-start.7 = (bf16[784,128]{1,0:T(8,128)(2,1)S(1)}, bf16[784,128]{1,0:T(8,128)(2,1)S(1)}, u32[]{:S(2)}, u32[]{:S(2)}) collective-permute-start(bf16[784,128]{1,0:T(8,128)(2,1)S(1)} %collective-permute-done.1.refs_2_), channel_id=1, source_target_pairs={{0,1},{1,0},{2,3},{3,2},{4,5},{5,4},{6,7},{7,6},{8,9},{9,8},{10,11... | collective-permute-start | bytes 602120 | tf_op jit(solution)/shard_map/ppermute | solution.py:241
  20.6 9.0 %collective-permute-start.8 = (bf16[784,128]{1,0:T(8,128)(2,1)S(1)}, bf16[784,128]{1,0:T(8,128)(2,1)S(1)}, u32[]{:S(2)}, u32[]{:S(2)}) collective-permute-start(bf16[784,128]{1,0:T(8,128)(2,1)S(1)} %collective-permute-done.1.refs_2_), channel_id=1, source_target_pairs={{0,16},{16,0},{1,17},{17,1},{2,18},{18,2},{3,19},{19,3},{4,20},{20... | collective-permute-start | bytes 602120 | tf_op jit(solution)/shard_map/ppermute | solution.py:245
  24.0 8.4 %collective-permute-start.4 = (bf16[784,128]{1,0:T(8,128)(2,1)S(1)}, bf16[784,128]{1,0:T(8,128)(2,1)S(1)}, u32[]{:S(2)}, u32[]{:S(2)}) collective-permute-start(bf16[784,128]{1,0:T(8,128)(2,1)S(1)} %collective-permute-done.2.refs_1_.refs_3_), channel_id=1, source_target_pairs={{0,1},{1,0},{2,3},{3,2},{4,5},{5,4},{6,7},{7,6},{8,9},{9,8},{10,11... | collective-permute-start | bytes 602120 | tf_op jit(solution)/shard_map/ppermute | solution.py:241
  29.6 2.8 %collective-permute-start.6 = (bf16[784,128]{1,0:T(8,128)(2,1)S(1)}, bf16[784,128]{1,0:T(8,128)(2,1)S(1)}, u32[]{:S(2)}, u32[]{:S(2)}) collective-permute-start(bf16[784,128]{1,0:T(8,128)(2,1)S(1)} %collective-permute-done.2.refs_1_.refs_3_), channel_id=1, source_target_pairs={{0,16},{16,0},{1,17},{17,1},{2,18},{18,2},{3,19},{19,3},{4,20},{20... | collective-permute-start | bytes 602120 | tf_op jit(solution)/shard_map/ppermute | solution.py:245
  30.0 3.4 %collective-permute-start.9 = (bf16[1024,512]{1,0:T(8,128)(2,1)S(1)}, bf16[1024,512]{1,0:T(8,128)(2,1)S(1)}, u32[]{:S(2)}, u32[]{:S(2)}) collective-permute-start(bf16[1024,512]{1,0:T(8,128)(2,1)S(1)} %spread_uppers.1.refs_8_.refs_4_), channel_id=1, source_target_pairs={{0,16},{16,0},{1,17},{17,1},{2,18},{18,2},{3,19},{19,3},{4,20},{20... | collective-permute-start | bytes 3145736 | tf_op jit(solution)/shard_map/ppermute | solution.py:245
  30.5 2.9 %collective-permute-start.5 = (bf16[1568,128]{1,0:T(8,128)(2,1)S(1)}, bf16[1568,128]{1,0:T(8,128)(2,1)S(1)}, u32[]{:S(2)}, u32[]{:S(2)}) collective-permute-start(bf16[1568,128]{1,0:T(8,128)(2,1)S(1)} %collective-permute-done.refs_0_.refs_1_), channel_id=1, source_target_pairs={{0,16},{16,0},{1,17},{17,1},{2,18},{18,2},{3,19},{19,3},{4,20},{20... | collective-permute-start | bytes 1204232 | tf_op jit(solution)/shard_map/ppermute | solution.py:245
  30.6 5.7 %collective-permute-start.10 = (bf16[784,128]{1,0:T(8,128)(2,1)S(1)}, bf16[784,128]{1,0:T(8,128)(2,1)S(1)}, u32[]{:S(2)}, u32[]{:S(2)}) collective-permute-start(bf16[784,128]{1,0:T(8,128)(2,1)S(1)} %collective-permute-done.7.refs_2_.refs_0_), channel_id=1, source_target_pairs={{0,16},{16,0},{1,17},{17,1},{2,18},{18,2},{3,19},{19,3},{4,20},{20... | collective-permute-start | bytes 602120 | tf_op jit(solution)/shard_map/ppermute | solution.py:245
  32.4 3.9 %copy-start = (f32[1024,512]{1,0:T(8,128)S(1)}, f32[1024,512]{1,0:T(8,128)}, u32[]{:S(2)}) copy-start(f32[1024,512]{1,0:T(8,128)} %ancestor.1) | copy-start | bytes 6291460
  33.4 3.0 %collective-permute-start.11 = (bf16[784,128]{1,0:T(8,128)(2,1)S(1)}, bf16[784,128]{1,0:T(8,128)(2,1)S(1)}, u32[]{:S(2)}, u32[]{:S(2)}) collective-permute-start(bf16[784,128]{1,0:T(8,128)(2,1)S(1)} %collective-permute-done.4.panel.refs_1_), channel_id=1, source_target_pairs={{0,16},{16,0},{1,17},{17,1},{2,18},{18,2},{3,19},{19,3},{4,20},{20... | collective-permute-start | bytes 602120 | tf_op jit(solution)/shard_map/ppermute | solution.py:245

commit v4 on v3

v4 whole, which is shorter than its diff:
```python
import functools

import jax
import jax.numpy as jnp
from jax import lax
from jax.experimental import pallas as pl
from jax.experimental.pallas import tpu as pltpu
from jax.sharding import PartitionSpec as P

VMEM_LIMIT = 24 * 1024 * 1024
ID_ROWS = 16
ROW_STEPS = 4
DECLARED_FLOPS = 10_000_000_000


def whole_vmem():
    return pl.BlockSpec(memory_space=pltpu.VMEM)


def pack_ids(ids, counts, supernodes, slots, width):
    at_row = lax.broadcasted_iota(jnp.int32, (ID_ROWS, width), 0)
    rows = jnp.zeros((ID_ROWS, width), jnp.int32)
    for k in range(supernodes):
        for s in range(slots):
            value = jnp.where(s < counts[0, 0, k], ids[0, k, s] + 1, 0)
            rows = jnp.where(at_row == k * slots + s, value, rows)
    return rows.astype(jnp.float32).astype(jnp.bfloat16)


def read_ids(rows):
    return rows.astype(jnp.float32).astype(jnp.int32)


def prepare_kernel(
    row_ids_in, row_counts_in, col_ids_in, col_counts_in, lower_in, inverse_in, upper_in,
    both, first, second, packed,
    row_ids, row_counts, col_ids, col_counts, lower, inverse, upper, arrived,
):
    supernodes, slots, width, _ = lower.shape
    tall = slots * width
    cut = first.shape[0] - ID_ROWS
    pairs = (
        (row_ids_in, row_ids),
        (row_counts_in, row_counts),
        (inverse_in.at[0], inverse),
        (lower_in.at[0, 0], lower.at[0]),
        (lower_in.at[0, 1], lower.at[1]),
        (col_ids_in, col_ids),
        (col_counts_in, col_counts),
        (upper_in.at[0], upper),
    )
    copies = [pltpu.make_async_copy(src, dst, arrived.at[n]) for n, (src, dst) in enumerate(pairs)]
    for copy in copies:
        copy.start()
    for copy in copies[:3]:
        copy.wait()
    ids = pack_ids(row_ids, row_counts, supernodes, slots, width)
    first[cut:, :] = ids
    both[supernodes * tall :, :] = ids
    for k in range(supernodes):
        copies[3 + k].wait()
        solved = jnp.dot(lower[k].reshape(tall, width), inverse[k], preferred_element_type=jnp.float32)
        solved = solved.astype(jnp.bfloat16)
        start, stop = k * tall, (k + 1) * tall
        both[start:stop, :] = solved
        middle = min(max(cut, start), stop)
        if middle > start:
            first[start:middle, :] = solved[: middle - start]
        if middle < stop:
            second[middle - cut : stop - cut, :] = solved[middle - start :]
    for copy in copies[5:]:
        copy.wait()
    slots = upper.shape[1]
    tall = slots * width
    for k in range(supernodes):
        packed[k * tall : (k + 1) * tall, :] = upper[k].reshape(tall, width)
    packed[supernodes * tall :, :] = pack_ids(col_ids, col_counts, supernodes, slots, width)


def prepare(lower, row_ids, row_counts, inverse, upper, col_ids, col_counts, cut):
    _, supernodes, slots, width, _ = lower.shape
    tiles = supernodes * slots
    row_counts = jnp.swapaxes(row_counts, 1, 2)
    col_counts = jnp.swapaxes(col_counts, 1, 2)
    return pl.pallas_call(
        prepare_kernel,
        out_shape=(
            jax.ShapeDtypeStruct((tiles * width + ID_ROWS, width), jnp.bfloat16),
            jax.ShapeDtypeStruct((cut * width + ID_ROWS, width), jnp.bfloat16),
            jax.ShapeDtypeStruct(((tiles - cut) * width, width), jnp.bfloat16),
            jax.ShapeDtypeStruct((supernodes * upper.shape[2] * width + ID_ROWS, width), jnp.bfloat16),
        ),
        in_specs=[pl.BlockSpec(memory_space=pltpu.HBM)] * 7,
        out_specs=(whole_vmem(),) * 4,
        scratch_shapes=[
            pltpu.SMEM(row_ids.shape, jnp.int32),
            pltpu.SMEM(row_counts.shape, jnp.int32),
            pltpu.SMEM(col_ids.shape, jnp.int32),
            pltpu.SMEM(col_counts.shape, jnp.int32),
            pltpu.VMEM(lower.shape[1:], jnp.bfloat16),
            pltpu.VMEM(inverse.shape[1:], jnp.bfloat16),
            pltpu.VMEM(upper.shape[1:], jnp.bfloat16),
            pltpu.SemaphoreType.DMA((8,)),
        ],
        compiler_params=pltpu.CompilerParams(vmem_limit_bytes=VMEM_LIMIT),
        name="solve_and_pack",
    )(
        *(
            pltpu.with_memory_space_constraint(array, pltpu.HBM)
            for array in (row_ids, row_counts, col_ids, col_counts, lower, inverse, upper)
        )
    )


def spread_kernel(slots, supernodes, packed, *refs):
    out, padded = refs[-2:]
    width = packed.shape[1]
    piece = supernodes * slots * width + ID_ROWS
    padded[...] = jnp.zeros_like(padded)
    for group in range(packed.shape[0] // piece):
        start = group * piece
        ids = read_ids(packed[start + piece - ID_ROWS : start + piece, :])
        for k in range(supernodes):
            rows = slice((group * supernodes + k) * width, (group * supernodes + k + 1) * width)
            for s in range(slots):
                tile = k * slots + s
                at = pl.multiple_of(ids[tile, 0] * width, width)
                padded[rows, pl.ds(at, width)] = packed[start + tile * width : start + (tile + 1) * width, :]
    out[...] = padded[:, width:]


def spread_uppers(packed, after, slots, supernodes, columns):
    width = packed.shape[1]
    deep = packed.shape[0] // (supernodes * slots * width + ID_ROWS) * supernodes * width
    return pl.pallas_call(
        functools.partial(spread_kernel, slots, supernodes),
        out_shape=jax.ShapeDtypeStruct((deep, columns), jnp.bfloat16),
        in_specs=[whole_vmem()] + [pl.BlockSpec(memory_space=pl.ANY)] * len(after),
        out_specs=whole_vmem(),
        scratch_shapes=[pltpu.VMEM((deep, columns + width), jnp.bfloat16)],
        compiler_params=pltpu.CompilerParams(vmem_limit_bytes=VMEM_LIMIT),
        name="spread_uppers",
    )(packed, *after)


def touch_kernel(panel, out):
    out[...] = panel[0:ID_ROWS, :]


def touched(panel):
    return pl.pallas_call(
        touch_kernel,
        out_shape=jax.ShapeDtypeStruct((ID_ROWS, panel.shape[1]), panel.dtype),
        in_specs=[whole_vmem()],
        out_specs=whole_vmem(),
        compiler_params=pltpu.CompilerParams(vmem_limit_bytes=VMEM_LIMIT),
        cost_estimate=pl.CostEstimate(flops=DECLARED_FLOPS, bytes_accessed=0, transcendentals=0),
        name="touch_chunk",
    )(panel)


def place_group(parts, slots, supernodes, left, base):
    width = parts[0].shape[1]
    ids = read_ids(parts[0][parts[0].shape[0] - ID_ROWS :, :])
    cut = (parts[0].shape[0] - ID_ROWS) // width
    for k in range(supernodes):
        columns = pl.ds(pl.multiple_of(base + k * width, width), width)
        for s in range(slots):
            tile = k * slots + s
            part, row = (parts[0], tile) if tile < cut else (parts[1], tile - cut)
            at = pl.multiple_of(ids[tile, 0] * width, width)
            left[pl.ds(at, width), columns] = part[row * width : (row + 1) * width, :]


def place_groups(plan, groups, panels, uppers, left, right):
    slots, supernodes = plan
    width = panels[0][0].shape[1]
    tall = supernodes * width
    column = lax.axis_index("col")
    layer = lax.axis_index("gz")
    left[...] = jnp.zeros_like(left)
    for side, (tiles, upper) in enumerate(zip(panels, uppers)):
        base = (layer if side == 0 else 1 - layer) * (len(groups) * tall)
        for n, (members, mask) in enumerate(groups):
            start = pl.multiple_of(base + n * tall, tall)
            right[pl.ds(start, tall), :] = upper[pl.ds(pl.multiple_of((column ^ mask) * tall, tall), tall), :]
            place_group([tiles[member] for member in members], slots, supernodes, left, start)


def sum_kernel(plan, groups, count, *refs):
    panels = (refs[:count], refs[count : 2 * count])
    uppers, (out, left, right) = refs[2 * count : 2 * count + 2], refs[2 * count + 2 :]
    width = panels[0][0].shape[1]
    place_groups(plan, groups, panels, uppers, left, right)
    rows = out.shape[0] // ROW_STEPS
    for i in range(ROW_STEPS):
        out[i * rows : (i + 1) * rows, :] = jnp.dot(
            left[width + i * rows : width + (i + 1) * rows, :], right[...], preferred_element_type=jnp.float32
        )


def sum_groups(plan, groups, own, other, uppers, shape):
    width = own[0].shape[1]
    depth = 2 * len(groups) * plan[1] * width
    return pl.pallas_call(
        functools.partial(sum_kernel, plan, groups, len(own)),
        out_shape=jax.ShapeDtypeStruct(shape, jnp.float32),
        in_specs=[whole_vmem()] * (2 * len(own) + 2),
        out_specs=whole_vmem(),
        scratch_shapes=[
            pltpu.VMEM((shape[0] + width, depth), jnp.bfloat16),
            pltpu.VMEM((depth, shape[1]), jnp.bfloat16),
        ],
        compiler_params=pltpu.CompilerParams(vmem_limit_bytes=VMEM_LIMIT),
        name="sum_groups",
    )(*own, *other, *uppers)


def finish_kernel(plan, groups, count, ancestor, early, *refs):
    panels = (refs[:count], refs[count : 2 * count])
    uppers, (out, left, right, result, sent) = refs[2 * count : 2 * count + 2], refs[-5:]
    width = panels[0][0].shape[1]
    place_groups(plan, groups, panels, uppers, left, right)
    rows = out.shape[0] // ROW_STEPS
    copies = []
    for i in range(ROW_STEPS):
        block = slice(i * rows, (i + 1) * rows)
        update = jnp.dot(
            left[width + i * rows : width + (i + 1) * rows, :], right[...], preferred_element_type=jnp.float32
        )
        result[block, :] = ancestor[block, :] - (early[block, :] + update)
        copy = pltpu.make_async_copy(result.at[block], out.at[block], sent.at[i])
        copy.start()
        copies.append(copy)
    for copy in copies:
        copy.wait()


def finish(plan, ancestor, early, groups, own, other, uppers, after):
    width = own[0].shape[1]
    depth = 2 * len(groups) * plan[1] * width
    return pl.pallas_call(
        functools.partial(finish_kernel, plan, groups, len(own)),
        out_shape=jax.ShapeDtypeStruct(ancestor.shape, jnp.float32),
        in_specs=[whole_vmem()] * (2 * len(own) + 4) + [pl.BlockSpec(memory_space=pl.ANY)] * len(after),
        out_specs=pl.BlockSpec(memory_space=pltpu.HBM),
        scratch_shapes=[
            pltpu.VMEM((ancestor.shape[0] + width, depth), jnp.bfloat16),
            pltpu.VMEM((depth, ancestor.shape[1]), jnp.bfloat16),
            pltpu.VMEM(ancestor.shape, jnp.float32),
            pltpu.SemaphoreType.DMA((ROW_STEPS,)),
        ],
        compiler_params=pltpu.CompilerParams(vmem_limit_bytes=VMEM_LIMIT),
        name="last_group_and_subtract",
    )(ancestor, early, *own, *other, *uppers, *after)


def swap(array, axis, mask):
    return lax.ppermute(array, axis, [(i, i ^ mask) for i in range(4)])


def siblings(array):
    return lax.ppermute(array, "gz", [(0, 1), (1, 0)])


def on_line_of_four(
    ancestor, lower_panel, row_ids, row_counts, diag_inverse, upper_panel, col_ids, col_counts
):
    supernodes, slots = lower_panel.shape[1:3]
    plan = (slots, supernodes)
    both, first, second, packed = prepare(
        lower_panel,
        row_ids,
        row_counts,
        diag_inverse,
        upper_panel,
        col_ids,
        col_counts,
        2 * supernodes * slots // 3,
    )
    near = swap(both, "col", 1)
    far_first = swap(first, "col", 2)
    far_second = swap(second, "col", 2)
    packed = lax.all_gather(packed, "row", axis=0, tiled=True)
    far_first, packed = lax.optimization_barrier((far_first, packed))
    last_first = swap(far_first, "col", 1)
    far_second, far_mark = lax.optimization_barrier((far_second, touched(far_second)))
    last_second = swap(far_second, "col", 1)
    other_both, other_first = siblings(both), siblings(far_first)
    upper = spread_uppers(
        packed,
        [near, far_second, other_both, other_first],
        upper_panel.shape[2],
        supernodes,
        ancestor.shape[1],
    )
    uppers = (upper, siblings(upper))
    last_first, first_mark = lax.optimization_barrier((last_first, touched(last_first)))
    last_second, second_mark = lax.optimization_barrier((last_second, touched(last_second)))
    early = sum_groups(
        plan,
        (((0,), 0), ((1,), 1), ((2, 3), 2)),
        [both, near, far_first, far_second],
        [other_both, siblings(near), other_first, siblings(far_second)],
        uppers,
        ancestor.shape,
    )
    return finish(
        plan,
        ancestor,
        early,
        (((0, 1), 3),),
        [last_first, last_second],
        [siblings(last_first), siblings(last_second)],
        uppers,
        [far_mark, first_mark, second_mark],
    )


def spread_tiles(tiles, ids, counts, blocks, rule):
    slot_index = jnp.arange(ids.shape[1], dtype=jnp.int32)
    alive = slot_index[None, :] < counts
    target = jnp.arange(blocks, dtype=jnp.int32)
    select = ((ids[:, :, None] == target[None, None, :]) & alive[:, :, None]).astype(jnp.bfloat16)
    return jnp.einsum(rule, select, tiles, preferred_element_type=jnp.float32).astype(jnp.bfloat16)


def on_device(
    ancestor, lower_panel, row_ids, row_counts, diag_inverse, upper_panel, col_ids, col_counts
):
    width = lower_panel.shape[-1]
    rows, columns = ancestor.shape
    solved = jnp.einsum(
        "ksab,kbc->ksac", lower_panel[0], diag_inverse[0], preferred_element_type=jnp.float32
    ).astype(jnp.bfloat16)
    piece = lax.all_gather((upper_panel[0], col_ids[0], col_counts[0]), "row", axis=0, tiled=True)
    upper_dense = spread_tiles(*piece, columns // width, "kcm,kcab->kamb").reshape(-1, columns)
    piece = lax.all_gather((solved, row_ids[0], row_counts[0]), "col", axis=0, tiled=True)
    lower_dense = spread_tiles(*piece, rows // width, "krl,krab->lakb").reshape(rows, -1)
    partial_sum = jnp.dot(lower_dense, upper_dense, preferred_element_type=jnp.float32)
    return ancestor - lax.psum(partial_sum, "gz")


def solution(mesh):
    placed = (
        P("row", "col"),
        P("gz", "col", "row", None, None),
        P("gz", "col", "row"),
        P("gz", "col", "row"),
        P("gz", "col", None, None),
        P("gz", "row", "col", None, None),
        P("gz", "row", "col"),
        P("gz", "row", "col"),
    )
    sizes = dict(mesh.shape)
    small = sizes["gz"] == 2 and sizes["row"] == 4 and sizes["col"] == 4

    def run(ancestor, lower_panel, *rest):
        two = lower_panel.shape[1] == 2 * sizes["col"]
        body = on_line_of_four if small and two else on_device
        return jax.shard_map(
            body, mesh=mesh, in_specs=placed, out_specs=P("row", "col"), check_vma=False
        )(ancestor, lower_panel, *rest)

    return run
```

time: 38.5 us -> 37 us (0.961)
  starting transfers between devices: 10.3 us -> 8.16 us
  waiting for transfers between devices: 9.06 us -> 9.63 us
    ppermute x5, waiting for transfers between devices: 8.09 us -> 9.61 us  [swap(): return lax.ppermute(array, axis, [(i, i ^ mask) for i in range(4)])]
    ppermute x5, starting transfers between devices: 8.85 us -> 7.57 us  [swap(): return lax.ppermute(array, axis, [(i, i ^ mask) for i in range(4)])]
    ppermute x7, waiting for transfers between devices: 0.97 us -> 0.02 us  [siblings(): return lax.ppermute(array, 'gz', [(0, 1), (1, 0)])]
    ppermute x7, starting transfers between devices: 1.46 us -> 0.59 us  [siblings(): return lax.ppermute(array, 'gz', [(0, 1), (1, 0)])]
    pallas_call x4 -> x6, Pallas kernels: 6.04 us -> 6.04 us  [the longest x1 2.57 us: sum_groups(): pl.pallas_call(functools.partial(sum_kernel, plan, groups, len(own)), out...]
where the time goes in v4:
time: 37 us; the launch traced here: 36.7 us
  blocking collectives  12.5 us (34%)
  waiting for transfers between devices  9.63 us (26%)
  starting transfers between devices  8.16 us (22%)
  Pallas kernels  6.38 us (17%)
    all_gather x1, blocking collectives, on_line_of_four(): packed = lax.all_gather(packed, 'row', axis=0, tiled=True)  12.5 us
    ppermute x5, waiting for transfers between devices, swap(): return lax.ppermute(array, axis, [(i, i ^ mask) for i in range(4)])  9.61 us
    ppermute x5, starting transfers between devices, swap(): return lax.ppermute(array, axis, [(i, i ^ mask) for i in range(4)])  7.57 us
    pallas_call x1, Pallas kernels, sum_groups(): pl.pallas_call(functools.partial(sum_kernel, plan, groups, len(own)), out...  2.57 us
    pallas_call x1, Pallas kernels, finish(): pl.pallas_call(functools.partial(finish_kernel, plan, groups, len(own)),...  1.93 us
    pallas_call x1, Pallas kernels, prepare(): pl.pallas_call(prepare_kernel, out_shape=(jax.ShapeDtypeStruct((tiles * w...  1.53 us
  transfers between devices with their start and end apart: 12, of which 4 were waited for; matrix products, arithmetic and copies ran while one was open for 0% of the time, Pallas kernels for 8%

profile of v4, /device:TPU:0, one launch (start us, length us, event | category | flops | bytes accessed | tf_op | source)
XLA Modules:
  0.0 36.7 jit_solution(4003721918210746045)
XLA Ops:
  0.0 1.5 %solve_and_pack.1 = (bf16[1552,128]{1,0:T(8,128)(2,1)S(1)}, bf16[1040,128]{1,0:T(8,128)(2,1)S(1)}, bf16[512,128]{1,0:T(8,128)(2,1)S(1)}, bf16[784,128]{1,0:T(8,128)(2,1)S(1)}) custom-call(s32[1,2,6]{2,1,0:T(2,128)} %row_ids_in.1, s32[1,1,2]{2,1,0:T(1,128)} %bitcast.2, s32[1,2,3]{2,1,0:T(2,128)} %col_ids_in.1, s32[1,1,2]{2,1,0:T(1,128)} %bitcast.3, ...), custom_call_target="tpu_custom_call" | custom-call | tf_op jit(solution)/shard_map/solve_and_pack/pallas_call | solution.py:85
  1.5 4.1 %collective-permute-start.1 = (bf16[1040,128]{1,0:T(8,128)(2,1)S(1)}, bf16[1040,128]{1,0:T(8,128)(2,1)S(1)}, u32[]{:S(2)}, u32[]{:S(2)}) collective-permute-start(bf16[1040,128]{1,0:T(8,128)(2,1)S(1)} %get-tuple-element.18), channel_id=1, source_target_pairs={{0,2},{1,3},{2,0},{3,1},{4,6},{5,7},{6,4},{7,5},{8,10},{9,11},{10,... | collective-permute-start | bytes 798728 | tf_op jit(solution)/shard_map/ppermute | solution.py:259
  5.6 1.6 %collective-permute-start = (bf16[1552,128]{1,0:T(8,128)(2,1)S(1)}, bf16[1552,128]{1,0:T(8,128)(2,1)S(1)}, u32[]{:S(2)}, u32[]{:S(2)}) collective-permute-start(bf16[1552,128]{1,0:T(8,128)(2,1)S(1)} %get-tuple-element.17.refs_0_), channel_id=1, source_target_pairs={{0,1},{1,0},{2,3},{3,2},{4,5},{5,4},{6,7},{7,6},{8,9},{9,8},{10,11... | collective-permute-start | bytes 1191944 | tf_op jit(solution)/shard_map/ppermute | solution.py:259
  7.2 0.0 collective-permute-start.3
  7.2 0.3 collective-permute-start.2
  7.6 12.5 %all_gather.3.packed = bf16[3136,128]{1,0:T(8,128)(2,1)S(1)} all-gather(bf16[784,128]{1,0:T(8,128)(2,1)S(1)} %get-tuple-element.19), channel_id=1, replica_groups=mesh['gz'=2,'row'=4,'col'=4] {'row'}, dimensions={0}, use_global_device_ids=true | all-gather | bytes 1003520 | tf_op jit(solution)/shard_map/all_gather | solution.py:284
  20.1 0.0 collective-permute-done.1.refs_2_
  20.1 0.0 collective-permute-start.5
  20.1 0.5 %collective-permute-start.8 = (bf16[1040,128]{1,0:T(8,128)(2,1)S(1)}, bf16[1040,128]{1,0:T(8,128)(2,1)S(1)}, u32[]{:S(2)}, u32[]{:S(2)}) collective-permute-start(bf16[1040,128]{1,0:T(8,128)(2,1)S(1)} %collective-permute-done.1.refs_2_), channel_id=1, source_target_pairs={{0,1},{1,0},{2,3},{3,2},{4,5},{5,4},{6,7},{7,6},{8,9},{9,8},{10,11... | collective-permute-start | bytes 798728 | tf_op jit(solution)/shard_map/ppermute | solution.py:259
  20.6 3.2 %collective-permute-done.2.panel.refs_1_.refs_3_ = bf16[512,128]{1,0:T(8,128)(2,1)S(1)} collective-permute-done((bf16[512,128]{1,0:T(8,128)(2,1)S(1)}, bf16[512,128]{1,0:T(8,128)(2,1)S(1)}, u32[]{:S(2)}, u32[]{:S(2)}) %collective-permute-start.2) | collective-permute-done | bytes 131104 | tf_op jit(solution)/shard_map/ppermute | solution.py:259
  23.8 0.0 collective-permute-start.6
  23.8 0.3 collective-permute-done.refs_0_.refs_1_
  24.1 1.0 %collective-permute-start.9 = (bf16[512,128]{1,0:T(8,128)(2,1)S(1)}, bf16[512,128]{1,0:T(8,128)(2,1)S(1)}, u32[]{:S(2)}, u32[]{:S(2)}) collective-permute-start(bf16[512,128]{1,0:T(8,128)(2,1)S(1)} %collective-permute-done.2.panel.refs_1_.refs_3_), channel_id=1, source_target_pairs={{0,1},{1,0},{2,3},{3,2},{4,5},{5,4},{6,7},{7,6},{8,9},{9,8},{10,11... | collective-permute-start | bytes 393224 | tf_op jit(solution)/shard_map/ppermute | solution.py:259
  25.1 0.0 collective-permute-done.3.refs_2_.refs_4_
  25.1 0.2 collective-permute-start.4
  25.3 0.0 collective-permute-done.5.refs_3_.refs_6_
  25.3 0.3 spread_uppers.1.refs_8_.refs_4_
  25.6 0.4 %collective-permute-start.7 = (bf16[1024,512]{1,0:T(8,128)(2,1)S(1)}, bf16[1024,512]{1,0:T(8,128)(2,1)S(1)}, u32[]{:S(2)}, u32[]{:S(2)}) collective-permute-start(bf16[1024,512]{1,0:T(8,128)(2,1)S(1)} %spread_uppers.1.refs_8_.refs_4_), channel_id=1, source_target_pairs={{0,16},{16,0},{1,17},{17,1},{2,18},{18,2},{3,19},{19,3},{4,20},{20... | collective-permute-start | bytes 3145736 | tf_op jit(solution)/shard_map/ppermute | solution.py:263
  26.0 3.7 %collective-permute-done.8.panel.refs_0_ = bf16[1040,128]{1,0:T(8,128)(2,1)S(1)} collective-permute-done((bf16[1040,128]{1,0:T(8,128)(2,1)S(1)}, bf16[1040,128]{1,0:T(8,128)(2,1)S(1)}, u32[]{:S(2)}, u32[]{:S(2)}) %collective-permute-start.8) | collective-permute-done | bytes 266272 | tf_op jit(solution)/shard_map/ppermute | solution.py:259
  29.8 0.0 collective-permute-start.10
  29.8 2.4 %collective-permute-done.9.panel.refs_1_ = bf16[512,128]{1,0:T(8,128)(2,1)S(1)} collective-permute-done((bf16[512,128]{1,0:T(8,128)(2,1)S(1)}, bf16[512,128]{1,0:T(8,128)(2,1)S(1)}, u32[]{:S(2)}, u32[]{:S(2)}) %collective-permute-start.9) | collective-permute-done | bytes 131104 | tf_op jit(solution)/shard_map/ppermute | solution.py:259
  32.2 0.0 copy-start
  32.2 0.0 collective-permute-start.11
  32.2 0.0 collective-permute-done.6.refs_7_
  32.2 0.0 collective-permute-done.4.refs_5_
  32.2 0.0 collective-permute-done.7.refs_9_.refs_5_
  32.2 2.6 %sum_groups.1.early = f32[1024,512]{1,0:T(8,128)S(1)} custom-call(bf16[1552,128]{1,0:T(8,128)(2,1)S(1)} %get-tuple-element.17.refs_0_, bf16[1552,128]{1,0:T(8,128)(2,1)S(1)} %collective-permute-done.refs_0_.refs_1_, bf16[1040,128]{1,0:T(8,128)(2,1)S(1)} %collective-permute-done.1.refs_2_, bf16[512,128]{1,0:T(8,128)(2,1)S(1)} %collective-permute-done.2.panel.refs_1_.refs_3_, ...), custom_call_target="tpu_custom_call" | custom-call | tf_op jit(solution)/shard_map/sum_groups/pallas_call | solution.py:205
  34.8 0.0 collective-permute-done.11.refs_3_
  34.8 0.0 collective-permute-done.10.refs_2_
  34.8 0.0 copy-done
  34.8 1.9 %last_group_and_subtract.1 = f32[1024,512]{1,0:T(8,128)} custom-call(f32[1024,512]{1,0:T(8,128)S(1)} %copy-done, f32[1024,512]{1,0:T(8,128)S(1)} %sum_groups.1.early, bf16[1040,128]{1,0:T(8,128)(2,1)S(1)} %collective-permute-done.8.panel.refs_0_, bf16[512,128]{1,0:T(8,128)(2,1)S(1)} %collective-permute-done.9.panel.refs_1_, ...), custom_call_target="tpu_custom_call" | custom-call | tf_op jit(solution)/shard_map/last_group_and_subtract/pallas_call | solution.py:242
  (3 shorter events, 0.0 us)
Async XLA Ops:
  1.5 18.5 %collective-permute-start.1 = (bf16[1040,128]{1,0:T(8,128)(2,1)S(1)}, bf16[1040,128]{1,0:T(8,128)(2,1)S(1)}, u32[]{:S(2)}, u32[]{:S(2)}) collective-permute-start(bf16[1040,128]{1,0:T(8,128)(2,1)S(1)} %get-tuple-element.18), channel_id=1, source_target_pairs={{0,2},{1,3},{2,0},{3,1},{4,6},{5,7},{6,4},{7,5},{8,10},{9,11},{10,... | collective-permute-start | bytes 798728 | tf_op jit(solution)/shard_map/ppermute | solution.py:259
  5.6 18.4 %collective-permute-start = (bf16[1552,128]{1,0:T(8,128)(2,1)S(1)}, bf16[1552,128]{1,0:T(8,128)(2,1)S(1)}, u32[]{:S(2)}, u32[]{:S(2)}) collective-permute-start(bf16[1552,128]{1,0:T(8,128)(2,1)S(1)} %get-tuple-element.17.refs_0_), channel_id=1, source_target_pairs={{0,1},{1,0},{2,3},{3,2},{4,5},{5,4},{6,7},{7,6},{8,9},{9,8},{10,11... | collective-permute-start | bytes 1191944 | tf_op jit(solution)/shard_map/ppermute | solution.py:259
  7.2 17.9 %collective-permute-start.3 = (bf16[1552,128]{1,0:T(8,128)(2,1)S(1)}, bf16[1552,128]{1,0:T(8,128)(2,1)S(1)}, u32[]{:S(2)}, u32[]{:S(2)}) collective-permute-start(bf16[1552,128]{1,0:T(8,128)(2,1)S(1)} %get-tuple-element.17.refs_0_), channel_id=1, source_target_pairs={{0,16},{16,0},{1,17},{17,1},{2,18},{18,2},{3,19},{19,3},{4,20},{20... | collective-permute-start | bytes 1191944 | tf_op jit(solution)/shard_map/ppermute | solution.py:263
  7.2 16.6 %collective-permute-start.2 = (bf16[512,128]{1,0:T(8,128)(2,1)S(1)}, bf16[512,128]{1,0:T(8,128)(2,1)S(1)}, u32[]{:S(2)}, u32[]{:S(2)}) collective-permute-start(bf16[512,128]{1,0:T(8,128)(2,1)S(1)} %get-tuple-element.21), channel_id=1, source_target_pairs={{0,2},{1,3},{2,0},{3,1},{4,6},{5,7},{6,4},{7,5},{8,10},{9,11},{10,... | collective-permute-start | bytes 393224 | tf_op jit(solution)/shard_map/ppermute | solution.py:259
  20.1 5.2 %collective-permute-start.5 = (bf16[1040,128]{1,0:T(8,128)(2,1)S(1)}, bf16[1040,128]{1,0:T(8,128)(2,1)S(1)}, u32[]{:S(2)}, u32[]{:S(2)}) collective-permute-start(bf16[1040,128]{1,0:T(8,128)(2,1)S(1)} %collective-permute-done.1.refs_2_), channel_id=1, source_target_pairs={{0,16},{16,0},{1,17},{17,1},{2,18},{18,2},{3,19},{19,3},{4,20},{20... | collective-permute-start | bytes 798728 | tf_op jit(solution)/shard_map/ppermute | solution.py:263
  20.1 9.7 %collective-permute-start.8 = (bf16[1040,128]{1,0:T(8,128)(2,1)S(1)}, bf16[1040,128]{1,0:T(8,128)(2,1)S(1)}, u32[]{:S(2)}, u32[]{:S(2)}) collective-permute-start(bf16[1040,128]{1,0:T(8,128)(2,1)S(1)} %collective-permute-done.1.refs_2_), channel_id=1, source_target_pairs={{0,1},{1,0},{2,3},{3,2},{4,5},{5,4},{6,7},{7,6},{8,9},{9,8},{10,11... | collective-permute-start | bytes 798728 | tf_op jit(solution)/shard_map/ppermute | solution.py:259
  23.8 8.4 %collective-permute-start.6 = (bf16[512,128]{1,0:T(8,128)(2,1)S(1)}, bf16[512,128]{1,0:T(8,128)(2,1)S(1)}, u32[]{:S(2)}, u32[]{:S(2)}) collective-permute-start(bf16[512,128]{1,0:T(8,128)(2,1)S(1)} %collective-permute-done.2.panel.refs_1_.refs_3_), channel_id=1, source_target_pairs={{0,16},{16,0},{1,17},{17,1},{2,18},{18,2},{3,19},{19,3},{4,20},{20... | collective-permute-start | bytes 393224 | tf_op jit(solution)/shard_map/ppermute | solution.py:263
  24.1 8.1 %collective-permute-start.9 = (bf16[512,128]{1,0:T(8,128)(2,1)S(1)}, bf16[512,128]{1,0:T(8,128)(2,1)S(1)}, u32[]{:S(2)}, u32[]{:S(2)}) collective-permute-start(bf16[512,128]{1,0:T(8,128)(2,1)S(1)} %collective-permute-done.2.panel.refs_1_.refs_3_), channel_id=1, source_target_pairs={{0,1},{1,0},{2,3},{3,2},{4,5},{5,4},{6,7},{7,6},{8,9},{9,8},{10,11... | collective-permute-start | bytes 393224 | tf_op jit(solution)/shard_map/ppermute | solution.py:259
  25.1 7.1 %collective-permute-start.4 = (bf16[1552,128]{1,0:T(8,128)(2,1)S(1)}, bf16[1552,128]{1,0:T(8,128)(2,1)S(1)}, u32[]{:S(2)}, u32[]{:S(2)}) collective-permute-start(bf16[1552,128]{1,0:T(8,128)(2,1)S(1)} %collective-permute-done.refs_0_.refs_1_), channel_id=1, source_target_pairs={{0,16},{16,0},{1,17},{17,1},{2,18},{18,2},{3,19},{19,3},{4,20},{20... | collective-permute-start | bytes 1191944 | tf_op jit(solution)/shard_map/ppermute | solution.py:263
  25.6 6.6 %collective-permute-start.7 = (bf16[1024,512]{1,0:T(8,128)(2,1)S(1)}, bf16[1024,512]{1,0:T(8,128)(2,1)S(1)}, u32[]{:S(2)}, u32[]{:S(2)}) collective-permute-start(bf16[1024,512]{1,0:T(8,128)(2,1)S(1)} %spread_uppers.1.refs_8_.refs_4_), channel_id=1, source_target_pairs={{0,16},{16,0},{1,17},{17,1},{2,18},{18,2},{3,19},{19,3},{4,20},{20... | collective-permute-start | bytes 3145736 | tf_op jit(solution)/shard_map/ppermute | solution.py:263
  29.8 5.0 %collective-permute-start.10 = (bf16[1040,128]{1,0:T(8,128)(2,1)S(1)}, bf16[1040,128]{1,0:T(8,128)(2,1)S(1)}, u32[]{:S(2)}, u32[]{:S(2)}) collective-permute-start(bf16[1040,128]{1,0:T(8,128)(2,1)S(1)} %collective-permute-done.8.panel.refs_0_), channel_id=1, source_target_pairs={{0,16},{16,0},{1,17},{17,1},{2,18},{18,2},{3,19},{19,3},{4,20},{20... | collective-permute-start | bytes 798728 | tf_op jit(solution)/shard_map/ppermute | solution.py:263
  32.2 2.6 %copy-start = (f32[1024,512]{1,0:T(8,128)S(1)}, f32[1024,512]{1,0:T(8,128)}, u32[]{:S(2)}) copy-start(f32[1024,512]{1,0:T(8,128)} %ancestor.1) | copy-start | bytes 6291460
  32.2 2.6 %collective-permute-start.11 = (bf16[512,128]{1,0:T(8,128)(2,1)S(1)}, bf16[512,128]{1,0:T(8,128)(2,1)S(1)}, u32[]{:S(2)}, u32[]{:S(2)}) collective-permute-start(bf16[512,128]{1,0:T(8,128)(2,1)S(1)} %collective-permute-done.9.panel.refs_1_), channel_id=1, source_target_pairs={{0,16},{16,0},{1,17},{17,1},{2,18},{18,2},{3,19},{19,3},{4,20},{20... | collective-permute-start | bytes 393224 | tf_op jit(solution)/shard_map/ppermute | solution.py:263

commit v5 on v4

--- a/solution.py
+++ b/solution.py
@@ -11,6 +11,7 @@
 ID_ROWS = 16
 ROW_STEPS = 4
 DECLARED_FLOPS = 10_000_000_000
+SUM_FLOPS = 2_000_000_000
 
 
 def whole_vmem():
@@ -143,33 +144,31 @@
     )(packed, *after)
 
 
-def touch_kernel(panel, out):
+def touch_kernel(panel, *refs):
+    out = refs[-1]
     out[...] = panel[0:ID_ROWS, :]
 
 
-def touched(panel):
+def touched(panel, after=()):
     return pl.pallas_call(
         touch_kernel,
         out_shape=jax.ShapeDtypeStruct((ID_ROWS, panel.shape[1]), panel.dtype),
-        in_specs=[whole_vmem()],
+        in_specs=[whole_vmem()] + [pl.BlockSpec(memory_space=pl.ANY)] * len(after),
         out_specs=whole_vmem(),
         compiler_params=pltpu.CompilerParams(vmem_limit_bytes=VMEM_LIMIT),
         cost_estimate=pl.CostEstimate(flops=DECLARED_FLOPS, bytes_accessed=0, transcendentals=0),
         name="touch_chunk",
-    )(panel)
-
-
-def place_group(parts, slots, supernodes, left, base):
+    )(panel, *after)
+
+
+def place_group(parts, ids, first, slots, supernodes, left, base):
     width = parts[0].shape[1]
-    ids = read_ids(parts[0][parts[0].shape[0] - ID_ROWS :, :])
-    cut = (parts[0].shape[0] - ID_ROWS) // width
-    for k in range(supernodes):
-        columns = pl.ds(pl.multiple_of(base + k * width, width), width)
-        for s in range(slots):
-            tile = k * slots + s
-            part, row = (parts[0], tile) if tile < cut else (parts[1], tile - cut)
-            at = pl.multiple_of(ids[tile, 0] * width, width)
-            left[pl.ds(at, width), columns] = part[row * width : (row + 1) * width, :]
+    tiles = [(part, row) for part in parts for row in range(part.shape[0] // width)]
+    ids = read_ids(ids[ids.shape[0] - ID_ROWS :, :])
+    for tile, (part, row) in enumerate(tiles, first):
+        at = pl.multiple_of(ids[tile, 0] * width, width)
+        columns = pl.ds(pl.multiple_of(base + tile // slots * width, width), width)
+        left[pl.ds(at, width), columns] = part[row * width : (row + 1) * width, :]
 
 
 def place_groups(plan, groups, panels, uppers, left, right):
@@ -181,54 +180,61 @@
     left[...] = jnp.zeros_like(left)
     for side, (tiles, upper) in enumerate(zip(panels, uppers)):
         base = (layer if side == 0 else 1 - layer) * (len(groups) * tall)
-        for n, (members, mask) in enumerate(groups):
+        for n, (members, ids, first, mask) in enumerate(groups):
             start = pl.multiple_of(base + n * tall, tall)
             right[pl.ds(start, tall), :] = upper[pl.ds(pl.multiple_of((column ^ mask) * tall, tall), tall), :]
-            place_group([tiles[member] for member in members], slots, supernodes, left, start)
-
-
-def sum_kernel(plan, groups, count, *refs):
+            place_group([tiles[member] for member in members], tiles[ids], first, slots, supernodes, left, start)
+
+
+def blocks_of(rows):
+    size = rows // ROW_STEPS
+    return [slice(i * size, (i + 1) * size) for i in range(ROW_STEPS)]
+
+
+def product(left, right, block):
+    width = left.shape[0] % (block.stop - block.start)
+    return jnp.dot(
+        left[width + block.start : width + block.stop, :], right[...], preferred_element_type=jnp.float32
+    )
+
+
+def sum_kernel(plan, groups, count, bases, *refs):
     panels = (refs[:count], refs[count : 2 * count])
-    uppers, (out, left, right) = refs[2 * count : 2 * count + 2], refs[2 * count + 2 :]
-    width = panels[0][0].shape[1]
+    uppers, base_refs = refs[2 * count : 2 * count + 2], refs[2 * count + 2 : 2 * count + 2 + bases]
+    out, left, right = refs[-3:]
     place_groups(plan, groups, panels, uppers, left, right)
-    rows = out.shape[0] // ROW_STEPS
-    for i in range(ROW_STEPS):
-        out[i * rows : (i + 1) * rows, :] = jnp.dot(
-            left[width + i * rows : width + (i + 1) * rows, :], right[...], preferred_element_type=jnp.float32
-        )
-
-
-def sum_groups(plan, groups, own, other, uppers, shape):
+    for block in blocks_of(out.shape[0]):
+        update = product(left, right, block)
+        if bases:
+            update = base_refs[0][block, :] + update
+        out[block, :] = update
+
+
+def sum_groups(plan, groups, own, other, uppers, shape, bases=()):
     width = own[0].shape[1]
     depth = 2 * len(groups) * plan[1] * width
     return pl.pallas_call(
-        functools.partial(sum_kernel, plan, groups, len(own)),
+        functools.partial(sum_kernel, plan, groups, len(own), len(bases)),
         out_shape=jax.ShapeDtypeStruct(shape, jnp.float32),
-        in_specs=[whole_vmem()] * (2 * len(own) + 2),
+        in_specs=[whole_vmem()] * (2 * len(own) + 2 + len(bases)),
         out_specs=whole_vmem(),
         scratch_shapes=[
             pltpu.VMEM((shape[0] + width, depth), jnp.bfloat16),
             pltpu.VMEM((depth, shape[1]), jnp.bfloat16),
         ],
         compiler_params=pltpu.CompilerParams(vmem_limit_bytes=VMEM_LIMIT),
+        cost_estimate=pl.CostEstimate(flops=SUM_FLOPS, bytes_accessed=0, transcendentals=0),
         name="sum_groups",
-    )(*own, *other, *uppers)
+    )(*own, *other, *uppers, *bases)
 
 
 def finish_kernel(plan, groups, count, ancestor, early, *refs):
     panels = (refs[:count], refs[count : 2 * count])
     uppers, (out, left, right, result, sent) = refs[2 * count : 2 * count + 2], refs[-5:]
-    width = panels[0][0].shape[1]
     place_groups(plan, groups, panels, uppers, left, right)
-    rows = out.shape[0] // ROW_STEPS
     copies = []
-    for i in range(ROW_STEPS):
-        block = slice(i * rows, (i + 1) * rows)
-        update = jnp.dot(
-            left[width + i * rows : width + (i + 1) * rows, :], right[...], preferred_element_type=jnp.float32
-        )
-        result[block, :] = ancestor[block, :] - (early[block, :] + update)
+    for i, block in enumerate(blocks_of(out.shape[0])):
+        result[block, :] = ancestor[block, :] - (early[block, :] + product(left, right, block))
         copy = pltpu.make_async_copy(result.at[block], out.at[block], sent.at[i])
         copy.start()
         copies.append(copy)
@@ -251,7 +257,7 @@
             pltpu.SemaphoreType.DMA((ROW_STEPS,)),
         ],
         compiler_params=pltpu.CompilerParams(vmem_limit_bytes=VMEM_LIMIT),
-        name="last_group_and_subtract",
+        name="last_chunk_and_write",
     )(ancestor, early, *own, *other, *uppers, *after)
 
 
@@ -268,6 +274,7 @@
 ):
     supernodes, slots = lower_panel.shape[1:3]
     plan = (slots, supernodes)
+    cut = 2 * supernodes * slots // 3
     both, first, second, packed = prepare(
         lower_panel,
         row_ids,
@@ -276,7 +283,7 @@
         upper_panel,
         col_ids,
         col_counts,
-        2 * supernodes * slots // 3,
+        cut,
     )
     near = swap(both, "col", 1)
     far_first = swap(first, "col", 2)
@@ -295,23 +302,33 @@
         ancestor.shape[1],
     )
     uppers = (upper, siblings(upper))
-    last_first, first_mark = lax.optimization_barrier((last_first, touched(last_first)))
-    last_second, second_mark = lax.optimization_barrier((last_second, touched(last_second)))
     early = sum_groups(
         plan,
-        (((0,), 0), ((1,), 1), ((2, 3), 2)),
-        [both, near, far_first, far_second],
-        [other_both, siblings(near), other_first, siblings(far_second)],
+        (((0,), 0, 0, 0), ((1, 2), 1, 0, 2)),
+        [both, far_first, far_second],
+        [other_both, other_first, siblings(far_second)],
         uppers,
         ancestor.shape,
+    )
+    last_first, first_mark = lax.optimization_barrier((last_first, touched(last_first)))
+    last_second, second_mark = lax.optimization_barrier((last_second, touched(last_second, [early])))
+    other_last = siblings(last_first)
+    early = sum_groups(
+        plan,
+        (((0,), 0, 0, 1), ((1,), 1, 0, 3)),
+        [near, last_first],
+        [siblings(near), other_last],
+        uppers,
+        ancestor.shape,
+        [early],
     )
     return finish(
         plan,
         ancestor,
         early,
-        (((0, 1), 3),),
-        [last_first, last_second],
-        [siblings(last_first), siblings(last_second)],
+        (((0,), 1, cut, 3),),
+        [last_second, last_first],
+        [siblings(last_second), other_last],
         uppers,
         [far_mark, first_mark, second_mark],
     )

time: 37 us -> 36.4 us (0.984)
  waiting for transfers between devices: 9.63 us -> 7.93 us
  Pallas kernels: 6.38 us -> 7.47 us
    ppermute x5, waiting for transfers between devices: 9.61 us -> 7.91 us  [swap(): return lax.ppermute(array, axis, [(i, i ^ mask) for i in range(4)])]
    pallas_call x1 -> x2, Pallas kernels: 2.57 us -> 3.78 us  [sum_groups(): pl.pallas_call(functools.partial(sum_kernel, plan, groups, len(own), len(...]
  transfers between devices with their start and end apart: 12 -> 12, of which waited for: 4 -> 4; matrix products, arithmetic and copies ran while one was open for 0% -> 0% of each run, Pallas kernels for 8% -> 11%
where the time goes in v5:
time: 36.4 us; the launch traced here: 36.2 us
  blocking collectives  12.5 us (34%)
  starting transfers between devices  8.21 us (23%)
  waiting for transfers between devices  7.93 us (22%)
  Pallas kernels  7.47 us (21%)
    all_gather x1, blocking collectives, on_line_of_four(): packed = lax.all_gather(packed, 'row', axis=0, tiled=True)  12.5 us
    ppermute x5, waiting for transfers between devices, swap(): return lax.ppermute(array, axis, [(i, i ^ mask) for i in range(4)])  7.91 us
    ppermute x5, starting transfers between devices, swap(): return lax.ppermute(array, axis, [(i, i ^ mask) for i in range(4)])  7.33 us
    pallas_call x2, Pallas kernels, sum_groups(): pl.pallas_call(functools.partial(sum_kernel, plan, groups, len(own), len(...  3.78 us
    pallas_call x1, Pallas kernels, finish(): pl.pallas_call(functools.partial(finish_kernel, plan, groups, len(own)),...  1.81 us
    pallas_call x1, Pallas kernels, prepare(): pl.pallas_call(prepare_kernel, out_shape=(jax.ShapeDtypeStruct((tiles * w...  1.53 us
    ppermute x7, starting transfers between devices, siblings(): return lax.ppermute(array, 'gz', [(0, 1), (1, 0)])  0.89 us
  transfers between devices with their start and end apart: 12, of which 4 were waited for; matrix products, arithmetic and copies ran while one was open for 0% of the time, Pallas kernels for 11%

profile of v5, /device:TPU:0, one launch (start us, length us, event | category | flops | bytes accessed | tf_op | source)
XLA Modules:
  0.0 36.2 jit_solution(9005775538713856043)
XLA Ops:
  0.0 1.5 %solve_and_pack.1 = (bf16[1552,128]{1,0:T(8,128)(2,1)S(1)}, bf16[1040,128]{1,0:T(8,128)(2,1)S(1)}, bf16[512,128]{1,0:T(8,128)(2,1)S(1)}, bf16[784,128]{1,0:T(8,128)(2,1)S(1)}) custom-call(s32[1,2,6]{2,1,0:T(2,128)} %row_ids_in.1, s32[1,1,2]{2,1,0:T(1,128)} %bitcast.2, s32[1,2,3]{2,1,0:T(2,128)} %col_ids_in.1, s32[1,1,2]{2,1,0:T(1,128)} %bitcast.3, ...), custom_call_target="tpu_custom_call" | custom-call | tf_op jit(solution)/shard_map/solve_and_pack/pallas_call | solution.py:86
  1.5 4.1 %collective-permute-start.1 = (bf16[1040,128]{1,0:T(8,128)(2,1)S(1)}, bf16[1040,128]{1,0:T(8,128)(2,1)S(1)}, u32[]{:S(2)}, u32[]{:S(2)}) collective-permute-start(bf16[1040,128]{1,0:T(8,128)(2,1)S(1)} %get-tuple-element.18), channel_id=1, source_target_pairs={{0,2},{1,3},{2,0},{3,1},{4,6},{5,7},{6,4},{7,5},{8,10},{9,11},{10,... | collective-permute-start | bytes 798728 | tf_op jit(solution)/shard_map/ppermute | solution.py:265
  5.6 1.6 %collective-permute-start = (bf16[1552,128]{1,0:T(8,128)(2,1)S(1)}, bf16[1552,128]{1,0:T(8,128)(2,1)S(1)}, u32[]{:S(2)}, u32[]{:S(2)}) collective-permute-start(bf16[1552,128]{1,0:T(8,128)(2,1)S(1)} %get-tuple-element.17.refs_0_), channel_id=1, source_target_pairs={{0,1},{1,0},{2,3},{3,2},{4,5},{5,4},{6,7},{7,6},{8,9},{9,8},{10,11... | collective-permute-start | bytes 1191944 | tf_op jit(solution)/shard_map/ppermute | solution.py:265
  7.2 0.0 collective-permute-start.6
  7.2 0.3 collective-permute-start.5
  7.6 12.5 %all_gather.3.packed = bf16[3136,128]{1,0:T(8,128)(2,1)S(1)} all-gather(bf16[784,128]{1,0:T(8,128)(2,1)S(1)} %get-tuple-element.19), channel_id=1, replica_groups=mesh['gz'=2,'row'=4,'col'=4] {'row'}, dimensions={0}, use_global_device_ids=true | all-gather | bytes 1003520 | tf_op jit(solution)/shard_map/all_gather | solution.py:291
  20.1 0.0 collective-permute-done.1.refs_1_
  20.1 0.5 %collective-permute-start.2 = (bf16[1040,128]{1,0:T(8,128)(2,1)S(1)}, bf16[1040,128]{1,0:T(8,128)(2,1)S(1)}, u32[]{:S(2)}, u32[]{:S(2)}) collective-permute-start(bf16[1040,128]{1,0:T(8,128)(2,1)S(1)} %collective-permute-done.1.refs_1_), channel_id=1, source_target_pairs={{0,1},{1,0},{2,3},{3,2},{4,5},{5,4},{6,7},{7,6},{8,9},{9,8},{10,11... | collective-permute-start | bytes 798728 | tf_op jit(solution)/shard_map/ppermute | solution.py:265
  20.5 0.0 collective-permute-start.7
  20.5 3.3 %collective-permute-done.5.panel.refs_1_.refs_2_ = bf16[512,128]{1,0:T(8,128)(2,1)S(1)} collective-permute-done((bf16[512,128]{1,0:T(8,128)(2,1)S(1)}, bf16[512,128]{1,0:T(8,128)(2,1)S(1)}, u32[]{:S(2)}, u32[]{:S(2)}) %collective-permute-start.5) | collective-permute-done | bytes 131104 | tf_op jit(solution)/shard_map/ppermute | solution.py:265
  23.8 1.3 %collective-permute-done.refs_0_ = bf16[1552,128]{1,0:T(8,128)(2,1)S(1)} collective-permute-done((bf16[1552,128]{1,0:T(8,128)(2,1)S(1)}, bf16[1552,128]{1,0:T(8,128)(2,1)S(1)}, u32[]{:S(2)}, u32[]{:S(2)}) %collective-permute-start) | collective-permute-done | bytes 397344 | tf_op jit(solution)/shard_map/ppermute | solution.py:265
  25.1 0.0 collective-permute-done.6.refs_2_.refs_3_
  25.1 0.0 collective-permute-done.7.refs_3_.refs_4_
  25.1 0.3 spread_uppers.1.refs_6_.refs_4_
  25.5 0.1 collective-permute-start.8
  25.6 0.5 %collective-permute-start.9 = (bf16[512,128]{1,0:T(8,128)(2,1)S(1)}, bf16[512,128]{1,0:T(8,128)(2,1)S(1)}, u32[]{:S(2)}, u32[]{:S(2)}) collective-permute-start(bf16[512,128]{1,0:T(8,128)(2,1)S(1)} %collective-permute-done.5.panel.refs_1_.refs_2_), channel_id=1, source_target_pairs={{0,16},{16,0},{1,17},{17,1},{2,18},{18,2},{3,19},{19,3},{4,20},{20... | collective-permute-start | bytes 393224 | tf_op jit(solution)/shard_map/ppermute | solution.py:269
  26.1 0.9 %collective-permute-start.10 = (bf16[512,128]{1,0:T(8,128)(2,1)S(1)}, bf16[512,128]{1,0:T(8,128)(2,1)S(1)}, u32[]{:S(2)}, u32[]{:S(2)}) collective-permute-start(bf16[512,128]{1,0:T(8,128)(2,1)S(1)} %collective-permute-done.5.panel.refs_1_.refs_2_), channel_id=1, source_target_pairs={{0,1},{1,0},{2,3},{3,2},{4,5},{5,4},{6,7},{7,6},{8,9},{9,8},{10,11... | collective-permute-start | bytes 393224 | tf_op jit(solution)/shard_map/ppermute | solution.py:265
  26.9 0.0 collective-permute-start.3
  26.9 3.0 %collective-permute-done.2.panel.refs_1_ = bf16[1040,128]{1,0:T(8,128)(2,1)S(1)} collective-permute-done((bf16[1040,128]{1,0:T(8,128)(2,1)S(1)}, bf16[1040,128]{1,0:T(8,128)(2,1)S(1)}, u32[]{:S(2)}, u32[]{:S(2)}) %collective-permute-start.2) | collective-permute-done | bytes 266272 | tf_op jit(solution)/shard_map/ppermute | solution.py:265
  29.9 0.0 collective-permute-start.4
  29.9 0.0 collective-permute-done.9.refs_5_
  29.9 0.0 collective-permute-done.8.refs_7_.refs_5_
  29.9 1.9 %sum_groups.2.refs_6_.refs_0_ = f32[1024,512]{1,0:T(8,128)S(1)} custom-call(bf16[1552,128]{1,0:T(8,128)(2,1)S(1)} %get-tuple-element.17.refs_0_, bf16[1040,128]{1,0:T(8,128)(2,1)S(1)} %collective-permute-done.1.refs_1_, bf16[512,128]{1,0:T(8,128)(2,1)S(1)} %collective-permute-done.5.panel.refs_1_.refs_2_, ...), custom_call_target="tpu_custom_call" | custom-call | flops 2000000000 | tf_op jit(solution)/shard_map/sum_groups/pallas_call | solution.py:216
  31.9 0.3 collective-permute-done.10.panel.refs_0_
  32.2 0.0 copy-start
  32.2 0.3 collective-permute-start.11
  32.5 0.0 collective-permute-done.3.refs_2_
  32.5 0.0 collective-permute-done.4.refs_3_
  32.5 1.9 %sum_groups.3.early = f32[1024,512]{1,0:T(8,128)S(1)} custom-call(bf16[1552,128]{1,0:T(8,128)(2,1)S(1)} %collective-permute-done.refs_0_, bf16[1040,128]{1,0:T(8,128)(2,1)S(1)} %collective-permute-done.2.panel.refs_1_, bf16[1552,128]{1,0:T(8,128)(2,1)S(1)} %collective-permute-done.3.refs_2_, bf16[1040,128]{1,0:T(8,128)(2,1)S(1)} %collective-permute-done.4.refs_3_, ...), custom_call_target="tpu_custom_call" | custom-call | flops 2000000000 | tf_op jit(solution)/shard_map/sum_groups/pallas_call | solution.py:216
  34.4 0.0 collective-permute-done.11.refs_2_
  34.4 0.0 copy-done
  34.4 1.8 %last_chunk_and_write.1 = f32[1024,512]{1,0:T(8,128)} custom-call(f32[1024,512]{1,0:T(8,128)S(1)} %copy-done, f32[1024,512]{1,0:T(8,128)S(1)} %sum_groups.3.early, bf16[512,128]{1,0:T(8,128)(2,1)S(1)} %collective-permute-done.10.panel.refs_0_, bf16[1040,128]{1,0:T(8,128)(2,1)S(1)} %collective-permute-done.2.panel.refs_1_, ...), custom_call_target="tpu_custom_call" | custom-call | tf_op jit(solution)/shard_map/last_chunk_and_write/pallas_call | solution.py:248
  (3 shorter events, 0.0 us)
Async XLA Ops:
  1.5 18.5 %collective-permute-start.1 = (bf16[1040,128]{1,0:T(8,128)(2,1)S(1)}, bf16[1040,128]{1,0:T(8,128)(2,1)S(1)}, u32[]{:S(2)}, u32[]{:S(2)}) collective-permute-start(bf16[1040,128]{1,0:T(8,128)(2,1)S(1)} %get-tuple-element.18), channel_id=1, source_target_pairs={{0,2},{1,3},{2,0},{3,1},{4,6},{5,7},{6,4},{7,5},{8,10},{9,11},{10,... | collective-permute-start | bytes 798728 | tf_op jit(solution)/shard_map/ppermute | solution.py:265
  5.6 19.5 %collective-permute-start = (bf16[1552,128]{1,0:T(8,128)(2,1)S(1)}, bf16[1552,128]{1,0:T(8,128)(2,1)S(1)}, u32[]{:S(2)}, u32[]{:S(2)}) collective-permute-start(bf16[1552,128]{1,0:T(8,128)(2,1)S(1)} %get-tuple-element.17.refs_0_), channel_id=1, source_target_pairs={{0,1},{1,0},{2,3},{3,2},{4,5},{5,4},{6,7},{7,6},{8,9},{9,8},{10,11... | collective-permute-start | bytes 1191944 | tf_op jit(solution)/shard_map/ppermute | solution.py:265
  7.2 17.9 %collective-permute-start.6 = (bf16[1552,128]{1,0:T(8,128)(2,1)S(1)}, bf16[1552,128]{1,0:T(8,128)(2,1)S(1)}, u32[]{:S(2)}, u32[]{:S(2)}) collective-permute-start(bf16[1552,128]{1,0:T(8,128)(2,1)S(1)} %get-tuple-element.17.refs_0_), channel_id=1, source_target_pairs={{0,16},{16,0},{1,17},{17,1},{2,18},{18,2},{3,19},{19,3},{4,20},{20... | collective-permute-start | bytes 1191944 | tf_op jit(solution)/shard_map/ppermute | solution.py:269
  7.2 16.6 %collective-permute-start.5 = (bf16[512,128]{1,0:T(8,128)(2,1)S(1)}, bf16[512,128]{1,0:T(8,128)(2,1)S(1)}, u32[]{:S(2)}, u32[]{:S(2)}) collective-permute-start(bf16[512,128]{1,0:T(8,128)(2,1)S(1)} %get-tuple-element.23), channel_id=1, source_target_pairs={{0,2},{1,3},{2,0},{3,1},{4,6},{5,7},{6,4},{7,5},{8,10},{9,11},{10,... | collective-permute-start | bytes 393224 | tf_op jit(solution)/shard_map/ppermute | solution.py:265
  20.1 9.9 %collective-permute-start.2 = (bf16[1040,128]{1,0:T(8,128)(2,1)S(1)}, bf16[1040,128]{1,0:T(8,128)(2,1)S(1)}, u32[]{:S(2)}, u32[]{:S(2)}) collective-permute-start(bf16[1040,128]{1,0:T(8,128)(2,1)S(1)} %collective-permute-done.1.refs_1_), channel_id=1, source_target_pairs={{0,1},{1,0},{2,3},{3,2},{4,5},{5,4},{6,7},{7,6},{8,9},{9,8},{10,11... | collective-permute-start | bytes 798728 | tf_op jit(solution)/shard_map/ppermute | solution.py:265
  20.5 4.6 %collective-permute-start.7 = (bf16[1040,128]{1,0:T(8,128)(2,1)S(1)}, bf16[1040,128]{1,0:T(8,128)(2,1)S(1)}, u32[]{:S(2)}, u32[]{:S(2)}) collective-permute-start(bf16[1040,128]{1,0:T(8,128)(2,1)S(1)} %collective-permute-done.1.refs_1_), channel_id=1, source_target_pairs={{0,16},{16,0},{1,17},{17,1},{2,18},{18,2},{3,19},{19,3},{4,20},{20... | collective-permute-start | bytes 798728 | tf_op jit(solution)/shard_map/ppermute | solution.py:269
  25.5 4.5 %collective-permute-start.8 = (bf16[1024,512]{1,0:T(8,128)(2,1)S(1)}, bf16[1024,512]{1,0:T(8,128)(2,1)S(1)}, u32[]{:S(2)}, u32[]{:S(2)}) collective-permute-start(bf16[1024,512]{1,0:T(8,128)(2,1)S(1)} %spread_uppers.1.refs_6_.refs_4_), channel_id=1, source_target_pairs={{0,16},{16,0},{1,17},{17,1},{2,18},{18,2},{3,19},{19,3},{4,20},{20... | collective-permute-start | bytes 3145736 | tf_op jit(solution)/shard_map/ppermute | solution.py:269
  25.6 4.4 %collective-permute-start.9 = (bf16[512,128]{1,0:T(8,128)(2,1)S(1)}, bf16[512,128]{1,0:T(8,128)(2,1)S(1)}, u32[]{:S(2)}, u32[]{:S(2)}) collective-permute-start(bf16[512,128]{1,0:T(8,128)(2,1)S(1)} %collective-permute-done.5.panel.refs_1_.refs_2_), channel_id=1, source_target_pairs={{0,16},{16,0},{1,17},{17,1},{2,18},{18,2},{3,19},{19,3},{4,20},{20... | collective-permute-start | bytes 393224 | tf_op jit(solution)/shard_map/ppermute | solution.py:269
  26.1 6.1 %collective-permute-start.10 = (bf16[512,128]{1,0:T(8,128)(2,1)S(1)}, bf16[512,128]{1,0:T(8,128)(2,1)S(1)}, u32[]{:S(2)}, u32[]{:S(2)}) collective-permute-start(bf16[512,128]{1,0:T(8,128)(2,1)S(1)} %collective-permute-done.5.panel.refs_1_.refs_2_), channel_id=1, source_target_pairs={{0,1},{1,0},{2,3},{3,2},{4,5},{5,4},{6,7},{7,6},{8,9},{9,8},{10,11... | collective-permute-start | bytes 393224 | tf_op jit(solution)/shard_map/ppermute | solution.py:265
  26.9 5.6 %collective-permute-start.3 = (bf16[1552,128]{1,0:T(8,128)(2,1)S(1)}, bf16[1552,128]{1,0:T(8,128)(2,1)S(1)}, u32[]{:S(2)}, u32[]{:S(2)}) collective-permute-start(bf16[1552,128]{1,0:T(8,128)(2,1)S(1)} %collective-permute-done.refs_0_), channel_id=1, source_target_pairs={{0,16},{16,0},{1,17},{17,1},{2,18},{18,2},{3,19},{19,3},{4,20},{20... | collective-permute-start | bytes 1191944 | tf_op jit(solution)/shard_map/ppermute | solution.py:269
  29.9 2.6 %collective-permute-start.4 = (bf16[1040,128]{1,0:T(8,128)(2,1)S(1)}, bf16[1040,128]{1,0:T(8,128)(2,1)S(1)}, u32[]{:S(2)}, u32[]{:S(2)}) collective-permute-start(bf16[1040,128]{1,0:T(8,128)(2,1)S(1)} %collective-permute-done.2.panel.refs_1_), channel_id=1, source_target_pairs={{0,16},{16,0},{1,17},{17,1},{2,18},{18,2},{3,19},{19,3},{4,20},{20... | collective-permute-start | bytes 798728 | tf_op jit(solution)/shard_map/ppermute | solution.py:269
  32.2 2.2 %copy-start = (f32[1024,512]{1,0:T(8,128)S(1)}, f32[1024,512]{1,0:T(8,128)}, u32[]{:S(2)}) copy-start(f32[1024,512]{1,0:T(8,128)} %ancestor.1) | copy-start | bytes 6291460
  32.2 2.2 %collective-permute-start.11 = (bf16[512,128]{1,0:T(8,128)(2,1)S(1)}, bf16[512,128]{1,0:T(8,128)(2,1)S(1)}, u32[]{:S(2)}, u32[]{:S(2)}) collective-permute-start(bf16[512,128]{1,0:T(8,128)(2,1)S(1)} %collective-permute-done.10.panel.refs_0_), channel_id=1, source_target_pairs={{0,16},{16,0},{1,17},{17,1},{2,18},{18,2},{3,19},{19,3},{4,20},{20... | collective-permute-start | bytes 393224 | tf_op jit(solution)/shard_map/ppermute | solution.py:269

commit v6 on v5

--- a/solution.py
+++ b/solution.py
@@ -291,12 +291,12 @@
     packed = lax.all_gather(packed, "row", axis=0, tiled=True)
     far_first, packed = lax.optimization_barrier((far_first, packed))
     last_first = swap(far_first, "col", 1)
-    far_second, far_mark = lax.optimization_barrier((far_second, touched(far_second)))
+    far_second, far_mark = lax.optimization_barrier((far_second, touched(far_second, [near])))
     last_second = swap(far_second, "col", 1)
     other_both, other_first = siblings(both), siblings(far_first)
     upper = spread_uppers(
         packed,
-        [near, far_second, other_both, other_first],
+        [near, far_second, other_both],
         upper_panel.shape[2],
         supernodes,
         ancestor.shape[1],

time: 36.4 us -> 35.2 us (0.967)
  waiting for transfers between devices: 7.93 us -> 2.01 us
  starting transfers between devices: 8.21 us -> 13 us
    ppermute x5, waiting for transfers between devices: 7.91 us -> 1.99 us  [swap(): return lax.ppermute(array, axis, [(i, i ^ mask) for i in range(4)])]
    ppermute x5, starting transfers between devices: 7.33 us -> 11.8 us  [swap(): return lax.ppermute(array, axis, [(i, i ^ mask) for i in range(4)])]
  transfers between devices with their start and end apart: 12 -> 12, of which waited for: 4 -> 3; matrix products, arithmetic and copies ran while one was open for 0% -> 0% of each run, Pallas kernels for 11% -> 12%
where the time goes in v6:
time: 35.2 us; the launch traced here: 35 us
  starting transfers between devices  13 us (37%)
  blocking collectives  12.5 us (36%)
  Pallas kernels  7.47 us (21%)
  waiting for transfers between devices  2.01 us (6%)
    all_gather x1, blocking collectives, on_line_of_four(): packed = lax.all_gather(packed, 'row', axis=0, tiled=True)  12.5 us
    ppermute x5, starting transfers between devices, swap(): return lax.ppermute(array, axis, [(i, i ^ mask) for i in range(4)])  11.8 us
    pallas_call x2, Pallas kernels, sum_groups(): pl.pallas_call(functools.partial(sum_kernel, plan, groups, len(own), len(...  3.78 us
    ppermute x5, waiting for transfers between devices, swap(): return lax.ppermute(array, axis, [(i, i ^ mask) for i in range(4)])  1.99 us
    pallas_call x1, Pallas kernels, finish(): pl.pallas_call(functools.partial(finish_kernel, plan, groups, len(own)),...  1.81 us
    pallas_call x1, Pallas kernels, prepare(): pl.pallas_call(prepare_kernel, out_shape=(jax.ShapeDtypeStruct((tiles * w...  1.53 us
    ppermute x7, starting transfers between devices, siblings(): return lax.ppermute(array, 'gz', [(0, 1), (1, 0)])  1.16 us
  transfers between devices with their start and end apart: 12, of which 3 were waited for; matrix products, arithmetic and copies ran while one was open for 0% of the time, Pallas kernels for 12%

profile of v6, /device:TPU:0, one launch (start us, length us, event | category | flops | bytes accessed | tf_op | source)
XLA Modules:
  0.0 35.0 jit_solution(7470881116464607316)
XLA Ops:
  0.0 1.5 %solve_and_pack.1 = (bf16[1552,128]{1,0:T(8,128)(2,1)S(1)}, bf16[1040,128]{1,0:T(8,128)(2,1)S(1)}, bf16[512,128]{1,0:T(8,128)(2,1)S(1)}, bf16[784,128]{1,0:T(8,128)(2,1)S(1)}) custom-call(s32[1,2,6]{2,1,0:T(2,128)} %row_ids_in.1, s32[1,1,2]{2,1,0:T(1,128)} %bitcast.2, s32[1,2,3]{2,1,0:T(2,128)} %col_ids_in.1, s32[1,1,2]{2,1,0:T(1,128)} %bitcast.3, ...), custom_call_target="tpu_custom_call" | custom-call | tf_op jit(solution)/shard_map/solve_and_pack/pallas_call | solution.py:86
  1.5 3.1 %collective-permute-start = (bf16[1552,128]{1,0:T(8,128)(2,1)S(1)}, bf16[1552,128]{1,0:T(8,128)(2,1)S(1)}, u32[]{:S(2)}, u32[]{:S(2)}) collective-permute-start(bf16[1552,128]{1,0:T(8,128)(2,1)S(1)} %get-tuple-element.17.refs_0_), channel_id=1, source_target_pairs={{0,1},{1,0},{2,3},{3,2},{4,5},{5,4},{6,7},{7,6},{8,9},{9,8},{10,11... | collective-permute-start | bytes 1191944 | tf_op jit(solution)/shard_map/ppermute | solution.py:265
  4.6 2.6 %collective-permute-start.1 = (bf16[1040,128]{1,0:T(8,128)(2,1)S(1)}, bf16[1040,128]{1,0:T(8,128)(2,1)S(1)}, u32[]{:S(2)}, u32[]{:S(2)}) collective-permute-start(bf16[1040,128]{1,0:T(8,128)(2,1)S(1)} %get-tuple-element.18), channel_id=1, source_target_pairs={{0,2},{1,3},{2,0},{3,1},{4,6},{5,7},{6,4},{7,5},{8,10},{9,11},{10,... | collective-permute-start | bytes 798728 | tf_op jit(solution)/shard_map/ppermute | solution.py:265
  7.2 0.0 collective-permute-start.6
  7.2 0.3 collective-permute-start.5
  7.6 12.5 %all_gather.3.packed = bf16[3136,128]{1,0:T(8,128)(2,1)S(1)} all-gather(bf16[784,128]{1,0:T(8,128)(2,1)S(1)} %get-tuple-element.19), channel_id=1, replica_groups=mesh['gz'=2,'row'=4,'col'=4] {'row'}, dimensions={0}, use_global_device_ids=true | all-gather | bytes 1003520 | tf_op jit(solution)/shard_map/all_gather | solution.py:291
  20.1 0.0 collective-permute-done.1.refs_1_
  20.1 3.5 %collective-permute-start.2 = (bf16[1040,128]{1,0:T(8,128)(2,1)S(1)}, bf16[1040,128]{1,0:T(8,128)(2,1)S(1)}, u32[]{:S(2)}, u32[]{:S(2)}) collective-permute-start(bf16[1040,128]{1,0:T(8,128)(2,1)S(1)} %collective-permute-done.1.refs_1_), channel_id=1, source_target_pairs={{0,1},{1,0},{2,3},{3,2},{4,5},{5,4},{6,7},{7,6},{8,9},{9,8},{10,11... | collective-permute-start | bytes 798728 | tf_op jit(solution)/shard_map/ppermute | solution.py:265
  23.5 0.3 collective-permute-done.5.panel.refs_1_.refs_2_
  23.9 0.0 collective-permute-done.refs_0_
  23.9 0.0 collective-permute-done.6.refs_2_.refs_3_
  23.9 0.3 spread_uppers.1.refs_6_.refs_4_
  24.2 0.1 collective-permute-start.7
  24.3 0.5 %collective-permute-start.8 = (bf16[1040,128]{1,0:T(8,128)(2,1)S(1)}, bf16[1040,128]{1,0:T(8,128)(2,1)S(1)}, u32[]{:S(2)}, u32[]{:S(2)}) collective-permute-start(bf16[1040,128]{1,0:T(8,128)(2,1)S(1)} %collective-permute-done.1.refs_1_), channel_id=1, source_target_pairs={{0,16},{16,0},{1,17},{17,1},{2,18},{18,2},{3,19},{19,3},{4,20},{20... | collective-permute-start | bytes 798728 | tf_op jit(solution)/shard_map/ppermute | solution.py:269
  24.8 0.1 collective-permute-start.9
  24.9 2.3 %collective-permute-start.10 = (bf16[512,128]{1,0:T(8,128)(2,1)S(1)}, bf16[512,128]{1,0:T(8,128)(2,1)S(1)}, u32[]{:S(2)}, u32[]{:S(2)}) collective-permute-start(bf16[512,128]{1,0:T(8,128)(2,1)S(1)} %collective-permute-done.5.panel.refs_1_.refs_2_), channel_id=1, source_target_pairs={{0,1},{1,0},{2,3},{3,2},{4,5},{5,4},{6,7},{7,6},{8,9},{9,8},{10,11... | collective-permute-start | bytes 393224 | tf_op jit(solution)/shard_map/ppermute | solution.py:265
  27.2 0.9 %collective-permute-done.2.panel.refs_1_ = bf16[1040,128]{1,0:T(8,128)(2,1)S(1)} collective-permute-done((bf16[1040,128]{1,0:T(8,128)(2,1)S(1)}, bf16[1040,128]{1,0:T(8,128)(2,1)S(1)}, u32[]{:S(2)}, u32[]{:S(2)}) %collective-permute-start.2) | collective-permute-done | bytes 266272 | tf_op jit(solution)/shard_map/ppermute | solution.py:265
  28.1 0.0 collective-permute-start.3
  28.1 0.0 collective-permute-done.9.refs_5_
  28.1 0.5 %collective-permute-start.4 = (bf16[1040,128]{1,0:T(8,128)(2,1)S(1)}, bf16[1040,128]{1,0:T(8,128)(2,1)S(1)}, u32[]{:S(2)}, u32[]{:S(2)}) collective-permute-start(bf16[1040,128]{1,0:T(8,128)(2,1)S(1)} %collective-permute-done.2.panel.refs_1_), channel_id=1, source_target_pairs={{0,16},{16,0},{1,17},{17,1},{2,18},{18,2},{3,19},{19,3},{4,20},{20... | collective-permute-start | bytes 798728 | tf_op jit(solution)/shard_map/ppermute | solution.py:269
  28.6 0.0 collective-permute-done.8.refs_4_
  28.6 0.0 collective-permute-done.7.refs_7_.refs_5_
  28.6 1.9 %sum_groups.2.refs_6_.refs_0_ = f32[1024,512]{1,0:T(8,128)S(1)} custom-call(bf16[1552,128]{1,0:T(8,128)(2,1)S(1)} %get-tuple-element.17.refs_0_, bf16[1040,128]{1,0:T(8,128)(2,1)S(1)} %collective-permute-done.1.refs_1_, bf16[512,128]{1,0:T(8,128)(2,1)S(1)} %collective-permute-done.5.panel.refs_1_.refs_2_, ...), custom_call_target="tpu_custom_call" | custom-call | flops 2000000000 | tf_op jit(solution)/shard_map/sum_groups/pallas_call | solution.py:216
  30.5 0.8 %collective-permute-done.10.panel.refs_0_ = bf16[512,128]{1,0:T(8,128)(2,1)S(1)} collective-permute-done((bf16[512,128]{1,0:T(8,128)(2,1)S(1)}, bf16[512,128]{1,0:T(8,128)(2,1)S(1)}, u32[]{:S(2)}, u32[]{:S(2)}) %collective-permute-start.10) | collective-permute-done | bytes 131104 | tf_op jit(solution)/shard_map/ppermute | solution.py:265
  31.3 0.0 copy-start
  31.3 0.0 collective-permute-start.11
  31.3 0.0 collective-permute-done.3.refs_2_
  31.3 0.0 collective-permute-done.4.refs_3_
  31.3 1.9 %sum_groups.3.early = f32[1024,512]{1,0:T(8,128)S(1)} custom-call(bf16[1552,128]{1,0:T(8,128)(2,1)S(1)} %collective-permute-done.refs_0_, bf16[1040,128]{1,0:T(8,128)(2,1)S(1)} %collective-permute-done.2.panel.refs_1_, bf16[1552,128]{1,0:T(8,128)(2,1)S(1)} %collective-permute-done.3.refs_2_, bf16[1040,128]{1,0:T(8,128)(2,1)S(1)} %collective-permute-done.4.refs_3_, ...), custom_call_target="tpu_custom_call" | custom-call | flops 2000000000 | tf_op jit(solution)/shard_map/sum_groups/pallas_call | solution.py:216
  33.2 0.0 collective-permute-done.11.refs_2_
  33.2 0.0 copy-done
  33.2 1.8 %last_chunk_and_write.1 = f32[1024,512]{1,0:T(8,128)} custom-call(f32[1024,512]{1,0:T(8,128)S(1)} %copy-done, f32[1024,512]{1,0:T(8,128)S(1)} %sum_groups.3.early, bf16[512,128]{1,0:T(8,128)(2,1)S(1)} %collective-permute-done.10.panel.refs_0_, bf16[1040,128]{1,0:T(8,128)(2,1)S(1)} %collective-permute-done.2.panel.refs_1_, ...), custom_call_target="tpu_custom_call" | custom-call | tf_op jit(solution)/shard_map/last_chunk_and_write/pallas_call | solution.py:248
  (3 shorter events, 0.0 us)
Async XLA Ops:
  1.5 22.3 %collective-permute-start = (bf16[1552,128]{1,0:T(8,128)(2,1)S(1)}, bf16[1552,128]{1,0:T(8,128)(2,1)S(1)}, u32[]{:S(2)}, u32[]{:S(2)}) collective-permute-start(bf16[1552,128]{1,0:T(8,128)(2,1)S(1)} %get-tuple-element.17.refs_0_), channel_id=1, source_target_pairs={{0,1},{1,0},{2,3},{3,2},{4,5},{5,4},{6,7},{7,6},{8,9},{9,8},{10,11... | collective-permute-start | bytes 1191944 | tf_op jit(solution)/shard_map/ppermute | solution.py:265
  4.6 15.4 %collective-permute-start.1 = (bf16[1040,128]{1,0:T(8,128)(2,1)S(1)}, bf16[1040,128]{1,0:T(8,128)(2,1)S(1)}, u32[]{:S(2)}, u32[]{:S(2)}) collective-permute-start(bf16[1040,128]{1,0:T(8,128)(2,1)S(1)} %get-tuple-element.18), channel_id=1, source_target_pairs={{0,2},{1,3},{2,0},{3,1},{4,6},{5,7},{6,4},{7,5},{8,10},{9,11},{10,... | collective-permute-start | bytes 798728 | tf_op jit(solution)/shard_map/ppermute | solution.py:265
  7.2 16.7 %collective-permute-start.6 = (bf16[1552,128]{1,0:T(8,128)(2,1)S(1)}, bf16[1552,128]{1,0:T(8,128)(2,1)S(1)}, u32[]{:S(2)}, u32[]{:S(2)}) collective-permute-start(bf16[1552,128]{1,0:T(8,128)(2,1)S(1)} %get-tuple-element.17.refs_0_), channel_id=1, source_target_pairs={{0,16},{16,0},{1,17},{17,1},{2,18},{18,2},{3,19},{19,3},{4,20},{20... | collective-permute-start | bytes 1191944 | tf_op jit(solution)/shard_map/ppermute | solution.py:269
  7.2 16.7 %collective-permute-start.5 = (bf16[512,128]{1,0:T(8,128)(2,1)S(1)}, bf16[512,128]{1,0:T(8,128)(2,1)S(1)}, u32[]{:S(2)}, u32[]{:S(2)}) collective-permute-start(bf16[512,128]{1,0:T(8,128)(2,1)S(1)} %get-tuple-element.23), channel_id=1, source_target_pairs={{0,2},{1,3},{2,0},{3,1},{4,6},{5,7},{6,4},{7,5},{8,10},{9,11},{10,... | collective-permute-start | bytes 393224 | tf_op jit(solution)/shard_map/ppermute | solution.py:265
  20.1 8.0 %collective-permute-start.2 = (bf16[1040,128]{1,0:T(8,128)(2,1)S(1)}, bf16[1040,128]{1,0:T(8,128)(2,1)S(1)}, u32[]{:S(2)}, u32[]{:S(2)}) collective-permute-start(bf16[1040,128]{1,0:T(8,128)(2,1)S(1)} %collective-permute-done.1.refs_1_), channel_id=1, source_target_pairs={{0,1},{1,0},{2,3},{3,2},{4,5},{5,4},{6,7},{7,6},{8,9},{9,8},{10,11... | collective-permute-start | bytes 798728 | tf_op jit(solution)/shard_map/ppermute | solution.py:265
  24.2 4.3 %collective-permute-start.7 = (bf16[1024,512]{1,0:T(8,128)(2,1)S(1)}, bf16[1024,512]{1,0:T(8,128)(2,1)S(1)}, u32[]{:S(2)}, u32[]{:S(2)}) collective-permute-start(bf16[1024,512]{1,0:T(8,128)(2,1)S(1)} %spread_uppers.1.refs_6_.refs_4_), channel_id=1, source_target_pairs={{0,16},{16,0},{1,17},{17,1},{2,18},{18,2},{3,19},{19,3},{4,20},{20... | collective-permute-start | bytes 3145736 | tf_op jit(solution)/shard_map/ppermute | solution.py:269
  24.3 4.3 %collective-permute-start.8 = (bf16[1040,128]{1,0:T(8,128)(2,1)S(1)}, bf16[1040,128]{1,0:T(8,128)(2,1)S(1)}, u32[]{:S(2)}, u32[]{:S(2)}) collective-permute-start(bf16[1040,128]{1,0:T(8,128)(2,1)S(1)} %collective-permute-done.1.refs_1_), channel_id=1, source_target_pairs={{0,16},{16,0},{1,17},{17,1},{2,18},{18,2},{3,19},{19,3},{4,20},{20... | collective-permute-start | bytes 798728 | tf_op jit(solution)/shard_map/ppermute | solution.py:269
  24.8 3.2 %collective-permute-start.9 = (bf16[512,128]{1,0:T(8,128)(2,1)S(1)}, bf16[512,128]{1,0:T(8,128)(2,1)S(1)}, u32[]{:S(2)}, u32[]{:S(2)}) collective-permute-start(bf16[512,128]{1,0:T(8,128)(2,1)S(1)} %collective-permute-done.5.panel.refs_1_.refs_2_), channel_id=1, source_target_pairs={{0,16},{16,0},{1,17},{17,1},{2,18},{18,2},{3,19},{19,3},{4,20},{20... | collective-permute-start | bytes 393224 | tf_op jit(solution)/shard_map/ppermute | solution.py:269
  24.9 6.4 %collective-permute-start.10 = (bf16[512,128]{1,0:T(8,128)(2,1)S(1)}, bf16[512,128]{1,0:T(8,128)(2,1)S(1)}, u32[]{:S(2)}, u32[]{:S(2)}) collective-permute-start(bf16[512,128]{1,0:T(8,128)(2,1)S(1)} %collective-permute-done.5.panel.refs_1_.refs_2_), channel_id=1, source_target_pairs={{0,1},{1,0},{2,3},{3,2},{4,5},{5,4},{6,7},{7,6},{8,9},{9,8},{10,11... | collective-permute-start | bytes 393224 | tf_op jit(solution)/shard_map/ppermute | solution.py:265
  28.1 3.2 %collective-permute-start.3 = (bf16[1552,128]{1,0:T(8,128)(2,1)S(1)}, bf16[1552,128]{1,0:T(8,128)(2,1)S(1)}, u32[]{:S(2)}, u32[]{:S(2)}) collective-permute-start(bf16[1552,128]{1,0:T(8,128)(2,1)S(1)} %collective-permute-done.refs_0_), channel_id=1, source_target_pairs={{0,16},{16,0},{1,17},{17,1},{2,18},{18,2},{3,19},{19,3},{4,20},{20... | collective-permute-start | bytes 1191944 | tf_op jit(solution)/shard_map/ppermute | solution.py:269
  28.1 3.2 %collective-permute-start.4 = (bf16[1040,128]{1,0:T(8,128)(2,1)S(1)}, bf16[1040,128]{1,0:T(8,128)(2,1)S(1)}, u32[]{:S(2)}, u32[]{:S(2)}) collective-permute-start(bf16[1040,128]{1,0:T(8,128)(2,1)S(1)} %collective-permute-done.2.panel.refs_1_), channel_id=1, source_target_pairs={{0,16},{16,0},{1,17},{17,1},{2,18},{18,2},{3,19},{19,3},{4,20},{20... | collective-permute-start | bytes 798728 | tf_op jit(solution)/shard_map/ppermute | solution.py:269
  31.3 1.9 %copy-start = (f32[1024,512]{1,0:T(8,128)S(1)}, f32[1024,512]{1,0:T(8,128)}, u32[]{:S(2)}) copy-start(f32[1024,512]{1,0:T(8,128)} %ancestor.1) | copy-start | bytes 6291460
  31.3 1.9 %collective-permute-start.11 = (bf16[512,128]{1,0:T(8,128)(2,1)S(1)}, bf16[512,128]{1,0:T(8,128)(2,1)S(1)}, u32[]{:S(2)}, u32[]{:S(2)}) collective-permute-start(bf16[512,128]{1,0:T(8,128)(2,1)S(1)} %collective-permute-done.10.panel.refs_0_), channel_id=1, source_target_pairs={{0,16},{16,0},{1,17},{17,1},{2,18},{18,2},{3,19},{19,3},{4,20},{20... | collective-permute-start | bytes 393224 | tf_op jit(solution)/shard_map/ppermute | solution.py:269

commit v7 on v6

--- a/solution.py
+++ b/solution.py
@@ -161,29 +161,36 @@
     )(panel, *after)
 
 
-def place_group(parts, ids, first, slots, supernodes, left, base):
+def place_group(parts, ids, first, slots, left, base):
     width = parts[0].shape[1]
     tiles = [(part, row) for part in parts for row in range(part.shape[0] // width)]
     ids = read_ids(ids[ids.shape[0] - ID_ROWS :, :])
     for tile, (part, row) in enumerate(tiles, first):
         at = pl.multiple_of(ids[tile, 0] * width, width)
-        columns = pl.ds(pl.multiple_of(base + tile // slots * width, width), width)
+        columns = pl.ds(pl.multiple_of(base + (tile // slots - first // slots) * width, width), width)
         left[pl.ds(at, width), columns] = part[row * width : (row + 1) * width, :]
+
+
+def deep_of(plan, groups):
+    slots, supernodes = plan
+    return [supernodes - first // slots for _, _, first, _ in groups]
 
 
 def place_groups(plan, groups, panels, uppers, left, right):
     slots, supernodes = plan
     width = panels[0][0].shape[1]
-    tall = supernodes * width
     column = lax.axis_index("col")
     layer = lax.axis_index("gz")
+    deep = deep_of(plan, groups)
     left[...] = jnp.zeros_like(left)
     for side, (tiles, upper) in enumerate(zip(panels, uppers)):
-        base = (layer if side == 0 else 1 - layer) * (len(groups) * tall)
-        for n, (members, ids, first, mask) in enumerate(groups):
-            start = pl.multiple_of(base + n * tall, tall)
-            right[pl.ds(start, tall), :] = upper[pl.ds(pl.multiple_of((column ^ mask) * tall, tall), tall), :]
-            place_group([tiles[member] for member in members], tiles[ids], first, slots, supernodes, left, start)
+        start = (layer if side == 0 else 1 - layer) * (sum(deep) * width)
+        for (members, ids, first, mask), span in zip(groups, deep):
+            start = pl.multiple_of(start, width)
+            rows = pl.multiple_of(((column ^ mask) * supernodes + first // slots) * width, width)
+            right[pl.ds(start, span * width), :] = upper[pl.ds(rows, span * width), :]
+            place_group([tiles[member] for member in members], tiles[ids], first, slots, left, start)
+            start += span * width
 
 
 def blocks_of(rows):
@@ -212,7 +219,7 @@
 
 def sum_groups(plan, groups, own, other, uppers, shape, bases=()):
     width = own[0].shape[1]
-    depth = 2 * len(groups) * plan[1] * width
+    depth = 2 * sum(deep_of(plan, groups)) * width
     return pl.pallas_call(
         functools.partial(sum_kernel, plan, groups, len(own), len(bases)),
         out_shape=jax.ShapeDtypeStruct(shape, jnp.float32),
@@ -244,7 +251,7 @@
 
 def finish(plan, ancestor, early, groups, own, other, uppers, after):
     width = own[0].shape[1]
-    depth = 2 * len(groups) * plan[1] * width
+    depth = 2 * sum(deep_of(plan, groups)) * width
     return pl.pallas_call(
         functools.partial(finish_kernel, plan, groups, len(own)),
         out_shape=jax.ShapeDtypeStruct(ancestor.shape, jnp.float32),
@@ -310,14 +317,17 @@
         uppers,
         ancestor.shape,
     )
+    early = sum_groups(
+        plan, (((0,), 0, 0, 1),), [near], [siblings(near)], uppers, ancestor.shape, [early]
+    )
     last_first, first_mark = lax.optimization_barrier((last_first, touched(last_first)))
     last_second, second_mark = lax.optimization_barrier((last_second, touched(last_second, [early])))
     other_last = siblings(last_first)
     early = sum_groups(
         plan,
-        (((0,), 0, 0, 1), ((1,), 1, 0, 3)),
-        [near, last_first],
-        [siblings(near), other_last],
+        (((0,), 0, 0, 3),),
+        [last_first],
+        [other_last],
         uppers,
         ancestor.shape,
         [early],

time: 35.2 us -> 35 us (level)
  waiting for transfers between devices: 2.01 us -> 1.52 us
    ppermute x5, waiting for transfers between devices: 1.99 us -> 1.2 us  [swap(): return lax.ppermute(array, axis, [(i, i ^ mask) for i in range(4)])]
    pallas_call x2 -> x3, Pallas kernels: 3.78 us -> 3.84 us  [sum_groups(): pl.pallas_call(functools.partial(sum_kernel, plan, groups, len(own), len(...]
where the time goes in v7:
time: 35 us; the launch traced here: 34.8 us
  starting transfers between devices  13.1 us (37%)
  blocking collectives  12.5 us (36%)
  Pallas kernels  7.41 us (21%)
  waiting for transfers between devices  1.52 us (4%)
    all_gather x1, blocking collectives, on_line_of_four(): packed = lax.all_gather(packed, 'row', axis=0, tiled=True)  12.5 us
    ppermute x5, starting transfers between devices, swap(): return lax.ppermute(array, axis, [(i, i ^ mask) for i in range(4)])  11.8 us
    pallas_call x3, Pallas kernels, sum_groups(): pl.pallas_call(functools.partial(sum_kernel, plan, groups, len(own), len(...  3.84 us
    pallas_call x1, Pallas kernels, finish(): pl.pallas_call(functools.partial(finish_kernel, plan, groups, len(own)),...  1.7 us
    pallas_call x1, Pallas kernels, prepare(): pl.pallas_call(prepare_kernel, out_shape=(jax.ShapeDtypeStruct((tiles * w...  1.53 us
    ppermute x7, starting transfers between devices, siblings(): return lax.ppermute(array, 'gz', [(0, 1), (1, 0)])  1.31 us
    ppermute x5, waiting for transfers between devices, swap(): return lax.ppermute(array, axis, [(i, i ^ mask) for i in range(4)])  1.2 us
  transfers between devices with their start and end apart: 12, of which 3 were waited for; matrix products, arithmetic and copies ran while one was open for 0% of the time, Pallas kernels for 12%

profile of v7, /device:TPU:0, one launch (start us, length us, event | category | flops | bytes accessed | tf_op | source)
XLA Modules:
  0.0 34.8 jit_solution(15282293542034162199)
XLA Ops:
  0.0 1.5 %solve_and_pack.1 = (bf16[1552,128]{1,0:T(8,128)(2,1)S(1)}, bf16[1040,128]{1,0:T(8,128)(2,1)S(1)}, bf16[512,128]{1,0:T(8,128)(2,1)S(1)}, bf16[784,128]{1,0:T(8,128)(2,1)S(1)}) custom-call(s32[1,2,6]{2,1,0:T(2,128)} %row_ids_in.1, s32[1,1,2]{2,1,0:T(1,128)} %bitcast.2, s32[1,2,3]{2,1,0:T(2,128)} %col_ids_in.1, s32[1,1,2]{2,1,0:T(1,128)} %bitcast.3, ...), custom_call_target="tpu_custom_call" | custom-call | tf_op jit(solution)/shard_map/solve_and_pack/pallas_call | solution.py:86
  1.5 3.1 %collective-permute-start.3 = (bf16[1552,128]{1,0:T(8,128)(2,1)S(1)}, bf16[1552,128]{1,0:T(8,128)(2,1)S(1)}, u32[]{:S(2)}, u32[]{:S(2)}) collective-permute-start(bf16[1552,128]{1,0:T(8,128)(2,1)S(1)} %get-tuple-element.22.refs_0_), channel_id=1, source_target_pairs={{0,1},{1,0},{2,3},{3,2},{4,5},{5,4},{6,7},{7,6},{8,9},{9,8},{10,11... | collective-permute-start | bytes 1191944 | tf_op jit(solution)/shard_map/ppermute | solution.py:272
  4.6 2.6 %collective-permute-start = (bf16[1040,128]{1,0:T(8,128)(2,1)S(1)}, bf16[1040,128]{1,0:T(8,128)(2,1)S(1)}, u32[]{:S(2)}, u32[]{:S(2)}) collective-permute-start(bf16[1040,128]{1,0:T(8,128)(2,1)S(1)} %get-tuple-element.17), channel_id=1, source_target_pairs={{0,2},{1,3},{2,0},{3,1},{4,6},{5,7},{6,4},{7,5},{8,10},{9,11},{10,... | collective-permute-start | bytes 798728 | tf_op jit(solution)/shard_map/ppermute | solution.py:272
  7.2 0.0 collective-permute-start.5
  7.2 0.3 collective-permute-start.4
  7.6 12.5 %all_gather.3.packed = bf16[3136,128]{1,0:T(8,128)(2,1)S(1)} all-gather(bf16[784,128]{1,0:T(8,128)(2,1)S(1)} %get-tuple-element.18), channel_id=1, replica_groups=mesh['gz'=2,'row'=4,'col'=4] {'row'}, dimensions={0}, use_global_device_ids=true | all-gather | bytes 1003520 | tf_op jit(solution)/shard_map/all_gather | solution.py:298
  20.1 0.0 collective-permute-done.refs_1_
  20.1 3.5 %collective-permute-start.1 = (bf16[1040,128]{1,0:T(8,128)(2,1)S(1)}, bf16[1040,128]{1,0:T(8,128)(2,1)S(1)}, u32[]{:S(2)}, u32[]{:S(2)}) collective-permute-start(bf16[1040,128]{1,0:T(8,128)(2,1)S(1)} %collective-permute-done.refs_1_), channel_id=1, source_target_pairs={{0,1},{1,0},{2,3},{3,2},{4,5},{5,4},{6,7},{7,6},{8,9},{9,8},{10,11... | collective-permute-start | bytes 798728 | tf_op jit(solution)/shard_map/ppermute | solution.py:272
  23.5 0.3 collective-permute-done.4.panel.refs_1_.refs_2_
  23.9 0.0 collective-permute-done.3.refs_0_
  23.9 0.0 collective-permute-done.5.refs_2_.refs_3_
  23.9 0.3 spread_uppers.1.refs_6_.refs_2_.refs_4_
  24.2 0.1 collective-permute-start.6
  24.3 0.5 %collective-permute-start.8 = (bf16[1040,128]{1,0:T(8,128)(2,1)S(1)}, bf16[1040,128]{1,0:T(8,128)(2,1)S(1)}, u32[]{:S(2)}, u32[]{:S(2)}) collective-permute-start(bf16[1040,128]{1,0:T(8,128)(2,1)S(1)} %collective-permute-done.refs_1_), channel_id=1, source_target_pairs={{0,16},{16,0},{1,17},{17,1},{2,18},{18,2},{3,19},{19,3},{4,20},{20... | collective-permute-start | bytes 798728 | tf_op jit(solution)/shard_map/ppermute | solution.py:276
  24.8 0.1 collective-permute-start.9
  24.9 2.3 %collective-permute-start.10 = (bf16[512,128]{1,0:T(8,128)(2,1)S(1)}, bf16[512,128]{1,0:T(8,128)(2,1)S(1)}, u32[]{:S(2)}, u32[]{:S(2)}) collective-permute-start(bf16[512,128]{1,0:T(8,128)(2,1)S(1)} %collective-permute-done.4.panel.refs_1_.refs_2_), channel_id=1, source_target_pairs={{0,1},{1,0},{2,3},{3,2},{4,5},{5,4},{6,7},{7,6},{8,9},{9,8},{10,11... | collective-permute-start | bytes 393224 | tf_op jit(solution)/shard_map/ppermute | solution.py:272
  27.2 0.9 %collective-permute-done.1.panel.refs_0_.refs_1_ = bf16[1040,128]{1,0:T(8,128)(2,1)S(1)} collective-permute-done((bf16[1040,128]{1,0:T(8,128)(2,1)S(1)}, bf16[1040,128]{1,0:T(8,128)(2,1)S(1)}, u32[]{:S(2)}, u32[]{:S(2)}) %collective-permute-start.1) | collective-permute-done | bytes 266272 | tf_op jit(solution)/shard_map/ppermute | solution.py:272
  28.1 0.0 collective-permute-start.7
  28.1 0.0 collective-permute-done.9.refs_5_
  28.1 0.5 %collective-permute-start.2 = (bf16[1040,128]{1,0:T(8,128)(2,1)S(1)}, bf16[1040,128]{1,0:T(8,128)(2,1)S(1)}, u32[]{:S(2)}, u32[]{:S(2)}) collective-permute-start(bf16[1040,128]{1,0:T(8,128)(2,1)S(1)} %collective-permute-done.1.panel.refs_0_.refs_1_), channel_id=1, source_target_pairs={{0,16},{16,0},{1,17},{17,1},{2,18},{18,2},{3,19},{19,3},{4,20},{20... | collective-permute-start | bytes 798728 | tf_op jit(solution)/shard_map/ppermute | solution.py:276
  28.6 0.0 collective-permute-done.8.refs_4_
  28.6 0.0 collective-permute-done.6.refs_7_.refs_3_.refs_5_
  28.6 1.9 %sum_groups.3.refs_4_ = f32[1024,512]{1,0:T(8,128)S(1)} custom-call(bf16[1552,128]{1,0:T(8,128)(2,1)S(1)} %get-tuple-element.22.refs_0_, bf16[1040,128]{1,0:T(8,128)(2,1)S(1)} %collective-permute-done.refs_1_, bf16[512,128]{1,0:T(8,128)(2,1)S(1)} %collective-permute-done.4.panel.refs_1_.refs_2_, ...), custom_call_target="tpu_custom_call" | custom-call | flops 2000000000 | tf_op jit(solution)/shard_map/sum_groups/pallas_call | solution.py:223
  30.5 1.0 %sum_groups.4.refs_4_.refs_0_ = f32[1024,512]{1,0:T(8,128)S(1)} custom-call(bf16[1552,128]{1,0:T(8,128)(2,1)S(1)} %collective-permute-done.3.refs_0_, bf16[1552,128]{1,0:T(8,128)(2,1)S(1)} %collective-permute-done.7.refs_1_, bf16[1024,512]{1,0:T(8,128)(2,1)S(1)} %spread_uppers.1.refs_6_.refs_2_.refs_4_, ...), custom_call_target="tpu_custom_call" | custom-call | flops 2000000000 | tf_op jit(solution)/shard_map/sum_groups/pallas_call | solution.py:223
  31.5 0.0 collective-permute-done.10.panel.refs_0_
  31.5 0.0 copy-start
  31.5 0.2 collective-permute-start.11
  31.7 0.0 collective-permute-done.2.refs_1_.refs_3_
  31.7 1.0 %sum_groups.5.early = f32[1024,512]{1,0:T(8,128)S(1)} custom-call(bf16[1040,128]{1,0:T(8,128)(2,1)S(1)} %collective-permute-done.1.panel.refs_0_.refs_1_, bf16[1040,128]{1,0:T(8,128)(2,1)S(1)} %collective-permute-done.2.refs_1_.refs_3_, bf16[1024,512]{1,0:T(8,128)(2,1)S(1)} %spread_uppers.1.refs_6_.refs_2_.refs_4_, ...), custom_call_target="tpu_custom_call" | custom-call | flops 2000000000 | tf_op jit(solution)/shard_map/sum_groups/pallas_call | solution.py:223
  32.6 0.3 collective-permute-done.11.refs_2_
  32.9 0.2 copy-done
  33.1 1.7 %last_chunk_and_write.1 = f32[1024,512]{1,0:T(8,128)} custom-call(f32[1024,512]{1,0:T(8,128)S(1)} %copy-done, f32[1024,512]{1,0:T(8,128)S(1)} %sum_groups.5.early, bf16[512,128]{1,0:T(8,128)(2,1)S(1)} %collective-permute-done.10.panel.refs_0_, bf16[1040,128]{1,0:T(8,128)(2,1)S(1)} %collective-permute-done.1.panel.refs_0_.refs_1_, ...), custom_call_target="tpu_custom_call" | custom-call | tf_op jit(solution)/shard_map/last_chunk_and_write/pallas_call | solution.py:255
  (4 shorter events, 0.0 us)
Async XLA Ops:
  1.5 22.3 %collective-permute-start.3 = (bf16[1552,128]{1,0:T(8,128)(2,1)S(1)}, bf16[1552,128]{1,0:T(8,128)(2,1)S(1)}, u32[]{:S(2)}, u32[]{:S(2)}) collective-permute-start(bf16[1552,128]{1,0:T(8,128)(2,1)S(1)} %get-tuple-element.22.refs_0_), channel_id=1, source_target_pairs={{0,1},{1,0},{2,3},{3,2},{4,5},{5,4},{6,7},{7,6},{8,9},{9,8},{10,11... | collective-permute-start | bytes 1191944 | tf_op jit(solution)/shard_map/ppermute | solution.py:272
  4.6 15.4 %collective-permute-start = (bf16[1040,128]{1,0:T(8,128)(2,1)S(1)}, bf16[1040,128]{1,0:T(8,128)(2,1)S(1)}, u32[]{:S(2)}, u32[]{:S(2)}) collective-permute-start(bf16[1040,128]{1,0:T(8,128)(2,1)S(1)} %get-tuple-element.17), channel_id=1, source_target_pairs={{0,2},{1,3},{2,0},{3,1},{4,6},{5,7},{6,4},{7,5},{8,10},{9,11},{10,... | collective-permute-start | bytes 798728 | tf_op jit(solution)/shard_map/ppermute | solution.py:272
  7.2 16.7 %collective-permute-start.5 = (bf16[1552,128]{1,0:T(8,128)(2,1)S(1)}, bf16[1552,128]{1,0:T(8,128)(2,1)S(1)}, u32[]{:S(2)}, u32[]{:S(2)}) collective-permute-start(bf16[1552,128]{1,0:T(8,128)(2,1)S(1)} %get-tuple-element.22.refs_0_), channel_id=1, source_target_pairs={{0,16},{16,0},{1,17},{17,1},{2,18},{18,2},{3,19},{19,3},{4,20},{20... | collective-permute-start | bytes 1191944 | tf_op jit(solution)/shard_map/ppermute | solution.py:276
  7.2 16.7 %collective-permute-start.4 = (bf16[512,128]{1,0:T(8,128)(2,1)S(1)}, bf16[512,128]{1,0:T(8,128)(2,1)S(1)}, u32[]{:S(2)}, u32[]{:S(2)}) collective-permute-start(bf16[512,128]{1,0:T(8,128)(2,1)S(1)} %get-tuple-element.23), channel_id=1, source_target_pairs={{0,2},{1,3},{2,0},{3,1},{4,6},{5,7},{6,4},{7,5},{8,10},{9,11},{10,... | collective-permute-start | bytes 393224 | tf_op jit(solution)/shard_map/ppermute | solution.py:272
  20.1 8.0 %collective-permute-start.1 = (bf16[1040,128]{1,0:T(8,128)(2,1)S(1)}, bf16[1040,128]{1,0:T(8,128)(2,1)S(1)}, u32[]{:S(2)}, u32[]{:S(2)}) collective-permute-start(bf16[1040,128]{1,0:T(8,128)(2,1)S(1)} %collective-permute-done.refs_1_), channel_id=1, source_target_pairs={{0,1},{1,0},{2,3},{3,2},{4,5},{5,4},{6,7},{7,6},{8,9},{9,8},{10,11... | collective-permute-start | bytes 798728 | tf_op jit(solution)/shard_map/ppermute | solution.py:272
  24.2 4.3 %collective-permute-start.6 = (bf16[1024,512]{1,0:T(8,128)(2,1)S(1)}, bf16[1024,512]{1,0:T(8,128)(2,1)S(1)}, u32[]{:S(2)}, u32[]{:S(2)}) collective-permute-start(bf16[1024,512]{1,0:T(8,128)(2,1)S(1)} %spread_uppers.1.refs_6_.refs_2_.refs_4_), channel_id=1, source_target_pairs={{0,16},{16,0},{1,17},{17,1},{2,18},{18,2},{3,19},{19,3},{4,20},{20... | collective-permute-start | bytes 3145736 | tf_op jit(solution)/shard_map/ppermute | solution.py:276
  24.3 4.3 %collective-permute-start.8 = (bf16[1040,128]{1,0:T(8,128)(2,1)S(1)}, bf16[1040,128]{1,0:T(8,128)(2,1)S(1)}, u32[]{:S(2)}, u32[]{:S(2)}) collective-permute-start(bf16[1040,128]{1,0:T(8,128)(2,1)S(1)} %collective-permute-done.refs_1_), channel_id=1, source_target_pairs={{0,16},{16,0},{1,17},{17,1},{2,18},{18,2},{3,19},{19,3},{4,20},{20... | collective-permute-start | bytes 798728 | tf_op jit(solution)/shard_map/ppermute | solution.py:276
  24.8 3.2 %collective-permute-start.9 = (bf16[512,128]{1,0:T(8,128)(2,1)S(1)}, bf16[512,128]{1,0:T(8,128)(2,1)S(1)}, u32[]{:S(2)}, u32[]{:S(2)}) collective-permute-start(bf16[512,128]{1,0:T(8,128)(2,1)S(1)} %collective-permute-done.4.panel.refs_1_.refs_2_), channel_id=1, source_target_pairs={{0,16},{16,0},{1,17},{17,1},{2,18},{18,2},{3,19},{19,3},{4,20},{20... | collective-permute-start | bytes 393224 | tf_op jit(solution)/shard_map/ppermute | solution.py:276
  24.9 6.6 %collective-permute-start.10 = (bf16[512,128]{1,0:T(8,128)(2,1)S(1)}, bf16[512,128]{1,0:T(8,128)(2,1)S(1)}, u32[]{:S(2)}, u32[]{:S(2)}) collective-permute-start(bf16[512,128]{1,0:T(8,128)(2,1)S(1)} %collective-permute-done.4.panel.refs_1_.refs_2_), channel_id=1, source_target_pairs={{0,1},{1,0},{2,3},{3,2},{4,5},{5,4},{6,7},{7,6},{8,9},{9,8},{10,11... | collective-permute-start | bytes 393224 | tf_op jit(solution)/shard_map/ppermute | solution.py:272
  28.1 2.5 %collective-permute-start.7 = (bf16[1552,128]{1,0:T(8,128)(2,1)S(1)}, bf16[1552,128]{1,0:T(8,128)(2,1)S(1)}, u32[]{:S(2)}, u32[]{:S(2)}) collective-permute-start(bf16[1552,128]{1,0:T(8,128)(2,1)S(1)} %collective-permute-done.3.refs_0_), channel_id=1, source_target_pairs={{0,16},{16,0},{1,17},{17,1},{2,18},{18,2},{3,19},{19,3},{4,20},{20... | collective-permute-start | bytes 1191944 | tf_op jit(solution)/shard_map/ppermute | solution.py:276
  28.1 3.6 %collective-permute-start.2 = (bf16[1040,128]{1,0:T(8,128)(2,1)S(1)}, bf16[1040,128]{1,0:T(8,128)(2,1)S(1)}, u32[]{:S(2)}, u32[]{:S(2)}) collective-permute-start(bf16[1040,128]{1,0:T(8,128)(2,1)S(1)} %collective-permute-done.1.panel.refs_0_.refs_1_), channel_id=1, source_target_pairs={{0,16},{16,0},{1,17},{17,1},{2,18},{18,2},{3,19},{19,3},{4,20},{20... | collective-permute-start | bytes 798728 | tf_op jit(solution)/shard_map/ppermute | solution.py:276
  31.5 1.6 %copy-start = (f32[1024,512]{1,0:T(8,128)S(1)}, f32[1024,512]{1,0:T(8,128)}, u32[]{:S(2)}) copy-start(f32[1024,512]{1,0:T(8,128)} %ancestor.1) | copy-start | bytes 6291460
  31.5 1.4 %collective-permute-start.11 = (bf16[512,128]{1,0:T(8,128)(2,1)S(1)}, bf16[512,128]{1,0:T(8,128)(2,1)S(1)}, u32[]{:S(2)}, u32[]{:S(2)}) collective-permute-start(bf16[512,128]{1,0:T(8,128)(2,1)S(1)} %collective-permute-done.10.panel.refs_0_), channel_id=1, source_target_pairs={{0,16},{16,0},{1,17},{17,1},{2,18},{18,2},{3,19},{19,3},{4,20},{20... | collective-permute-start | bytes 393224 | tf_op jit(solution)/shard_map/ppermute | solution.py:276

commit v8 on v7

--- a/solution.py
+++ b/solution.py
@@ -11,7 +11,7 @@
 ID_ROWS = 16
 ROW_STEPS = 4
 DECLARED_FLOPS = 10_000_000_000
-SUM_FLOPS = 2_000_000_000
+SUM_FLOPS = 1_000_000_000
 
 
 def whole_vmem():
@@ -130,18 +130,20 @@
     out[...] = padded[:, width:]
 
 
-def spread_uppers(packed, after, slots, supernodes, columns):
+def spread_uppers(packed, after, held, slots, supernodes, columns):
     width = packed.shape[1]
     deep = packed.shape[0] // (supernodes * slots * width + ID_ROWS) * supernodes * width
     return pl.pallas_call(
         functools.partial(spread_kernel, slots, supernodes),
         out_shape=jax.ShapeDtypeStruct((deep, columns), jnp.bfloat16),
-        in_specs=[whole_vmem()] + [pl.BlockSpec(memory_space=pl.ANY)] * len(after),
+        in_specs=[whole_vmem()]
+        + [pl.BlockSpec(memory_space=pl.ANY)] * len(after)
+        + [whole_vmem()] * len(held),
         out_specs=whole_vmem(),
         scratch_shapes=[pltpu.VMEM((deep, columns + width), jnp.bfloat16)],
         compiler_params=pltpu.CompilerParams(vmem_limit_bytes=VMEM_LIMIT),
         name="spread_uppers",
-    )(packed, *after)
+    )(packed, *after, *held)
 
 
 def touch_kernel(panel, *refs):
@@ -184,7 +186,7 @@
     deep = deep_of(plan, groups)
     left[...] = jnp.zeros_like(left)
     for side, (tiles, upper) in enumerate(zip(panels, uppers)):
-        start = (layer if side == 0 else 1 - layer) * (sum(deep) * width)
+        start = (layer if side == 0 else 1 - layer) * (sum(deep) * width) if len(panels) == 2 else 0
         for (members, ids, first, mask), span in zip(groups, deep):
             start = pl.multiple_of(start, width)
             rows = pl.multiple_of(((column ^ mask) * supernodes + first // slots) * width, width)
@@ -205,10 +207,11 @@
     )
 
 
-def sum_kernel(plan, groups, count, bases, *refs):
-    panels = (refs[:count], refs[count : 2 * count])
-    uppers, base_refs = refs[2 * count : 2 * count + 2], refs[2 * count + 2 : 2 * count + 2 + bases]
-    out, left, right = refs[-3:]
+def sum_kernel(plan, groups, sides, bases, *refs):
+    count = (len(refs) - sides - bases - 3) // sides
+    panels = [refs[side * count : (side + 1) * count] for side in range(sides)]
+    uppers = refs[sides * count : sides * count + sides]
+    base_refs, (out, left, right) = refs[sides * (count + 1) : -3], refs[-3:]
     place_groups(plan, groups, panels, uppers, left, right)
     for block in blocks_of(out.shape[0]):
         update = product(left, right, block)
@@ -217,13 +220,14 @@
         out[block, :] = update
 
 
-def sum_groups(plan, groups, own, other, uppers, shape, bases=()):
-    width = own[0].shape[1]
-    depth = 2 * sum(deep_of(plan, groups)) * width
-    return pl.pallas_call(
-        functools.partial(sum_kernel, plan, groups, len(own), len(bases)),
+def sum_groups(plan, groups, panels, uppers, shape, bases=()):
+    sides = len(panels)
+    width = panels[0][0].shape[1]
+    depth = sides * sum(deep_of(plan, groups)) * width
+    return pl.pallas_call(
+        functools.partial(sum_kernel, plan, groups, sides, len(bases)),
         out_shape=jax.ShapeDtypeStruct(shape, jnp.float32),
-        in_specs=[whole_vmem()] * (2 * len(own) + 2 + len(bases)),
+        in_specs=[whole_vmem()] * (sides * (len(panels[0]) + 1) + len(bases)),
         out_specs=whole_vmem(),
         scratch_shapes=[
             pltpu.VMEM((shape[0] + width, depth), jnp.bfloat16),
@@ -232,7 +236,7 @@
         compiler_params=pltpu.CompilerParams(vmem_limit_bytes=VMEM_LIMIT),
         cost_estimate=pl.CostEstimate(flops=SUM_FLOPS, bytes_accessed=0, transcendentals=0),
         name="sum_groups",
-    )(*own, *other, *uppers, *bases)
+    )(*(panel for side in panels for panel in side), *uppers, *bases)
 
 
 def finish_kernel(plan, groups, count, ancestor, early, *refs):
@@ -304,33 +308,24 @@
     upper = spread_uppers(
         packed,
         [near, far_second, other_both],
+        [ancestor],
         upper_panel.shape[2],
         supernodes,
         ancestor.shape[1],
     )
     uppers = (upper, siblings(upper))
+    groups = (((0,), 0, 0, 0), ((1, 2), 1, 0, 2))
+    early = sum_groups(plan, groups, [[both, far_first, far_second]], [upper], ancestor.shape)
+    others = [other_both, other_first, siblings(far_second)]
+    early = sum_groups(plan, groups, [others], [uppers[1]], ancestor.shape, [early])
     early = sum_groups(
-        plan,
-        (((0,), 0, 0, 0), ((1, 2), 1, 0, 2)),
-        [both, far_first, far_second],
-        [other_both, other_first, siblings(far_second)],
-        uppers,
-        ancestor.shape,
-    )
-    early = sum_groups(
-        plan, (((0,), 0, 0, 1),), [near], [siblings(near)], uppers, ancestor.shape, [early]
+        plan, (((0,), 0, 0, 1),), [[near], [siblings(near)]], uppers, ancestor.shape, [early]
     )
     last_first, first_mark = lax.optimization_barrier((last_first, touched(last_first)))
     last_second, second_mark = lax.optimization_barrier((last_second, touched(last_second, [early])))
     other_last = siblings(last_first)
     early = sum_groups(
-        plan,
-        (((0,), 0, 0, 3),),
-        [last_first],
-        [other_last],
-        uppers,
-        ancestor.shape,
-        [early],
+        plan, (((0,), 0, 0, 3),), [[last_first], [other_last]], uppers, ancestor.shape, [early]
     )
     return finish(
         plan,

time: 35 us -> 34.5 us (0.986)
    ppermute x5, waiting for transfers between devices: 1.2 us -> 0.79 us  [swap(): return lax.ppermute(array, axis, [(i, i ^ mask) for i in range(4)])]
    pallas_call x3 -> x4, Pallas kernels: 3.84 us -> 3.78 us  [sum_groups(): pl.pallas_call(functools.partial(sum_kernel, plan, groups, sides, len(bas...]
  transfers between devices with their start and end apart: 12 -> 12, of which waited for: 3 -> 4; matrix products, arithmetic and copies ran while one was open for 0% -> 0% of each run, Pallas kernels for 12% -> 12%
where the time goes in v8:
time: 34.5 us; the launch traced here: 34.3 us
  starting transfers between devices  12.9 us (37%)
  blocking collectives  12.5 us (36%)
  Pallas kernels  7.37 us (21%)
  waiting for transfers between devices  1.44 us (4%)
    all_gather x1, blocking collectives, on_line_of_four(): packed = lax.all_gather(packed, 'row', axis=0, tiled=True)  12.5 us
    ppermute x5, starting transfers between devices, swap(): return lax.ppermute(array, axis, [(i, i ^ mask) for i in range(4)])  11.7 us
    pallas_call x4, Pallas kernels, sum_groups(): pl.pallas_call(functools.partial(sum_kernel, plan, groups, sides, len(bas...  3.78 us
    pallas_call x1, Pallas kernels, finish(): pl.pallas_call(functools.partial(finish_kernel, plan, groups, len(own)),...  1.7 us
    pallas_call x1, Pallas kernels, prepare(): pl.pallas_call(prepare_kernel, out_shape=(jax.ShapeDtypeStruct((tiles * w...  1.53 us
    ppermute x7, starting transfers between devices, siblings(): return lax.ppermute(array, 'gz', [(0, 1), (1, 0)])  1.23 us
    ppermute x5, waiting for transfers between devices, swap(): return lax.ppermute(array, axis, [(i, i ^ mask) for i in range(4)])  0.79 us
  transfers between devices with their start and end apart: 12, of which 4 were waited for; matrix products, arithmetic and copies ran while one was open for 0% of the time, Pallas kernels for 12%

profile of v8, /device:TPU:0, one launch (start us, length us, event | category | flops | bytes accessed | tf_op | source)
XLA Modules:
  0.0 34.3 jit_solution(3858499529028239527)
XLA Ops:
  0.0 1.5 %solve_and_pack.1 = (bf16[1552,128]{1,0:T(8,128)(2,1)S(1)}, bf16[1040,128]{1,0:T(8,128)(2,1)S(1)}, bf16[512,128]{1,0:T(8,128)(2,1)S(1)}, bf16[784,128]{1,0:T(8,128)(2,1)S(1)}) custom-call(s32[1,2,6]{2,1,0:T(2,128)} %row_ids_in.1, s32[1,1,2]{2,1,0:T(1,128)} %bitcast.2, s32[1,2,3]{2,1,0:T(2,128)} %col_ids_in.1, s32[1,1,2]{2,1,0:T(1,128)} %bitcast.3, ...), custom_call_target="tpu_custom_call" | custom-call | tf_op jit(solution)/shard_map/solve_and_pack/pallas_call | solution.py:86
  1.5 3.1 %collective-permute-start.3 = (bf16[1552,128]{1,0:T(8,128)(2,1)S(1)}, bf16[1552,128]{1,0:T(8,128)(2,1)S(1)}, u32[]{:S(2)}, u32[]{:S(2)}) collective-permute-start(bf16[1552,128]{1,0:T(8,128)(2,1)S(1)} %get-tuple-element.22.refs_0_), channel_id=1, source_target_pairs={{0,1},{1,0},{2,3},{3,2},{4,5},{5,4},{6,7},{7,6},{8,9},{9,8},{10,11... | collective-permute-start | bytes 1191944 | tf_op jit(solution)/shard_map/ppermute | solution.py:276
  4.6 2.6 %collective-permute-start = (bf16[1040,128]{1,0:T(8,128)(2,1)S(1)}, bf16[1040,128]{1,0:T(8,128)(2,1)S(1)}, u32[]{:S(2)}, u32[]{:S(2)}) collective-permute-start(bf16[1040,128]{1,0:T(8,128)(2,1)S(1)} %get-tuple-element.17), channel_id=1, source_target_pairs={{0,2},{1,3},{2,0},{3,1},{4,6},{5,7},{6,4},{7,5},{8,10},{9,11},{10,... | collective-permute-start | bytes 798728 | tf_op jit(solution)/shard_map/ppermute | solution.py:276
  7.2 0.0 collective-permute-start.5
  7.2 0.3 collective-permute-start.4
  7.6 12.5 %all_gather.3.packed = bf16[3136,128]{1,0:T(8,128)(2,1)S(1)} all-gather(bf16[784,128]{1,0:T(8,128)(2,1)S(1)} %get-tuple-element.18), channel_id=1, replica_groups=mesh['gz'=2,'row'=4,'col'=4] {'row'}, dimensions={0}, use_global_device_ids=true | all-gather | bytes 1003520 | tf_op jit(solution)/shard_map/all_gather | solution.py:302
  20.1 0.0 collective-permute-done.refs_1_
  20.1 3.5 %collective-permute-start.1 = (bf16[1040,128]{1,0:T(8,128)(2,1)S(1)}, bf16[1040,128]{1,0:T(8,128)(2,1)S(1)}, u32[]{:S(2)}, u32[]{:S(2)}) collective-permute-start(bf16[1040,128]{1,0:T(8,128)(2,1)S(1)} %collective-permute-done.refs_1_), channel_id=1, source_target_pairs={{0,1},{1,0},{2,3},{3,2},{4,5},{5,4},{6,7},{7,6},{8,9},{9,8},{10,11... | collective-permute-start | bytes 798728 | tf_op jit(solution)/shard_map/ppermute | solution.py:276
  23.5 0.4 %collective-permute-done.4.panel.refs_1_.refs_2_ = bf16[512,128]{1,0:T(8,128)(2,1)S(1)} collective-permute-done((bf16[512,128]{1,0:T(8,128)(2,1)S(1)}, bf16[512,128]{1,0:T(8,128)(2,1)S(1)}, u32[]{:S(2)}, u32[]{:S(2)}) %collective-permute-start.4) | collective-permute-done | bytes 131104 | tf_op jit(solution)/shard_map/ppermute | solution.py:276
  24.0 0.0 collective-permute-done.3.refs_0_
  24.0 0.0 collective-permute-done.5.refs_2_.refs_0_
  24.0 0.3 spread_uppers.1.refs_3_.refs_2_.refs_4_
  24.3 0.1 collective-permute-start.6
  24.4 0.5 %collective-permute-start.8 = (bf16[1040,128]{1,0:T(8,128)(2,1)S(1)}, bf16[1040,128]{1,0:T(8,128)(2,1)S(1)}, u32[]{:S(2)}, u32[]{:S(2)}) collective-permute-start(bf16[1040,128]{1,0:T(8,128)(2,1)S(1)} %collective-permute-done.refs_1_), channel_id=1, source_target_pairs={{0,16},{16,0},{1,17},{17,1},{2,18},{18,2},{3,19},{19,3},{4,20},{20... | collective-permute-start | bytes 798728 | tf_op jit(solution)/shard_map/ppermute | solution.py:280
  24.9 0.1 collective-permute-start.9
  25.0 2.2 %collective-permute-start.10 = (bf16[512,128]{1,0:T(8,128)(2,1)S(1)}, bf16[512,128]{1,0:T(8,128)(2,1)S(1)}, u32[]{:S(2)}, u32[]{:S(2)}) collective-permute-start(bf16[512,128]{1,0:T(8,128)(2,1)S(1)} %collective-permute-done.4.panel.refs_1_.refs_2_), channel_id=1, source_target_pairs={{0,1},{1,0},{2,3},{3,2},{4,5},{5,4},{6,7},{7,6},{8,9},{9,8},{10,11... | collective-permute-start | bytes 393224 | tf_op jit(solution)/shard_map/ppermute | solution.py:276
  27.1 0.9 %sum_groups.4.refs_4_ = f32[1024,512]{1,0:T(8,128)S(1)} custom-call(bf16[1552,128]{1,0:T(8,128)(2,1)S(1)} %get-tuple-element.22.refs_0_, bf16[1040,128]{1,0:T(8,128)(2,1)S(1)} %collective-permute-done.refs_1_, bf16[512,128]{1,0:T(8,128)(2,1)S(1)} %collective-permute-done.4.panel.refs_1_.refs_2_, bf16[1024,512]{1,0:T(8,128)(2,1)S(1)} %spread_uppers.1.refs_3_.refs_2_.refs_4_), custom_call_target="tpu_custom_call" | custom-call | flops 1000000000 | tf_op jit(solution)/shard_map/sum_groups/pallas_call | solution.py:227
  28.1 0.0 collective-permute-done.1.panel.refs_0_.refs_1_
  28.1 0.2 collective-permute-start.7
  28.3 0.0 collective-permute-done.9.refs_2_
  28.3 0.3 %collective-permute-start.2 = (bf16[1040,128]{1,0:T(8,128)(2,1)S(1)}, bf16[1040,128]{1,0:T(8,128)(2,1)S(1)}, u32[]{:S(2)}, u32[]{:S(2)}) collective-permute-start(bf16[1040,128]{1,0:T(8,128)(2,1)S(1)} %collective-permute-done.1.panel.refs_0_.refs_1_), channel_id=1, source_target_pairs={{0,16},{16,0},{1,17},{17,1},{2,18},{18,2},{3,19},{19,3},{4,20},{20... | collective-permute-start | bytes 798728 | tf_op jit(solution)/shard_map/ppermute | solution.py:280
  28.7 0.0 collective-permute-done.8.refs_1_
  28.7 0.0 collective-permute-done.6.refs_3_.refs_5_
  28.7 0.9 %sum_groups.5.refs_4_ = f32[1024,512]{1,0:T(8,128)S(1)} custom-call(bf16[1552,128]{1,0:T(8,128)(2,1)S(1)} %collective-permute-done.5.refs_2_.refs_0_, bf16[1040,128]{1,0:T(8,128)(2,1)S(1)} %collective-permute-done.8.refs_1_, bf16[512,128]{1,0:T(8,128)(2,1)S(1)} %collective-permute-done.9.refs_2_, ...), custom_call_target="tpu_custom_call" | custom-call | flops 1000000000 | tf_op jit(solution)/shard_map/sum_groups/pallas_call | solution.py:227
  29.6 0.3 collective-permute-done.7.refs_1_
  29.9 1.0 %sum_groups.6.refs_4_.refs_0_ = f32[1024,512]{1,0:T(8,128)S(1)} custom-call(bf16[1552,128]{1,0:T(8,128)(2,1)S(1)} %collective-permute-done.3.refs_0_, bf16[1552,128]{1,0:T(8,128)(2,1)S(1)} %collective-permute-done.7.refs_1_, bf16[1024,512]{1,0:T(8,128)(2,1)S(1)} %spread_uppers.1.refs_3_.refs_2_.refs_4_, ...), custom_call_target="tpu_custom_call" | custom-call | flops 1000000000 | tf_op jit(solution)/shard_map/sum_groups/pallas_call | solution.py:227
  30.9 0.4 %collective-permute-done.10.panel.refs_0_ = bf16[512,128]{1,0:T(8,128)(2,1)S(1)} collective-permute-done((bf16[512,128]{1,0:T(8,128)(2,1)S(1)}, bf16[512,128]{1,0:T(8,128)(2,1)S(1)}, u32[]{:S(2)}, u32[]{:S(2)}) %collective-permute-start.10) | collective-permute-done | bytes 131104 | tf_op jit(solution)/shard_map/ppermute | solution.py:276
  31.2 0.0 collective-permute-start.11
  31.2 0.0 collective-permute-done.2.refs_1_.refs_3_
  31.2 1.0 %sum_groups.7.early = f32[1024,512]{1,0:T(8,128)S(1)} custom-call(bf16[1040,128]{1,0:T(8,128)(2,1)S(1)} %collective-permute-done.1.panel.refs_0_.refs_1_, bf16[1040,128]{1,0:T(8,128)(2,1)S(1)} %collective-permute-done.2.refs_1_.refs_3_, bf16[1024,512]{1,0:T(8,128)(2,1)S(1)} %spread_uppers.1.refs_3_.refs_2_.refs_4_, ...), custom_call_target="tpu_custom_call" | custom-call | flops 1000000000 | tf_op jit(solution)/shard_map/sum_groups/pallas_call | solution.py:227
  32.2 0.4 %collective-permute-done.11.refs_2_ = bf16[512,128]{1,0:T(8,128)(2,1)S(1)} collective-permute-done((bf16[512,128]{1,0:T(8,128)(2,1)S(1)}, bf16[512,128]{1,0:T(8,128)(2,1)S(1)}, u32[]{:S(2)}, u32[]{:S(2)}) %collective-permute-start.11) | collective-permute-done | bytes 131104 | tf_op jit(solution)/shard_map/ppermute | solution.py:280
  32.6 1.7 %last_chunk_and_write.1 = f32[1024,512]{1,0:T(8,128)} custom-call(f32[1024,512]{1,0:T(8,128)S(1)} %copy-done, f32[1024,512]{1,0:T(8,128)S(1)} %sum_groups.7.early, bf16[512,128]{1,0:T(8,128)(2,1)S(1)} %collective-permute-done.10.panel.refs_0_, bf16[1040,128]{1,0:T(8,128)(2,1)S(1)} %collective-permute-done.1.panel.refs_0_.refs_1_, ...), custom_call_target="tpu_custom_call" | custom-call | tf_op jit(solution)/shard_map/last_chunk_and_write/pallas_call | solution.py:259
  (5 shorter events, 0.0 us)
Async XLA Ops:
  1.5 22.4 %collective-permute-start.3 = (bf16[1552,128]{1,0:T(8,128)(2,1)S(1)}, bf16[1552,128]{1,0:T(8,128)(2,1)S(1)}, u32[]{:S(2)}, u32[]{:S(2)}) collective-permute-start(bf16[1552,128]{1,0:T(8,128)(2,1)S(1)} %get-tuple-element.22.refs_0_), channel_id=1, source_target_pairs={{0,1},{1,0},{2,3},{3,2},{4,5},{5,4},{6,7},{7,6},{8,9},{9,8},{10,11... | collective-permute-start | bytes 1191944 | tf_op jit(solution)/shard_map/ppermute | solution.py:276
  4.6 15.4 %collective-permute-start = (bf16[1040,128]{1,0:T(8,128)(2,1)S(1)}, bf16[1040,128]{1,0:T(8,128)(2,1)S(1)}, u32[]{:S(2)}, u32[]{:S(2)}) collective-permute-start(bf16[1040,128]{1,0:T(8,128)(2,1)S(1)} %get-tuple-element.17), channel_id=1, source_target_pairs={{0,2},{1,3},{2,0},{3,1},{4,6},{5,7},{6,4},{7,5},{8,10},{9,11},{10,... | collective-permute-start | bytes 798728 | tf_op jit(solution)/shard_map/ppermute | solution.py:276
  7.2 16.7 %collective-permute-start.5 = (bf16[1552,128]{1,0:T(8,128)(2,1)S(1)}, bf16[1552,128]{1,0:T(8,128)(2,1)S(1)}, u32[]{:S(2)}, u32[]{:S(2)}) collective-permute-start(bf16[1552,128]{1,0:T(8,128)(2,1)S(1)} %get-tuple-element.22.refs_0_), channel_id=1, source_target_pairs={{0,16},{16,0},{1,17},{17,1},{2,18},{18,2},{3,19},{19,3},{4,20},{20... | collective-permute-start | bytes 1191944 | tf_op jit(solution)/shard_map/ppermute | solution.py:280
  7.2 16.7 %collective-permute-start.4 = (bf16[512,128]{1,0:T(8,128)(2,1)S(1)}, bf16[512,128]{1,0:T(8,128)(2,1)S(1)}, u32[]{:S(2)}, u32[]{:S(2)}) collective-permute-start(bf16[512,128]{1,0:T(8,128)(2,1)S(1)} %get-tuple-element.23), channel_id=1, source_target_pairs={{0,2},{1,3},{2,0},{3,1},{4,6},{5,7},{6,4},{7,5},{8,10},{9,11},{10,... | collective-permute-start | bytes 393224 | tf_op jit(solution)/shard_map/ppermute | solution.py:276
  20.1 3.9 %copy-start = (f32[1024,512]{1,0:T(8,128)S(1)}, f32[1024,512]{1,0:T(8,128)}, u32[]{:S(2)}) copy-start(f32[1024,512]{1,0:T(8,128)} %ancestor.1) | copy-start | bytes 6291460
  20.1 8.0 %collective-permute-start.1 = (bf16[1040,128]{1,0:T(8,128)(2,1)S(1)}, bf16[1040,128]{1,0:T(8,128)(2,1)S(1)}, u32[]{:S(2)}, u32[]{:S(2)}) collective-permute-start(bf16[1040,128]{1,0:T(8,128)(2,1)S(1)} %collective-permute-done.refs_1_), channel_id=1, source_target_pairs={{0,1},{1,0},{2,3},{3,2},{4,5},{5,4},{6,7},{7,6},{8,9},{9,8},{10,11... | collective-permute-start | bytes 798728 | tf_op jit(solution)/shard_map/ppermute | solution.py:276
  24.3 4.3 %collective-permute-start.6 = (bf16[1024,512]{1,0:T(8,128)(2,1)S(1)}, bf16[1024,512]{1,0:T(8,128)(2,1)S(1)}, u32[]{:S(2)}, u32[]{:S(2)}) collective-permute-start(bf16[1024,512]{1,0:T(8,128)(2,1)S(1)} %spread_uppers.1.refs_3_.refs_2_.refs_4_), channel_id=1, source_target_pairs={{0,16},{16,0},{1,17},{17,1},{2,18},{18,2},{3,19},{19,3},{4,20},{20... | collective-permute-start | bytes 3145736 | tf_op jit(solution)/shard_map/ppermute | solution.py:280
  24.4 4.3 %collective-permute-start.8 = (bf16[1040,128]{1,0:T(8,128)(2,1)S(1)}, bf16[1040,128]{1,0:T(8,128)(2,1)S(1)}, u32[]{:S(2)}, u32[]{:S(2)}) collective-permute-start(bf16[1040,128]{1,0:T(8,128)(2,1)S(1)} %collective-permute-done.refs_1_), channel_id=1, source_target_pairs={{0,16},{16,0},{1,17},{17,1},{2,18},{18,2},{3,19},{19,3},{4,20},{20... | collective-permute-start | bytes 798728 | tf_op jit(solution)/shard_map/ppermute | solution.py:280
  24.9 3.4 %collective-permute-start.9 = (bf16[512,128]{1,0:T(8,128)(2,1)S(1)}, bf16[512,128]{1,0:T(8,128)(2,1)S(1)}, u32[]{:S(2)}, u32[]{:S(2)}) collective-permute-start(bf16[512,128]{1,0:T(8,128)(2,1)S(1)} %collective-permute-done.4.panel.refs_1_.refs_2_), channel_id=1, source_target_pairs={{0,16},{16,0},{1,17},{17,1},{2,18},{18,2},{3,19},{19,3},{4,20},{20... | collective-permute-start | bytes 393224 | tf_op jit(solution)/shard_map/ppermute | solution.py:280
  25.0 6.3 %collective-permute-start.10 = (bf16[512,128]{1,0:T(8,128)(2,1)S(1)}, bf16[512,128]{1,0:T(8,128)(2,1)S(1)}, u32[]{:S(2)}, u32[]{:S(2)}) collective-permute-start(bf16[512,128]{1,0:T(8,128)(2,1)S(1)} %collective-permute-done.4.panel.refs_1_.refs_2_), channel_id=1, source_target_pairs={{0,1},{1,0},{2,3},{3,2},{4,5},{5,4},{6,7},{7,6},{8,9},{9,8},{10,11... | collective-permute-start | bytes 393224 | tf_op jit(solution)/shard_map/ppermute | solution.py:276
  28.1 1.8 %collective-permute-start.7 = (bf16[1552,128]{1,0:T(8,128)(2,1)S(1)}, bf16[1552,128]{1,0:T(8,128)(2,1)S(1)}, u32[]{:S(2)}, u32[]{:S(2)}) collective-permute-start(bf16[1552,128]{1,0:T(8,128)(2,1)S(1)} %collective-permute-done.3.refs_0_), channel_id=1, source_target_pairs={{0,16},{16,0},{1,17},{17,1},{2,18},{18,2},{3,19},{19,3},{4,20},{20... | collective-permute-start | bytes 1191944 | tf_op jit(solution)/shard_map/ppermute | solution.py:280
  28.3 2.9 %collective-permute-start.2 = (bf16[1040,128]{1,0:T(8,128)(2,1)S(1)}, bf16[1040,128]{1,0:T(8,128)(2,1)S(1)}, u32[]{:S(2)}, u32[]{:S(2)}) collective-permute-start(bf16[1040,128]{1,0:T(8,128)(2,1)S(1)} %collective-permute-done.1.panel.refs_0_.refs_1_), channel_id=1, source_target_pairs={{0,16},{16,0},{1,17},{17,1},{2,18},{18,2},{3,19},{19,3},{4,20},{20... | collective-permute-start | bytes 798728 | tf_op jit(solution)/shard_map/ppermute | solution.py:280
  31.2 1.3 %collective-permute-start.11 = (bf16[512,128]{1,0:T(8,128)(2,1)S(1)}, bf16[512,128]{1,0:T(8,128)(2,1)S(1)}, u32[]{:S(2)}, u32[]{:S(2)}) collective-permute-start(bf16[512,128]{1,0:T(8,128)(2,1)S(1)} %collective-permute-done.10.panel.refs_0_), channel_id=1, source_target_pairs={{0,16},{16,0},{1,17},{17,1},{2,18},{18,2},{3,19},{19,3},{4,20},{20... | collective-permute-start | bytes 393224 | tf_op jit(solution)/shard_map/ppermute | solution.py:280

commit v9 on v8

--- a/solution.py
+++ b/solution.py
@@ -217,7 +217,7 @@
         update = product(left, right, block)
         if bases:
             update = base_refs[0][block, :] + update
-        out[block, :] = update
+        out[block, :] = base_refs[1][block, :] - update if bases == 2 else update
 
 
 def sum_groups(plan, groups, panels, uppers, shape, bases=()):
@@ -239,13 +239,13 @@
     )(*(panel for side in panels for panel in side), *uppers, *bases)
 
 
-def finish_kernel(plan, groups, count, ancestor, early, *refs):
+def finish_kernel(plan, groups, count, base, *refs):
     panels = (refs[:count], refs[count : 2 * count])
     uppers, (out, left, right, result, sent) = refs[2 * count : 2 * count + 2], refs[-5:]
     place_groups(plan, groups, panels, uppers, left, right)
     copies = []
     for i, block in enumerate(blocks_of(out.shape[0])):
-        result[block, :] = ancestor[block, :] - (early[block, :] + product(left, right, block))
+        result[block, :] = base[block, :] - product(left, right, block)
         copy = pltpu.make_async_copy(result.at[block], out.at[block], sent.at[i])
         copy.start()
         copies.append(copy)
@@ -253,23 +253,23 @@
         copy.wait()
 
 
-def finish(plan, ancestor, early, groups, own, other, uppers, after):
+def finish(plan, base, groups, own, other, uppers, after):
     width = own[0].shape[1]
     depth = 2 * sum(deep_of(plan, groups)) * width
     return pl.pallas_call(
         functools.partial(finish_kernel, plan, groups, len(own)),
-        out_shape=jax.ShapeDtypeStruct(ancestor.shape, jnp.float32),
-        in_specs=[whole_vmem()] * (2 * len(own) + 4) + [pl.BlockSpec(memory_space=pl.ANY)] * len(after),
+        out_shape=jax.ShapeDtypeStruct(base.shape, jnp.float32),
+        in_specs=[whole_vmem()] * (2 * len(own) + 3) + [pl.BlockSpec(memory_space=pl.ANY)] * len(after),
         out_specs=pl.BlockSpec(memory_space=pltpu.HBM),
         scratch_shapes=[
-            pltpu.VMEM((ancestor.shape[0] + width, depth), jnp.bfloat16),
-            pltpu.VMEM((depth, ancestor.shape[1]), jnp.bfloat16),
-            pltpu.VMEM(ancestor.shape, jnp.float32),
+            pltpu.VMEM((base.shape[0] + width, depth), jnp.bfloat16),
+            pltpu.VMEM((depth, base.shape[1]), jnp.bfloat16),
+            pltpu.VMEM(base.shape, jnp.float32),
             pltpu.SemaphoreType.DMA((ROW_STEPS,)),
         ],
         compiler_params=pltpu.CompilerParams(vmem_limit_bytes=VMEM_LIMIT),
         name="last_chunk_and_write",
-    )(ancestor, early, *own, *other, *uppers, *after)
+    )(base, *own, *other, *uppers, *after)
 
 
 def swap(array, axis, mask):
@@ -324,13 +324,12 @@
     last_first, first_mark = lax.optimization_barrier((last_first, touched(last_first)))
     last_second, second_mark = lax.optimization_barrier((last_second, touched(last_second, [early])))
     other_last = siblings(last_first)
-    early = sum_groups(
-        plan, (((0,), 0, 0, 3),), [[last_first], [other_last]], uppers, ancestor.shape, [early]
+    base = sum_groups(
+        plan, (((0,), 0, 0, 3),), [[last_first], [other_last]], uppers, ancestor.shape, [early, ancestor]
     )
     return finish(
         plan,
-        ancestor,
-        early,
+        base,
         (((0,), 1, cut, 3),),
         [last_second, last_first],
         [siblings(last_second), other_last],

time: 34.5 us -> 34.4 us (level)
  no operation moved by 1% of the time
where the time goes in v9:
time: 34.4 us; the launch traced here: 34.3 us
  starting transfers between devices  12.9 us (38%)
  blocking collectives  12.5 us (36%)
  Pallas kernels  7.28 us (21%)
  waiting for transfers between devices  1.5 us (4%)
    all_gather x1, blocking collectives, on_line_of_four(): packed = lax.all_gather(packed, 'row', axis=0, tiled=True)  12.5 us
    ppermute x5, starting transfers between devices, swap(): return lax.ppermute(array, axis, [(i, i ^ mask) for i in range(4)])  11.7 us
    pallas_call x4, Pallas kernels, sum_groups(): pl.pallas_call(functools.partial(sum_kernel, plan, groups, sides, len(bas...  3.72 us
    pallas_call x1, Pallas kernels, finish(): pl.pallas_call(functools.partial(finish_kernel, plan, groups, len(own)),...  1.68 us
    pallas_call x1, Pallas kernels, prepare(): pl.pallas_call(prepare_kernel, out_shape=(jax.ShapeDtypeStruct((tiles * w...  1.53 us
    ppermute x7, starting transfers between devices, siblings(): return lax.ppermute(array, 'gz', [(0, 1), (1, 0)])  1.23 us
    ppermute x5, waiting for transfers between devices, swap(): return lax.ppermute(array, axis, [(i, i ^ mask) for i in range(4)])  0.79 us
    ppermute x7, waiting for transfers between devices, siblings(): return lax.ppermute(array, 'gz', [(0, 1), (1, 0)])  0.71 us
  transfers between devices with their start and end apart: 12, of which 4 were waited for; matrix products, arithmetic and copies ran while one was open for 0% of the time, Pallas kernels for 12%

profile of v9, /device:TPU:0, one launch (start us, length us, event | category | flops | bytes accessed | tf_op | source)
XLA Modules:
  0.0 34.3 jit_solution(13664167077429486701)
XLA Ops:
  0.0 1.5 %solve_and_pack.1 = (bf16[1552,128]{1,0:T(8,128)(2,1)S(1)}, bf16[1040,128]{1,0:T(8,128)(2,1)S(1)}, bf16[512,128]{1,0:T(8,128)(2,1)S(1)}, bf16[784,128]{1,0:T(8,128)(2,1)S(1)}) custom-call(s32[1,2,6]{2,1,0:T(2,128)} %row_ids_in.1, s32[1,1,2]{2,1,0:T(1,128)} %bitcast.2, s32[1,2,3]{2,1,0:T(2,128)} %col_ids_in.1, s32[1,1,2]{2,1,0:T(1,128)} %bitcast.3, ...), custom_call_target="tpu_custom_call" | custom-call | tf_op jit(solution)/shard_map/solve_and_pack/pallas_call | solution.py:86
  1.5 3.1 %collective-permute-start.3 = (bf16[1552,128]{1,0:T(8,128)(2,1)S(1)}, bf16[1552,128]{1,0:T(8,128)(2,1)S(1)}, u32[]{:S(2)}, u32[]{:S(2)}) collective-permute-start(bf16[1552,128]{1,0:T(8,128)(2,1)S(1)} %get-tuple-element.22.refs_0_), channel_id=1, source_target_pairs={{0,1},{1,0},{2,3},{3,2},{4,5},{5,4},{6,7},{7,6},{8,9},{9,8},{10,11... | collective-permute-start | bytes 1191944 | tf_op jit(solution)/shard_map/ppermute | solution.py:276
  4.6 2.6 %collective-permute-start = (bf16[1040,128]{1,0:T(8,128)(2,1)S(1)}, bf16[1040,128]{1,0:T(8,128)(2,1)S(1)}, u32[]{:S(2)}, u32[]{:S(2)}) collective-permute-start(bf16[1040,128]{1,0:T(8,128)(2,1)S(1)} %get-tuple-element.17), channel_id=1, source_target_pairs={{0,2},{1,3},{2,0},{3,1},{4,6},{5,7},{6,4},{7,5},{8,10},{9,11},{10,... | collective-permute-start | bytes 798728 | tf_op jit(solution)/shard_map/ppermute | solution.py:276
  7.2 0.0 collective-permute-start.5
  7.2 0.3 collective-permute-start.4
  7.6 12.5 %all_gather.3.packed = bf16[3136,128]{1,0:T(8,128)(2,1)S(1)} all-gather(bf16[784,128]{1,0:T(8,128)(2,1)S(1)} %get-tuple-element.18), channel_id=1, replica_groups=mesh['gz'=2,'row'=4,'col'=4] {'row'}, dimensions={0}, use_global_device_ids=true | all-gather | bytes 1003520 | tf_op jit(solution)/shard_map/all_gather | solution.py:302
  20.1 0.0 collective-permute-done.refs_1_
  20.1 3.5 %collective-permute-start.1 = (bf16[1040,128]{1,0:T(8,128)(2,1)S(1)}, bf16[1040,128]{1,0:T(8,128)(2,1)S(1)}, u32[]{:S(2)}, u32[]{:S(2)}) collective-permute-start(bf16[1040,128]{1,0:T(8,128)(2,1)S(1)} %collective-permute-done.refs_1_), channel_id=1, source_target_pairs={{0,1},{1,0},{2,3},{3,2},{4,5},{5,4},{6,7},{7,6},{8,9},{9,8},{10,11... | collective-permute-start | bytes 798728 | tf_op jit(solution)/shard_map/ppermute | solution.py:276
  23.5 0.4 %collective-permute-done.4.panel.refs_1_.refs_2_ = bf16[512,128]{1,0:T(8,128)(2,1)S(1)} collective-permute-done((bf16[512,128]{1,0:T(8,128)(2,1)S(1)}, bf16[512,128]{1,0:T(8,128)(2,1)S(1)}, u32[]{:S(2)}, u32[]{:S(2)}) %collective-permute-start.4) | collective-permute-done | bytes 131104 | tf_op jit(solution)/shard_map/ppermute | solution.py:276
  24.0 0.0 collective-permute-done.3.refs_0_
  24.0 0.0 collective-permute-done.5.refs_2_.refs_0_
  24.0 0.3 spread_uppers.1.refs_3_.refs_2_.refs_4_
  24.3 0.1 collective-permute-start.6
  24.4 0.5 %collective-permute-start.8 = (bf16[1040,128]{1,0:T(8,128)(2,1)S(1)}, bf16[1040,128]{1,0:T(8,128)(2,1)S(1)}, u32[]{:S(2)}, u32[]{:S(2)}) collective-permute-start(bf16[1040,128]{1,0:T(8,128)(2,1)S(1)} %collective-permute-done.refs_1_), channel_id=1, source_target_pairs={{0,16},{16,0},{1,17},{17,1},{2,18},{18,2},{3,19},{19,3},{4,20},{20... | collective-permute-start | bytes 798728 | tf_op jit(solution)/shard_map/ppermute | solution.py:280
  24.9 0.1 collective-permute-start.9
  25.0 2.2 %collective-permute-start.10 = (bf16[512,128]{1,0:T(8,128)(2,1)S(1)}, bf16[512,128]{1,0:T(8,128)(2,1)S(1)}, u32[]{:S(2)}, u32[]{:S(2)}) collective-permute-start(bf16[512,128]{1,0:T(8,128)(2,1)S(1)} %collective-permute-done.4.panel.refs_1_.refs_2_), channel_id=1, source_target_pairs={{0,1},{1,0},{2,3},{3,2},{4,5},{5,4},{6,7},{7,6},{8,9},{9,8},{10,11... | collective-permute-start | bytes 393224 | tf_op jit(solution)/shard_map/ppermute | solution.py:276
  27.1 0.9 %sum_groups.4.refs_4_ = f32[1024,512]{1,0:T(8,128)S(1)} custom-call(bf16[1552,128]{1,0:T(8,128)(2,1)S(1)} %get-tuple-element.22.refs_0_, bf16[1040,128]{1,0:T(8,128)(2,1)S(1)} %collective-permute-done.refs_1_, bf16[512,128]{1,0:T(8,128)(2,1)S(1)} %collective-permute-done.4.panel.refs_1_.refs_2_, bf16[1024,512]{1,0:T(8,128)(2,1)S(1)} %spread_uppers.1.refs_3_.refs_2_.refs_4_), custom_call_target="tpu_custom_call" | custom-call | flops 1000000000 | tf_op jit(solution)/shard_map/sum_groups/pallas_call | solution.py:227
  28.1 0.0 collective-permute-done.1.panel.refs_0_.refs_1_
  28.1 0.2 collective-permute-start.7
  28.3 0.0 collective-permute-done.9.refs_2_
  28.3 0.3 %collective-permute-start.2 = (bf16[1040,128]{1,0:T(8,128)(2,1)S(1)}, bf16[1040,128]{1,0:T(8,128)(2,1)S(1)}, u32[]{:S(2)}, u32[]{:S(2)}) collective-permute-start(bf16[1040,128]{1,0:T(8,128)(2,1)S(1)} %collective-permute-done.1.panel.refs_0_.refs_1_), channel_id=1, source_target_pairs={{0,16},{16,0},{1,17},{17,1},{2,18},{18,2},{3,19},{19,3},{4,20},{20... | collective-permute-start | bytes 798728 | tf_op jit(solution)/shard_map/ppermute | solution.py:280
  28.7 0.0 collective-permute-done.8.refs_1_
  28.7 0.0 collective-permute-done.6.refs_3_.refs_5_
  28.7 0.9 %sum_groups.5.refs_4_ = f32[1024,512]{1,0:T(8,128)S(1)} custom-call(bf16[1552,128]{1,0:T(8,128)(2,1)S(1)} %collective-permute-done.5.refs_2_.refs_0_, bf16[1040,128]{1,0:T(8,128)(2,1)S(1)} %collective-permute-done.8.refs_1_, bf16[512,128]{1,0:T(8,128)(2,1)S(1)} %collective-permute-done.9.refs_2_, ...), custom_call_target="tpu_custom_call" | custom-call | flops 1000000000 | tf_op jit(solution)/shard_map/sum_groups/pallas_call | solution.py:227
  29.6 0.3 collective-permute-done.7.refs_1_
  29.9 1.0 %sum_groups.6.refs_4_.refs_0_ = f32[1024,512]{1,0:T(8,128)S(1)} custom-call(bf16[1552,128]{1,0:T(8,128)(2,1)S(1)} %collective-permute-done.3.refs_0_, bf16[1552,128]{1,0:T(8,128)(2,1)S(1)} %collective-permute-done.7.refs_1_, bf16[1024,512]{1,0:T(8,128)(2,1)S(1)} %spread_uppers.1.refs_3_.refs_2_.refs_4_, ...), custom_call_target="tpu_custom_call" | custom-call | flops 1000000000 | tf_op jit(solution)/shard_map/sum_groups/pallas_call | solution.py:227
  30.9 0.4 %collective-permute-done.10.panel.refs_0_ = bf16[512,128]{1,0:T(8,128)(2,1)S(1)} collective-permute-done((bf16[512,128]{1,0:T(8,128)(2,1)S(1)}, bf16[512,128]{1,0:T(8,128)(2,1)S(1)}, u32[]{:S(2)}, u32[]{:S(2)}) %collective-permute-start.10) | collective-permute-done | bytes 131104 | tf_op jit(solution)/shard_map/ppermute | solution.py:276
  31.2 0.0 collective-permute-start.11
  31.2 0.0 collective-permute-done.2.refs_1_.refs_3_
  31.2 0.9 %sum_groups.7.base = f32[1024,512]{1,0:T(8,128)S(1)} custom-call(bf16[1040,128]{1,0:T(8,128)(2,1)S(1)} %collective-permute-done.1.panel.refs_0_.refs_1_, bf16[1040,128]{1,0:T(8,128)(2,1)S(1)} %collective-permute-done.2.refs_1_.refs_3_, bf16[1024,512]{1,0:T(8,128)(2,1)S(1)} %spread_uppers.1.refs_3_.refs_2_.refs_4_, ...), custom_call_target="tpu_custom_call" | custom-call | flops 1000000000 | tf_op jit(solution)/shard_map/sum_groups/pallas_call | solution.py:227
  32.2 0.4 %collective-permute-done.11.refs_2_ = bf16[512,128]{1,0:T(8,128)(2,1)S(1)} collective-permute-done((bf16[512,128]{1,0:T(8,128)(2,1)S(1)}, bf16[512,128]{1,0:T(8,128)(2,1)S(1)}, u32[]{:S(2)}, u32[]{:S(2)}) %collective-permute-start.11) | collective-permute-done | bytes 131104 | tf_op jit(solution)/shard_map/ppermute | solution.py:280
  32.6 1.7 %last_chunk_and_write.1 = f32[1024,512]{1,0:T(8,128)} custom-call(f32[1024,512]{1,0:T(8,128)S(1)} %sum_groups.7.base, bf16[512,128]{1,0:T(8,128)(2,1)S(1)} %collective-permute-done.10.panel.refs_0_, bf16[1040,128]{1,0:T(8,128)(2,1)S(1)} %collective-permute-done.1.panel.refs_0_.refs_1_, bf16[512,128]{1,0:T(8,128)(2,1)S(1)} %collective-permute-done.11.refs_2_, ...), custom_call_target="tpu_custom_call" | custom-call | tf_op jit(solution)/shard_map/last_chunk_and_write/pallas_call | solution.py:259
  (5 shorter events, 0.0 us)
Async XLA Ops:
  1.5 22.4 %collective-permute-start.3 = (bf16[1552,128]{1,0:T(8,128)(2,1)S(1)}, bf16[1552,128]{1,0:T(8,128)(2,1)S(1)}, u32[]{:S(2)}, u32[]{:S(2)}) collective-permute-start(bf16[1552,128]{1,0:T(8,128)(2,1)S(1)} %get-tuple-element.22.refs_0_), channel_id=1, source_target_pairs={{0,1},{1,0},{2,3},{3,2},{4,5},{5,4},{6,7},{7,6},{8,9},{9,8},{10,11... | collective-permute-start | bytes 1191944 | tf_op jit(solution)/shard_map/ppermute | solution.py:276
  4.6 15.4 %collective-permute-start = (bf16[1040,128]{1,0:T(8,128)(2,1)S(1)}, bf16[1040,128]{1,0:T(8,128)(2,1)S(1)}, u32[]{:S(2)}, u32[]{:S(2)}) collective-permute-start(bf16[1040,128]{1,0:T(8,128)(2,1)S(1)} %get-tuple-element.17), channel_id=1, source_target_pairs={{0,2},{1,3},{2,0},{3,1},{4,6},{5,7},{6,4},{7,5},{8,10},{9,11},{10,... | collective-permute-start | bytes 798728 | tf_op jit(solution)/shard_map/ppermute | solution.py:276
  7.2 16.7 %collective-permute-start.5 = (bf16[1552,128]{1,0:T(8,128)(2,1)S(1)}, bf16[1552,128]{1,0:T(8,128)(2,1)S(1)}, u32[]{:S(2)}, u32[]{:S(2)}) collective-permute-start(bf16[1552,128]{1,0:T(8,128)(2,1)S(1)} %get-tuple-element.22.refs_0_), channel_id=1, source_target_pairs={{0,16},{16,0},{1,17},{17,1},{2,18},{18,2},{3,19},{19,3},{4,20},{20... | collective-permute-start | bytes 1191944 | tf_op jit(solution)/shard_map/ppermute | solution.py:280
  7.2 16.7 %collective-permute-start.4 = (bf16[512,128]{1,0:T(8,128)(2,1)S(1)}, bf16[512,128]{1,0:T(8,128)(2,1)S(1)}, u32[]{:S(2)}, u32[]{:S(2)}) collective-permute-start(bf16[512,128]{1,0:T(8,128)(2,1)S(1)} %get-tuple-element.23), channel_id=1, source_target_pairs={{0,2},{1,3},{2,0},{3,1},{4,6},{5,7},{6,4},{7,5},{8,10},{9,11},{10,... | collective-permute-start | bytes 393224 | tf_op jit(solution)/shard_map/ppermute | solution.py:276
  20.1 3.9 %copy-start = (f32[1024,512]{1,0:T(8,128)S(1)}, f32[1024,512]{1,0:T(8,128)}, u32[]{:S(2)}) copy-start(f32[1024,512]{1,0:T(8,128)} %refs_5_.1) | copy-start | bytes 6291460
  20.1 8.0 %collective-permute-start.1 = (bf16[1040,128]{1,0:T(8,128)(2,1)S(1)}, bf16[1040,128]{1,0:T(8,128)(2,1)S(1)}, u32[]{:S(2)}, u32[]{:S(2)}) collective-permute-start(bf16[1040,128]{1,0:T(8,128)(2,1)S(1)} %collective-permute-done.refs_1_), channel_id=1, source_target_pairs={{0,1},{1,0},{2,3},{3,2},{4,5},{5,4},{6,7},{7,6},{8,9},{9,8},{10,11... | collective-permute-start | bytes 798728 | tf_op jit(solution)/shard_map/ppermute | solution.py:276
  24.3 4.3 %collective-permute-start.6 = (bf16[1024,512]{1,0:T(8,128)(2,1)S(1)}, bf16[1024,512]{1,0:T(8,128)(2,1)S(1)}, u32[]{:S(2)}, u32[]{:S(2)}) collective-permute-start(bf16[1024,512]{1,0:T(8,128)(2,1)S(1)} %spread_uppers.1.refs_3_.refs_2_.refs_4_), channel_id=1, source_target_pairs={{0,16},{16,0},{1,17},{17,1},{2,18},{18,2},{3,19},{19,3},{4,20},{20... | collective-permute-start | bytes 3145736 | tf_op jit(solution)/shard_map/ppermute | solution.py:280
  24.4 4.3 %collective-permute-start.8 = (bf16[1040,128]{1,0:T(8,128)(2,1)S(1)}, bf16[1040,128]{1,0:T(8,128)(2,1)S(1)}, u32[]{:S(2)}, u32[]{:S(2)}) collective-permute-start(bf16[1040,128]{1,0:T(8,128)(2,1)S(1)} %collective-permute-done.refs_1_), channel_id=1, source_target_pairs={{0,16},{16,0},{1,17},{17,1},{2,18},{18,2},{3,19},{19,3},{4,20},{20... | collective-permute-start | bytes 798728 | tf_op jit(solution)/shard_map/ppermute | solution.py:280
  24.9 3.4 %collective-permute-start.9 = (bf16[512,128]{1,0:T(8,128)(2,1)S(1)}, bf16[512,128]{1,0:T(8,128)(2,1)S(1)}, u32[]{:S(2)}, u32[]{:S(2)}) collective-permute-start(bf16[512,128]{1,0:T(8,128)(2,1)S(1)} %collective-permute-done.4.panel.refs_1_.refs_2_), channel_id=1, source_target_pairs={{0,16},{16,0},{1,17},{17,1},{2,18},{18,2},{3,19},{19,3},{4,20},{20... | collective-permute-start | bytes 393224 | tf_op jit(solution)/shard_map/ppermute | solution.py:280
  25.0 6.3 %collective-permute-start.10 = (bf16[512,128]{1,0:T(8,128)(2,1)S(1)}, bf16[512,128]{1,0:T(8,128)(2,1)S(1)}, u32[]{:S(2)}, u32[]{:S(2)}) collective-permute-start(bf16[512,128]{1,0:T(8,128)(2,1)S(1)} %collective-permute-done.4.panel.refs_1_.refs_2_), channel_id=1, source_target_pairs={{0,1},{1,0},{2,3},{3,2},{4,5},{5,4},{6,7},{7,6},{8,9},{9,8},{10,11... | collective-permute-start | bytes 393224 | tf_op jit(solution)/shard_map/ppermute | solution.py:276
  28.1 1.8 %collective-permute-start.7 = (bf16[1552,128]{1,0:T(8,128)(2,1)S(1)}, bf16[1552,128]{1,0:T(8,128)(2,1)S(1)}, u32[]{:S(2)}, u32[]{:S(2)}) collective-permute-start(bf16[1552,128]{1,0:T(8,128)(2,1)S(1)} %collective-permute-done.3.refs_0_), channel_id=1, source_target_pairs={{0,16},{16,0},{1,17},{17,1},{2,18},{18,2},{3,19},{19,3},{4,20},{20... | collective-permute-start | bytes 1191944 | tf_op jit(solution)/shard_map/ppermute | solution.py:280
  28.3 2.9 %collective-permute-start.2 = (bf16[1040,128]{1,0:T(8,128)(2,1)S(1)}, bf16[1040,128]{1,0:T(8,128)(2,1)S(1)}, u32[]{:S(2)}, u32[]{:S(2)}) collective-permute-start(bf16[1040,128]{1,0:T(8,128)(2,1)S(1)} %collective-permute-done.1.panel.refs_0_.refs_1_), channel_id=1, source_target_pairs={{0,16},{16,0},{1,17},{17,1},{2,18},{18,2},{3,19},{19,3},{4,20},{20... | collective-permute-start | bytes 798728 | tf_op jit(solution)/shard_map/ppermute | solution.py:280
  31.2 1.3 %collective-permute-start.11 = (bf16[512,128]{1,0:T(8,128)(2,1)S(1)}, bf16[512,128]{1,0:T(8,128)(2,1)S(1)}, u32[]{:S(2)}, u32[]{:S(2)}) collective-permute-start(bf16[512,128]{1,0:T(8,128)(2,1)S(1)} %collective-permute-done.10.panel.refs_0_), channel_id=1, source_target_pairs={{0,16},{16,0},{1,17},{17,1},{2,18},{18,2},{3,19},{19,3},{4,20},{20... | collective-permute-start | bytes 393224 | tf_op jit(solution)/shard_map/ppermute | solution.py:280
